TPU v7x, 32 devices: a whole 2x2x4 slice. The times are simulated.
32 devices in a mesh: seq: 4 (over y, core), head: 4 (over z), rep: 2 (over x).
Axes of the slice: x: 2, y: 2, z: 4, core: 2. Of those that a mesh axis runs over, the one named last changes fastest.
Arguments:
- queries: bfloat16 [2048, 3072], P(('seq', 'rep'), 'head'), may hold values from -190 to 190
- keys: bfloat16 [2048, 3072], P(('seq', 'rep'), 'head'), may hold values from -6 to 6
- values: bfloat16 [2048, 3072], P(('seq', 'rep'), 'head'), may hold values from -6 to 6
- grad_output: bfloat16 [2048, 3072], P(('seq', 'rep'), 'head'), may hold values from -12 to 12
- out_weight: bfloat16 [3072, 3072], P('head'), may hold values from -0.109375 to 0.109375
- text_keys: bfloat16 [256, 3072], P(None, 'head'), may hold values from -7 to 7
- text_values: bfloat16 [256, 3072], P(None, 'head'), may hold values from -6 to 6
- mask_lists: int32 [16, 3], replicated, may hold values from 0 to 15, as said below
- text_owner: int32 [256], replicated, may hold values from 0 to 7, as said below
Outputs:
- query_grads: bfloat16 [2048, 3072], P(('seq', 'rep'), 'head')
- key_grads: bfloat16 [2048, 3072], P(('seq', 'rep'), 'head')
- value_grads: bfloat16 [2048, 3072], P(('seq', 'rep'), 'head')
- text_key_grads: bfloat16 [512, 3072], P(('seq', 'rep'), 'head')
- text_value_grads: bfloat16 [512, 3072], P(('seq', 'rep'), 'head')
Inputs may be any that keep to these rules, and one draw needn't show every extreme that they name: Video tokens s * 256 to (s + 1) * 256 - 1 form slab s. Row t of mask_lists begins with t itself; its other 2 entries are distinct existing tiles other than t of the slabs t // 2 - 1, t // 2 and t // 2 + 1. `text_owner`: no slab owns more than 64 text tokens, and some slab owns exactly 64.
All inputs are finite; a program needn't handle non-finite values.
Results may differ from a plain program's by a relative error of at most 0.0156.
Values may be sent and summed in bfloat16 or wider, within the bound.
No kernel may reach another device: no remote copies, remote signals or barrier semaphores. Data moves between devices by JAX's collectives and lax.ppermute only.
A program may use at most 64 MiB of HBM per device.

v0:
```python
import jax
import jax.numpy as jnp
from jax import lax
from jax.sharding import PartitionSpec as P

HD = 128
TILE = 128


def extended(cells, sides, width):
    for axis, dim in sides:
        count = lax.axis_size(axis)
        ends = count - 1
        head = lax.slice_in_dim(cells, 0, width, axis=dim)
        tail = lax.slice_in_dim(cells, cells.shape[dim] - width, cells.shape[dim], axis=dim)
        cells = jnp.concatenate(
            [
                lax.ppermute(tail, axis, [(i, (i + 1) % count) for i in range(ends)]),
                cells,
                lax.ppermute(head, axis, [((i + 1) % count, i) for i in range(ends)]),
            ],
            axis=dim,
        )
    return cells


def tile_allowed(lists, first_tile, count):
    tile_ids = first_tile + jnp.arange(count, dtype=jnp.int32)
    return jnp.any(lists[:, :, None] == tile_ids[None, None, :], axis=1)


def token_mask(allowed):
    return jnp.repeat(jnp.repeat(allowed, TILE, axis=0), TILE, axis=1)


def local(
    queries, keys, values, grad_output, out_weight, text_keys, text_values, mask_lists, text_owner
):
    frame = queries.shape[0]
    width = queries.shape[1]
    heads_here = width // HD
    tiles_here = frame // TILE
    text_count = text_keys.shape[0]
    scale = HD ** (-0.5)
    slab = lax.axis_index(("seq", "rep"))
    grad_sum = lax.dot_general(
        lax.all_gather(grad_output, "head", axis=1, tiled=True),
        out_weight,
        (((1,), (1,)), ((), ())),
        preferred_element_type=jnp.float32,
    )
    grad_heads = grad_sum.astype(jnp.bfloat16)
    wide = extended(jnp.stack([keys, values]), ((("seq", "rep"), 1),), frame)
    own_lists = lax.dynamic_slice_in_dim(mask_lists, slab * tiles_here, tiles_here, 0)
    video_mask = token_mask(tile_allowed(own_lists, (slab - 1) * tiles_here, 3 * tiles_here))
    q_rows = queries.reshape(frame, heads_here, HD)
    g_rows = grad_heads.reshape(frame, heads_here, HD)
    near_keys = wide[0].reshape(3 * frame, heads_here, HD)
    near_values = wide[1].reshape(3 * frame, heads_here, HD)
    text_k = text_keys.reshape(text_count, heads_here, HD)
    text_v = text_values.reshape(text_count, heads_here, HD)
    video_scores = scale * jnp.einsum(
        "qhe,khe->hqk", q_rows, near_keys, preferred_element_type=jnp.float32
    )
    video_scores = jnp.where(video_mask[None], video_scores, -jnp.inf)
    text_scores = scale * jnp.einsum(
        "qhe,khe->hqk", q_rows, text_k, preferred_element_type=jnp.float32
    )
    top = jnp.maximum(jnp.max(video_scores, axis=2), jnp.max(text_scores, axis=2))
    total = jnp.sum(jnp.exp(video_scores - top[:, :, None]), axis=2) + jnp.sum(
        jnp.exp(text_scores - top[:, :, None]), axis=2
    )
    lse = top + jnp.log(total)
    video_prob = jnp.exp(video_scores - lse[:, :, None])
    text_prob = jnp.exp(text_scores - lse[:, :, None])
    video_half = video_prob.astype(jnp.bfloat16)
    text_half = text_prob.astype(jnp.bfloat16)
    attended = jnp.einsum(
        "hqk,khe->qhe", video_half, near_values, preferred_element_type=jnp.float32
    )
    attended = attended + jnp.einsum(
        "hqk,khe->qhe", text_half, text_v, preferred_element_type=jnp.float32
    )
    delta = jnp.einsum("qhe,qhe->hq", g_rows.astype(jnp.float32), attended)
    video_dprob = jnp.einsum(
        "qhe,khe->hqk", g_rows, near_values, preferred_element_type=jnp.float32
    )
    text_dprob = jnp.einsum("qhe,khe->hqk", g_rows, text_v, preferred_element_type=jnp.float32)
    video_ds = (video_prob * (video_dprob - delta[:, :, None])).astype(jnp.bfloat16)
    text_ds = (text_prob * (text_dprob - delta[:, :, None])).astype(jnp.bfloat16)
    query_sum = jnp.einsum("hqk,khe->qhe", video_ds, near_keys, preferred_element_type=jnp.float32)
    query_sum = query_sum + jnp.einsum(
        "hqk,khe->qhe", text_ds, text_k, preferred_element_type=jnp.float32
    )
    query_grads = (scale * query_sum).reshape(frame, width).astype(jnp.bfloat16)
    key_wide = scale * jnp.einsum(
        "hqk,qhe->khe", video_ds, q_rows, preferred_element_type=jnp.float32
    )
    value_wide = jnp.einsum("hqk,qhe->khe", video_half, g_rows, preferred_element_type=jnp.float32)
    grads_wide = jnp.stack(
        [key_wide.reshape(3 * frame, width), value_wide.reshape(3 * frame, width)]
    )
    outgoing = jnp.concatenate([grads_wide[:, :frame], grads_wide[:, 2 * frame :]], axis=1)
    arrived = extended(outgoing.astype(jnp.bfloat16), ((("seq", "rep"), 1),), frame).astype(
        outgoing.dtype
    )
    own_grads = grads_wide[:, frame : 2 * frame] + arrived[:, :frame] + arrived[:, 3 * frame :]
    key_grads = own_grads[0].astype(jnp.bfloat16)
    value_grads = own_grads[1].astype(jnp.bfloat16)
    text_key_part = (
        scale * jnp.einsum("hqk,qhe->khe", text_ds, q_rows, preferred_element_type=jnp.float32)
    ).reshape(text_count, width)
    text_value_part = jnp.einsum(
        "hqk,qhe->khe", text_half, g_rows, preferred_element_type=jnp.float32
    ).reshape(text_count, width)
    groups = lax.axis_size(("seq", "rep"))
    capacity = 2 * text_count // groups
    owner_hot = (text_owner[:, None] == jnp.arange(groups, dtype=jnp.int32)[None, :]).astype(
        jnp.int32
    )
    rank = jnp.sum(owner_hot * (jnp.cumsum(owner_hot, axis=0) - 1), axis=1)
    slot = text_owner * capacity + rank
    placing = (jnp.arange(groups * capacity, dtype=jnp.int32)[:, None] == slot[None, :]).astype(
        jnp.float32
    )
    key_slots = jnp.dot(
        placing, text_key_part, precision=lax.Precision.HIGHEST, preferred_element_type=jnp.float32
    )
    value_slots = jnp.dot(
        placing,
        text_value_part,
        precision=lax.Precision.HIGHEST,
        preferred_element_type=jnp.float32,
    )
    key_mine, value_mine = (
        lax.psum_scatter(key_slots, ("seq", "rep"), scatter_dimension=0, tiled=True),
        lax.psum_scatter(value_slots, ("seq", "rep"), scatter_dimension=0, tiled=True),
    )
    return (
        query_grads,
        key_grads,
        value_grads,
        key_mine.astype(jnp.bfloat16),
        value_mine.astype(jnp.bfloat16),
    )


def solution(mesh):
    return jax.shard_map(
        local,
        mesh=mesh,
        in_specs=(
            P(("seq", "rep"), "head"),
            P(("seq", "rep"), "head"),
            P(("seq", "rep"), "head"),
            P(("seq", "rep"), "head"),
            P("head", None),
            P(None, "head"),
            P(None, "head"),
            P(),
            P(),
        ),
        out_specs=(
            P(("seq", "rep"), "head"),
            P(("seq", "rep"), "head"),
            P(("seq", "rep"), "head"),
            P(("seq", "rep"), "head"),
            P(("seq", "rep"), "head"),
        ),
        check_vma=False,
    )
```

profile of v0, /device:TPU:0, one launch (start us, length us, event | category | flops | bytes accessed | tf_op | source)
XLA Modules:
  0.0 159.6 jit_solution(14934168173552479575)
XLA Ops:
  11.9 6.4 %collective-permute-start = (bf16[2,256,768]{1,2,0:T(8,128)(2,1)}, bf16[2,256,768]{1,2,0:T(8,128)(2,1)}, u32[]{:S(2)}, u32[]{:S(2)}) collective-permute-start(bf16[2,256,768]{1,2,0:T(8,128)(2,1)} %pad_maximum_fusion.5), channel_id=1, source_target_pairs={{0,1},{1,8},{8,9},{9,16},{16,17},{17,24},{24,25},{2,3},{3,10},{10,... | collective-permute-start | bytes 2359304 | tf_op jit(solution)/shard_map/ppermute | solution.py:18
  20.5 13.7 %collective-permute-done.1 = bf16[2,256,768]{1,2,0:T(8,128)(2,1)} collective-permute-done((bf16[2,256,768]{1,2,0:T(8,128)(2,1)}, bf16[2,256,768]{1,2,0:T(8,128)(2,1)}, u32[]{:S(2)}, u32[]{:S(2)}) %collective-permute-start.1) | collective-permute-done | bytes 786464 | tf_op jit(solution)/shard_map/ppermute | solution.py:20
  34.1 1.6 collective-permute-done
  35.7 1.5 pad_maximum_fusion.1
  41.6 14.6 %all-gather.2.cloned.1.call-done = bf16[256,3072]{1,0:T(8,128)(2,1)} async-done(((bf16[256,768]{1,0:T(8,128)(2,1)}), bf16[256,3072]{1,0:T(8,128)(2,1)}) %all-gather.2.cloned.1.call-update) | async-done | bytes 1572880 | tf_op jit(solution)/shard_map/all_gather | solution.py:47
  56.2 5.0 %convolution_convert_fusion = bf16[256,768]{1,0:T(8,128)(2,1)} fusion(bf16[256,3072]{1,0:T(8,128)(2,1)} %all-gather.2.cloned.1.call-done, bf16[768,3072]{1,0:T(8,128)(2,1)} %param.13), kind=kOutput, calls=%fused_computation.32 | convolution fusion | flops 1208156160 | bytes 6684672 | tf_op jit(solution)/shard_map/dot_general | solution.py:46
  62.7 2.1 %fusion.15 = f32[512,768]{1,0:T(8,128)} fusion(f32[256,768]{0,1:T(8,128)S(1)} %bitcast.130, s32[256]{0:T(256)S(1)} %multiply_add_fusion), kind=kOutput, calls=%fused_computation.39 | convolution fusion | flops 1208090624 | bytes 2360320 | tf_op jit(solution)/shard_map/dot_general | solution.py:129
  65.1 1.9 %copy.77 = bf16[256,768]{0,1:T(8,128)(2,1)} copy(bf16[256,768]{1,0:T(8,128)(2,1)} %param.15) | data formatting | bytes 786432 | tf_op args[6]
  68.6 3.8 %fusion.14 = f32[6,256]{1,0:T(8,128)S(1)} fusion(f32[256,6,128]{0,2,1:T(8,128)S(1)} %convolution_bitcast_fusion.1, bf16[768,6,128]{0,2,1:T(8,128)(2,1)S(1)} %bitcast.133, bf16[6,256,128]{1,2,0:T(8,128)(2,1)S(1)} %bitcast.112, f32[6,768,256]{2,1,0:T(8,128)} %copy-done.1, f32[6,256]{1,0:T(8,128)S(1)} %log_add_fusion, pred[256,768]{0,1:T(8,128)(4,1)S(1)} %bitcast.127), kind=kOutput, calls=%fused_computation.33 | convolution fusion | flops 307493376 | bytes 7286784 | tf_op jit(solution)/shard_map/hqk,khe->qhe/dot_general | solution.py:78
  74.2 2.1 %fusion.16 = f32[512,768]{1,0:T(8,128)} fusion(f32[256,768]{0,1:T(8,128)S(1)} %bitcast.129, s32[256]{0:T(256)S(1)} %multiply_add_fusion), kind=kOutput, calls=%fused_computation.40 | convolution fusion | flops 1208090624 | bytes 2360320 | tf_op jit(solution)/shard_map/dot_general | solution.py:126
  76.3 6.0 %multiply_convert_fusion = bf16[6,256,768]{1,2,0:T(8,128)(2,1)} fusion(f32[6,768,256]{2,1,0:T(8,128)} %copy-done.1, f32[6,256]{1,0:T(8,128)S(1)} %copy-done.17, f32[6,256]{1,0:T(8,128)S(1)} %log_add_fusion, pred[256,768]{0,1:T(8,128)(4,1)S(1)} %bitcast.128, bf16[256,6,128]{0,2,1:T(8,128)(2,1)S(1)} %bitcast.114, bf16[768,6,128]{0,2,1:T(8,128)(2,1)} %bitcast.132), kind=kOutput, calls=%fused_computation.5 | convolution fusion | flops 309067776 | bytes 8859648 | tf_op jit(solution)/shard_map/qhe,khe->hqk/dot_general | solution.py:85
  82.3 4.0 %convolution_multiply_fusion = f32[6,768,128]{1,2,0:T(8,128)} fusion(bf16[6,256,768]{1,2,0:T(8,128)(2,1)} %multiply_convert_fusion, bf16[256,6,128]{0,2,1:T(8,128)(2,1)S(1)} %bitcast.108), kind=kOutput, calls=%fused_computation.11 | convolution fusion | flops 302579712 | bytes 5111808 | tf_op jit(solution)/shard_map/hqk,qhe->khe/dot_general | solution.py:96
  86.3 2.3 %copy.89 = f32[1,768,768]{2,1,0:T(8,128)S(1)} copy(f32[1,768,768]{1,2,0:T(8,128)} %bitcast.110) | data formatting | bytes 4718592 | tf_op jit(solution)/shard_map/stack;reshape | solution.py:100
  88.6 5.3 %fusion.24 = f32[6,128,768]{2,1,0:T(8,128)} fusion(bf16[256,6,128]{0,2,1:T(8,128)(2,1)} %bitcast.115, f32[6,768,256]{2,1,0:T(8,128)} %copy-done.1, f32[6,256]{1,0:T(8,128)S(1)} %log_add_fusion, pred[256,768]{0,1:T(8,128)(4,1)} %bitcast.126), kind=kOutput, calls=%fused_computation.58 | convolution fusion | flops 306708480 | bytes 7673856 | tf_op jit(solution)/shard_map/hqk,qhe->khe/dot_general | solution.py:99
  93.9 3.1 %copy.90 = f32[1,768,768]{2,1,0:T(8,128)} copy(f32[1,768,768]{1,2,0:T(8,128)} %bitcast.109) | data formatting | bytes 4718592 | tf_op jit(solution)/shard_map/stack;reshape | solution.py:100
  96.9 2.1 %fusion = bf16[2,768,768]{2,1,0:T(8,128)(2,1)S(1)} fusion(f32[1,768,768]{2,1,0:T(8,128)} %copy.90, f32[1,768,768]{2,1,0:T(8,128)S(1)} %copy.89), kind=kLoop, calls=%fused_computation.3 | loop fusion | flops 1179648 | bytes 7077888 | tf_op jit(solution)/shard_map/convert.4
  100.4 4.2 %collective-permute-start.2 = (bf16[2,256,768]{2,1,0:T(8,128)(2,1)}, bf16[2,256,768]{2,1,0:T(8,128)(2,1)}, u32[]{:S(2)}, u32[]{:S(2)}) collective-permute-start(bf16[2,256,768]{2,1,0:T(8,128)(2,1)} %get-tuple-element.20), channel_id=1, source_target_pairs={{0,1},{1,8},{8,9},{9,16},{16,17},{17,24},{24,25},{2,3},{3,10},{10,... | collective-permute-start | bytes 2359304 | tf_op jit(solution)/shard_map/ppermute | solution.py:18
  107.4 1.9 %copy.93 = bf16[256,768]{1,0:T(8,128)(2,1)} copy(bf16[256,768]{0,1:T(8,128)(2,1)} %bitcast.131) | data formatting | bytes 786432
  109.3 12.6 %collective-permute-done.2 = bf16[2,256,768]{2,1,0:T(8,128)(2,1)} collective-permute-done((bf16[2,256,768]{2,1,0:T(8,128)(2,1)}, bf16[2,256,768]{2,1,0:T(8,128)(2,1)}, u32[]{:S(2)}, u32[]{:S(2)}) %collective-permute-start.2) | collective-permute-done | bytes 786464 | tf_op jit(solution)/shard_map/ppermute | solution.py:18
  122.0 21.2 %collective-permute-done.3 = bf16[2,256,768]{2,1,0:T(8,128)(2,1)} collective-permute-done((bf16[2,256,768]{2,1,0:T(8,128)(2,1)}, bf16[2,256,768]{2,1,0:T(8,128)(2,1)}, u32[]{:S(2)}, u32[]{:S(2)}) %collective-permute-start.3) | collective-permute-done | bytes 786464 | tf_op jit(solution)/shard_map/ppermute | solution.py:20
  143.2 1.9 %fusion.6 = bf16[2,256,768]{2,1,0:T(8,128)(2,1)S(1)} fusion(f32[1,768,768]{2,1,0:T(8,128)S(1)} %copy.89, f32[1,768,768]{2,1,0:T(8,128)} %copy.90, bf16[2,256,768]{2,1,0:T(8,128)(2,1)} %collective-permute-done.3, bf16[2,256,768]{2,1,0:T(8,128)(2,1)} %get-tuple-element.20, bf16[2,256,768]{2,1,0:T(8,128)(2,1)} %get-tuple-element.21, ...), kind=kLoop, calls=%fused_computation.15 | loop fusion | flops 7864320 | bytes 8650752 | tf_op jit(solution)/shard_map/convert.1
  146.0 1.6 convert_element_type.58
  147.6 3.9 %reduce-scatter.3.cloned.1.call-done = f32[64,768]{1,0:T(8,128)} async-done(((f32[512,768]{1,0:T(8,128)}), f32[64,768]{1,0:T(8,128)}) %reduce-scatter.3.cloned.1.call-update) | async-done | bytes 196624 | tf_op jit(solution)/shard_map/reduce_scatter | solution.py:136
  151.5 1.6 convert_element_type.57
  (79 shorter events, 21.3 us)
Async XLA Ops:
  7.2 11.2 %copy-start = (s32[16,3]{0,1:T(4,128)S(1)}, s32[16,3]{0,1:T(4,128)}, u32[]{:S(2)}) copy-start(s32[16,3]{0,1:T(4,128)} %param.16) | copy-start | bytes 580
  7.2 11.4 %copy-start.15 = (s32[256]{0:T(256)S(1)}, s32[256]{0:T(256)}, u32[]{:S(2)}) copy-start(s32[256]{0:T(256)} %param.17) | copy-start | bytes 3076
  7.2 12.4 %copy-start.13 = (bf16[256,768]{1,0:T(8,128)(2,1)S(1)}, bf16[256,768]{1,0:T(8,128)(2,1)}, u32[]{:S(2)}) copy-start(bf16[256,768]{1,0:T(8,128)(2,1)} %param.9) | copy-start | bytes 1179652
  7.2 12.5 %copy-start.14 = (bf16[256,768]{1,0:T(8,128)(2,1)S(1)}, bf16[256,768]{1,0:T(8,128)(2,1)}, u32[]{:S(2)}) copy-start(bf16[256,768]{1,0:T(8,128)(2,1)} %param.14) | copy-start | bytes 1179652
  7.2 48.9 %all-gather.2.cloned.1.call-start = ((), (), s32[]{:S(2)}) async-start(), calls=%async_computation.2 | async-start | bytes 1966080 | tf_op jit(solution)/shard_map/all_gather | solution.py:47
  10.6 23.5 %collective-permute-start.1 = (bf16[2,256,768]{1,2,0:T(8,128)(2,1)}, bf16[2,256,768]{1,2,0:T(8,128)(2,1)}, u32[]{:S(2)}, u32[]{:S(2)}) collective-permute-start(bf16[2,256,768]{1,2,0:T(8,128)(2,1)} %pad_maximum_fusion.5), channel_id=1, source_target_pairs={{1,0},{8,1},{9,8},{16,9},{17,16},{24,17},{25,24},{3,2},{10,3},{11,... | collective-permute-start | bytes 2359304 | tf_op jit(solution)/shard_map/ppermute | solution.py:20
  11.9 23.8 %collective-permute-start = (bf16[2,256,768]{1,2,0:T(8,128)(2,1)}, bf16[2,256,768]{1,2,0:T(8,128)(2,1)}, u32[]{:S(2)}, u32[]{:S(2)}) collective-permute-start(bf16[2,256,768]{1,2,0:T(8,128)(2,1)} %pad_maximum_fusion.5), channel_id=1, source_target_pairs={{0,1},{1,8},{8,9},{9,16},{16,17},{17,24},{24,25},{2,3},{3,10},{10,... | collective-permute-start | bytes 2359304 | tf_op jit(solution)/shard_map/ppermute | solution.py:18
  18.3 127.7 %reduce-scatter.5.cloned.1.call-start = ((), (), s32[]{:S(2)}) async-start(), calls=%async_computation.4 | async-start | bytes 1769472 | tf_op jit(solution)/shard_map/reduce_scatter | solution.py:137
  19.9 15.8 %copy-start.6 = (bf16[256,768]{0,1:T(8,128)(2,1)}, bf16[256,768]{0,1:T(8,128)(2,1)S(1)}, u32[]{:S(2)}) copy-start(bf16[256,768]{0,1:T(8,128)(2,1)S(1)} %copy.70) | copy-start | bytes 1179652
  38.5 1.3 copy-start.9
  39.5 2.1 %copy-start.1 = (f32[6,768,256]{2,1,0:T(8,128)}, f32[6,768,256]{2,1,0:T(8,128)S(1)}, u32[]{:S(2)}) copy-start(f32[6,768,256]{2,1,0:T(8,128)S(1)} %get-tuple-element.27) | copy-start | bytes 14155780
  62.3 13.9 %copy-start.5 = (bf16[256,768]{0,1:T(8,128)(2,1)}, bf16[256,768]{0,1:T(8,128)(2,1)S(1)}, u32[]{:S(2)}) copy-start(bf16[256,768]{0,1:T(8,128)(2,1)S(1)} %copy.73) | copy-start | bytes 1179652
  64.9 86.7 %reduce-scatter.3.cloned.1.call-start = ((), (), s32[]{:S(2)}) async-start(), calls=%async_computation.3 | async-start | bytes 1769472 | tf_op jit(solution)/shard_map/reduce_scatter | solution.py:136
  67.0 1.5 copy-start.10
  67.0 1.5 copy-start.12
  68.5 3.8 %copy-start.8 = (bf16[256,768]{0,1:T(8,128)(2,1)S(1)}, bf16[256,768]{0,1:T(8,128)(2,1)}, u32[]{:S(2)}) copy-start(bf16[256,768]{0,1:T(8,128)(2,1)} %copy.77) | copy-start | bytes 1179652
  72.4 1.8 %copy-start.16 = (f32[6,256]{1,0:T(8,128)}, f32[6,256]{1,0:T(8,128)S(1)}, u32[]{:S(2)}) copy-start(f32[6,256]{1,0:T(8,128)S(1)} %fusion.14) | copy-start | bytes 18436
  73.8 2.5 %copy-start.11 = (pred[256,6,128]{0,2,1:T(8,128)(4,1)S(1)}, pred[256,6,128]{0,2,1:T(8,128)(4,1)}, u32[]{:S(2)}) copy-start(pred[256,6,128]{0,2,1:T(8,128)(4,1)} %copy-done.9) | copy-start | bytes 589828
  74.2 2.1 %copy-start.17 = (f32[6,256]{1,0:T(8,128)S(1)}, f32[6,256]{1,0:T(8,128)}, u32[]{:S(2)}) copy-start(f32[6,256]{1,0:T(8,128)} %copy-done.16) | copy-start | bytes 18436
  96.9 8.9 %copy-start.7 = (bf16[256,768]{0,1:T(8,128)(2,1)S(1)}, bf16[256,768]{0,1:T(8,128)(2,1)}, u32[]{:S(2)}) copy-start(bf16[256,768]{0,1:T(8,128)(2,1)} %copy-done.6) | copy-start | bytes 1179652
  99.1 6.8 %copy-start.4 = (bf16[6,256,256]{1,2,0:T(8,128)(2,1)S(1)}, bf16[6,256,256]{1,2,0:T(8,128)(2,1)}, u32[]{:S(2)}) copy-start(bf16[6,256,256]{1,2,0:T(8,128)(2,1)} %copy-done.3) | copy-start | bytes 2359300
  99.1 7.1 %copy-start.2 = (bf16[6,256,768]{1,2,0:T(8,128)(2,1)S(1)}, bf16[6,256,768]{1,2,0:T(8,128)(2,1)}, u32[]{:S(2)}) copy-start(bf16[6,256,768]{1,2,0:T(8,128)(2,1)} %multiply_convert_fusion) | copy-start | bytes 7077892
  100.4 21.6 %collective-permute-start.2 = (bf16[2,256,768]{2,1,0:T(8,128)(2,1)}, bf16[2,256,768]{2,1,0:T(8,128)(2,1)}, u32[]{:S(2)}, u32[]{:S(2)}) collective-permute-start(bf16[2,256,768]{2,1,0:T(8,128)(2,1)} %get-tuple-element.20), channel_id=1, source_target_pairs={{0,1},{1,8},{8,9},{9,16},{16,17},{17,24},{24,25},{2,3},{3,10},{10,... | collective-permute-start | bytes 2359304 | tf_op jit(solution)/shard_map/ppermute | solution.py:18
  104.6 38.6 %collective-permute-start.3 = (bf16[2,256,768]{2,1,0:T(8,128)(2,1)}, bf16[2,256,768]{2,1,0:T(8,128)(2,1)}, u32[]{:S(2)}, u32[]{:S(2)}) collective-permute-start(bf16[2,256,768]{2,1,0:T(8,128)(2,1)} %get-tuple-element.21), channel_id=1, source_target_pairs={{1,0},{8,1},{9,8},{16,9},{17,16},{24,17},{25,24},{3,2},{10,3},{11,... | collective-permute-start | bytes 2359304 | tf_op jit(solution)/shard_map/ppermute | solution.py:20
  (1 other events, 0.9 us)
Sparse Core Ops, SparseCore 0:
  18.4 37.6 all-gather.1
  65.0 40.3 reduce-scatter.4
  108.7 42.8 reduce-scatter.2
where the time goes:
time: 160 us
  waiting for transfers between devices  67.6 us (42%)
  matrix products  34 us (21%)
  local copies, waits for them, and re-layouts  18.8 us (12%)
  between operations  14.1 us (9%)
  starting transfers between devices  13.4 us (8%)
  other arithmetic  11.7 us (7%)
    ppermute x2, waiting for transfers between devices, extended(): lax.ppermute(head, axis, [((i + 1) % count, i) for i in range(ends)])  34.9 us
    all_gather x1, waiting for transfers between devices, local(): lax.all_gather(grad_output, 'head', axis=1, tiled=True)  14.6 us
    ppermute x2, waiting for transfers between devices, extended(): lax.ppermute(tail, axis, [(i, (i + 1) % count) for i in range(ends)])  14.2 us
    ppermute x2, starting transfers between devices, extended(): lax.ppermute(tail, axis, [(i, (i + 1) % count) for i in range(ends)])  10.6 us
    unnamed x42, local copies, waits for them, and re-layouts  8.45 us
    dot_general x1, matrix products, local(): jnp.einsum('qhe,khe->hqk', g_rows, near_values, preferred_element_type=jn...  5.99 us
    another operation x2, local copies, waits for them, and re-layouts, local(): jnp.stack([key_wide.reshape(3 * frame, width), value_wide.reshape(3 * fra...  5.34 us
    dot_general x1, matrix products, local(): jnp.einsum('hqk,qhe->khe', video_half, g_rows, preferred_element_type=jnp...  5.29 us
  transfers between devices with their start and end apart: 7, of which 6 were waited for; matrix products, arithmetic and copies ran while one was open for 31% of the time, Pallas kernels for 0%

commit v1 on v0

v1 whole, which is shorter than its diff:
```python
import functools
import math

import jax
import jax.numpy as jnp
from jax import lax
from jax.experimental import pallas as pl
from jax.experimental.pallas import tpu as pltpu
from jax.sharding import PartitionSpec as P

HD = 128
TILE = 128
AUX = 16
SCALE = HD ** (-0.5)
SCALE2 = SCALE * math.log2(math.e)
OFF = 1e30
BF = jnp.bfloat16
F32 = jnp.float32


def nt(a, b):
    return lax.dot_general(a, b, (((1,), (1,)), ((), ())), preferred_element_type=F32)


def nn(a, b):
    return lax.dot_general(a, b, (((1,), (0,)), ((), ())), preferred_element_type=F32)


def tn(a, b):
    return lax.dot_general(a, b, (((0,), (0,)), ((), ())), preferred_element_type=F32)


def lanes(h):
    return slice(h * HD, (h + 1) * HD)


def source_tile(place, lists, tile, entry):
    slab, mate = place[0], place[1]
    listed = lists[tile, entry]
    owner = lax.shift_right_logical(listed, 1)
    source = jnp.where(owner == slab, 0, jnp.where(owner == mate, 1, 2))
    return pl.multiple_of((source * 2 + (listed & 1)) * TILE, TILE)


def stack_tiles(parts, wide):
    frame = parts[0].shape[0]
    for i, part in enumerate(parts):
        wide[i * frame : (i + 1) * frame, :] = part[...]


def forward_kernel(
    place, lists, q, k0, k1, k2, v0, v1, v2, tk, tv, out, lse, wide_k, wide_v
):
    stack_tiles((k0, k1, k2), wide_k)
    stack_tiles((v0, v1, v2), wide_v)
    heads = q.shape[1] // HD
    for tile in range(q.shape[0] // TILE):
        starts = [source_tile(place, lists, place[0] * 2 + tile, e) for e in range(3)]
        rows = slice(tile * TILE, (tile + 1) * TILE)
        for h in range(heads):
            cols = lanes(h)
            keys = jnp.concatenate(
                [wide_k[pl.ds(a, TILE), cols] for a in starts] + [tk[:, cols]], axis=0
            )
            values = jnp.concatenate(
                [wide_v[pl.ds(a, TILE), cols] for a in starts] + [tv[:, cols]], axis=0
            )
            score = nt(keys, q[rows, cols])
            top = jnp.max(score, axis=0, keepdims=True)
            weight = jnp.exp2((score - top) * SCALE2)
            total = jnp.sum(weight, axis=0, keepdims=True)
            prob = (weight * (1.0 / total)).astype(BF)
            out[rows, cols] = tn(prob, values)
            lse[tile * 8 : (tile + 1) * 8, cols] = jnp.broadcast_to(
                top * SCALE2 + jnp.log2(total), (8, TILE)
            )


def split(x, count):
    parts = []
    for _ in range(count):
        head = x.astype(BF).astype(F32)
        parts.append(head)
        x = x - head
    return parts


def grad_kernel(chunk, n, place, *refs):
    parts, (weight, attended, lse, message) = refs[:n], refs[n:]
    rank = place[2]
    total = None
    depth = weight.shape[1] // n
    for step in range(n):
        source = lax.rem(rank - step + n, n)
        block = weight[:, pl.ds(pl.multiple_of(source * depth, 128), depth)]
        term = nt(parts[step][...], block)
        total = term if total is None else total + term
    half = total.astype(BF)
    message[:TILE, :] = half
    wide = half.astype(F32)
    row = lax.broadcasted_iota(jnp.int32, (AUX, TILE), 0)
    for h in range(half.shape[1] // HD):
        cols = lanes(h)
        product = wide[:, cols] * attended[chunk * TILE : (chunk + 1) * TILE, cols]
        delta = jnp.sum(product.T, axis=0, keepdims=True)
        extra = split(delta, 2) + split(lse[chunk * 8 : chunk * 8 + 1, cols], 3)
        block = jnp.zeros((AUX, TILE), F32)
        for i, line in enumerate(extra):
            block = jnp.where(row == i, jnp.broadcast_to(line, (AUX, TILE)), block)
        message[TILE : TILE + AUX, cols] = block.astype(BF)


def read_message(message, cols):
    g = message[:TILE, cols]
    aux = message[TILE : TILE + AUX, cols].astype(F32)
    delta = aux[0:1] + aux[1:2]
    lse = (aux[2:3] + aux[3:4]) + aux[4:5]
    return g, delta, lse


def query_kernel(
    place, lists, q, k0, k1, k2, v0, v1, v2, tk, tv, m0, m1, out, wide_k, wide_v
):
    stack_tiles((k0, k1, k2), wide_k)
    stack_tiles((v0, v1, v2), wide_v)
    heads = q.shape[1] // HD
    for tile, message in enumerate((m0, m1)):
        starts = [source_tile(place, lists, place[0] * 2 + tile, e) for e in range(3)]
        rows = slice(tile * TILE, (tile + 1) * TILE)
        for h in range(heads):
            cols = lanes(h)
            g, delta, lse = read_message(message, cols)
            keys = jnp.concatenate(
                [wide_k[pl.ds(a, TILE), cols] for a in starts] + [tk[:, cols]], axis=0
            )
            values = jnp.concatenate(
                [wide_v[pl.ds(a, TILE), cols] for a in starts] + [tv[:, cols]], axis=0
            )
            prob = jnp.exp2(nt(keys, q[rows, cols]) * SCALE2 - lse)
            dscore = (prob * (nt(values, g) - delta)).astype(BF)
            out[rows, cols] = (SCALE * tn(dscore, keys)).astype(BF)


def listed(place, lists, slab, tile, key_tile):
    count = lists.shape[0]
    query_tile = slab * 2 + tile
    row = jnp.clip(query_tile, 0, count - 1)
    wanted = place[0] * 2 + key_tile
    found = (lists[row, 0] == wanted) | (lists[row, 1] == wanted) | (lists[row, 2] == wanted)
    found = found & (query_tile >= 0) & (query_tile < count)
    return jnp.where(found, 0.0, OFF)


def key_terms(place, lists, slab, tile, keys, values, q, message, cols):
    g, delta, lse = read_message(message, cols)
    score = nt(keys, q) * SCALE2
    pieces = []
    for i in range(2):
        block = score[i * TILE : (i + 1) * TILE]
        pieces.append(block - (lse + listed(place, lists, slab, tile, i)))
    if keys.shape[0] > 2 * TILE:
        pieces.append(score[2 * TILE :] - lse)
    prob = jnp.exp2(jnp.concatenate(pieces, axis=0))
    dscore = (prob * (nt(values, g) - delta)).astype(BF)
    return nn(dscore, q), nn(prob.astype(BF), g)


def near_kernel(
    place, lists, k, v, sk, sv, valid, q0, q1, a0, a1, b0, b1,
    key_acc, value_acc, keep_k, keep_v, send_k, send_v,
):
    frame = k.shape[0]
    half = keep_k.shape[0]
    live = valid[...] > 0
    for h in range(k.shape[1] // HD):
        cols = lanes(h)
        keys = jnp.concatenate([k[:, cols], sk[:, cols]], axis=0)
        values = jnp.concatenate([v[:, cols], sv[:, cols]], axis=0)
        key_sum = value_sum = None
        for who, (q, messages) in enumerate(((q0, (a0, a1)), (q1, (b0, b1)))):
            for tile, message in enumerate(messages):
                rows = slice(tile * TILE, (tile + 1) * TILE)
                dk, dv = key_terms(
                    place, lists, place[who], tile, keys, values, q[rows, cols], message, cols
                )
                key_sum = dk if key_sum is None else key_sum + dk
                value_sum = dv if value_sum is None else value_sum + dv
        key_acc[:, cols] = key_sum[:frame]
        value_acc[:, cols] = value_sum[:frame]
        text_k = jnp.where(live, key_sum[frame:] * SCALE, 0.0)
        text_v = jnp.where(live, value_sum[frame:], 0.0)
        keep_k[:, cols] = text_k[:half]
        keep_v[:, cols] = text_v[:half]
        send_k[:, cols] = text_k[half:].astype(BF)
        send_v[:, cols] = text_v[half:].astype(BF)


def far_kernel(place, lists, k, v, q, m0, m1, key_acc, value_acc, key_out, value_out):
    for h in range(k.shape[1] // HD):
        cols = lanes(h)
        key_sum = key_acc[:, cols]
        value_sum = value_acc[:, cols]
        for tile, message in enumerate((m0, m1)):
            rows = slice(tile * TILE, (tile + 1) * TILE)
            dk, dv = key_terms(
                place, lists, place[3], tile, k[:, cols], v[:, cols], q[rows, cols], message, cols
            )
            key_sum = key_sum + dk
            value_sum = value_sum + dv
        key_out[:, cols] = (key_sum * SCALE).astype(BF)
        value_out[:, cols] = value_sum.astype(BF)


def call(kernel, name, outs, scalars, arrays, scratch=(), flops=0, size=0):
    return pl.pallas_call(
        kernel,
        name=name,
        out_shape=outs,
        in_specs=[pl.BlockSpec(memory_space=pltpu.SMEM)] * scalars
        + [pl.BlockSpec(memory_space=pltpu.VMEM)] * (len(arrays) - scalars),
        out_specs=jax.tree.map(lambda _: pl.BlockSpec(memory_space=pltpu.VMEM), outs),
        scratch_shapes=list(scratch),
        compiler_params=pltpu.CompilerParams(vmem_limit_bytes=48 << 20),
        cost_estimate=pl.CostEstimate(flops=flops, bytes_accessed=size, transcendentals=0),
    )(*arrays)


def local(
    queries, keys, values, grad_output, out_weight, text_keys, text_values, mask_lists, text_owner
):
    frame, width = queries.shape
    text_count = text_keys.shape[0]
    both = ("seq", "rep")
    seqs, reps, ranks = lax.axis_size("seq"), lax.axis_size("rep"), lax.axis_size("head")
    groups = seqs * reps
    slab = lax.axis_index(both)
    mate = slab ^ 1
    other = jnp.where(slab & 1, slab + 1, slab - 1)
    place = jnp.stack([slab, mate, lax.axis_index("head"), other]).astype(jnp.int32)

    def swap(x, distance=1):
        return lax.ppermute(x, both, [(i, i ^ distance) for i in range(groups)])

    def relay(x):
        def target(i):
            if i % 2 == 0:
                return i + 2 if i + 2 < groups else i + 1
            return i - 2 if i >= 2 else i - 1

        return lax.ppermute(x, both, [(i, target(i)) for i in range(groups)])

    def ring(x):
        return lax.ppermute(x, "head", [(i, (i + 1) % ranks) for i in range(ranks)])

    parts = [[grad_output[:TILE]], [grad_output[TILE:]]]
    for _ in range(ranks - 1):
        for chunk in parts:
            chunk.append(ring(chunk[-1]))

    mate_k, mate_v, mate_q = swap(keys), swap(values), swap(queries)
    far_k, far_v, far_q = relay(mate_k), relay(mate_v), relay(mate_q)

    capacity = 2 * text_count // groups
    slots = groups // 2 * capacity
    stages = []
    distance = 2
    while distance < groups:
        stages.append(distance)
        distance *= 2
    offsets = [0]
    for d in reversed(stages):
        offsets = offsets + [o ^ d for o in offsets]
    owners = slab ^ jnp.repeat(jnp.asarray(offsets, jnp.int32), capacity)
    wanted = owners * capacity + jnp.tile(jnp.arange(capacity, dtype=jnp.int32), len(offsets))
    token = jnp.arange(text_count, dtype=jnp.int32)
    same = (text_owner[:, None] == text_owner[None, :]) & (token[None, :] < token[:, None])
    slot = text_owner * capacity + jnp.sum(same.astype(jnp.int32), axis=1)
    placing = wanted[:, None] == slot[None, :]
    valid = jnp.broadcast_to(
        jnp.any(placing, axis=1, keepdims=True).astype(F32), (slots, HD)
    )
    placing = placing.astype(BF)
    slot_k = jnp.dot(placing, text_keys, preferred_element_type=BF)
    slot_v = jnp.dot(placing, text_values, preferred_element_type=BF)

    wide = pltpu.VMEM((3 * frame, width), BF)
    sds = jax.ShapeDtypeStruct
    attended, lse = call(
        forward_kernel,
        "attend",
        (sds((frame, width), F32), sds((16, width), F32)),
        2,
        (place, mask_lists, queries, keys, mate_k, far_k, values, mate_v, far_v, text_keys, text_values),
        (wide, wide),
        flops=2 * 2 * frame * 640 * width,
        size=5 << 20,
    )
    messages = [
        call(
            functools.partial(grad_kernel, i, ranks),
            f"grad_heads_{i}",
            sds((TILE + AUX, width), BF),
            1,
            (place, *parts[i], out_weight, attended, lse),
            flops=2 * TILE * width * out_weight.shape[1],
            size=7 << 20,
        )
        for i in range(2)
    ]
    mates = [swap(m) for m in messages]
    fars = [relay(m) for m in mates]
    query_grads = call(
        query_kernel,
        "query_grads",
        sds((frame, width), BF),
        2,
        (place, mask_lists, queries, keys, mate_k, far_k, values, mate_v, far_v, text_keys, text_values, *messages),
        (wide, wide),
        flops=3 * 2 * frame * 640 * width,
        size=5 << 20,
    )
    key_acc, value_acc, keep_k, keep_v, send_k, send_v = call(
        near_kernel,
        "near_keys",
        (sds((frame, width), F32),) * 2
        + (sds((slots // 2, width), F32),) * 2
        + (sds((slots // 2, width), BF),) * 2,
        2,
        (place, mask_lists, keys, values, slot_k, slot_v, valid, queries, mate_q, *messages, *mates),
        flops=4 * 2 * 512 * 512 * width,
        size=8 << 20,
    )
    key_grads, value_grads = call(
        far_kernel,
        "far_keys",
        (sds((frame, width), BF),) * 2,
        2,
        (place, mask_lists, keys, values, far_q, *fars, key_acc, value_acc),
        flops=4 * 2 * 256 * 256 * width,
        size=5 << 20,
    )
    keep = jnp.concatenate([keep_k, keep_v], axis=1)
    send = jnp.concatenate([send_k, send_v], axis=1)
    for i, d in enumerate(stages):
        total = keep + swap(send, d).astype(F32)
        if i + 1 < len(stages):
            rows = total.shape[0] // 2
            keep, send = total[:rows], total[rows:].astype(BF)
    total = total.astype(BF)
    return query_grads, key_grads, value_grads, total[:, :width], total[:, width:]


def solution(mesh):
    rows = P(("seq", "rep"), "head")
    return jax.shard_map(
        local,
        mesh=mesh,
        in_specs=(rows, rows, rows, rows, P("head", None), P(None, "head"), P(None, "head"), P(), P()),
        out_specs=(rows,) * 5,
        check_vma=False,
    )
```

time: 160 us -> 91.1 us (0.57)
  waiting for transfers between devices: 67.6 us -> 33.4 us
  matrix products: 34 us -> 1.6 us
  Pallas kernels: 0 us -> 25.8 us
  between operations: 14.1 us -> 0.84 us
  local copies, waits for them, and re-layouts: 18.8 us -> 7.69 us
  other arithmetic: 11.7 us -> 2.77 us
  starting transfers between devices: 13.4 us -> 17.8 us
    dot_general x15 -> x2, matrix products: 34 us -> 1.6 us  [the longest x1 1.3 us: local(): slot_v = jnp.dot(placing, text_values, preferred_element_type=BF)]
    pallas_call x0 -> x6, Pallas kernels: none -> 25.8 us  [call(): pl.pallas_call(kernel, name=name, out_shape=outs, in_specs=[pl.BlockSpec(...]
    ppermute x4 -> x18, waiting for transfers between devices: 49 us -> 33.4 us  [the longest x7 22.5 us: swap(): return lax.ppermute(x, both, [(i, i ^ distance) for i in range(groups)])]
    all_gather x1 -> x0, waiting for transfers between devices: 14.6 us -> none  [local(): lax.all_gather(grad_output, 'head', axis=1, tiled=True)]
    another operation x5 -> x1, other arithmetic: 5.62 us -> 0.08 us  [local(): jnp.stack([slab, mate, lax.axis_index('head'), other]).astype(jnp.int32)]
    another operation x3 -> x0, local copies, waits for them, and re-layouts: 5.34 us -> none  [the longest x2 5.34 us: local(): jnp.stack([key_wide.reshape(3 * frame, width), value_wide.reshape(3 * fra...]
    ppermute x4 -> x18, starting transfers between devices: 13.1 us -> 17.8 us  [the longest x6 7.99 us: ring(): return lax.ppermute(x, 'head', [(i, (i + 1) % ranks) for i in range(ranks)])]
    reduce_scatter x2 -> x0, waiting for transfers between devices: 3.95 us -> none  [the longest x1 3.95 us: local(): lax.psum_scatter(key_slots, ('seq', 'rep'), scatter_dimension=0, tiled=True)]
  transfers between devices with their start and end apart: 7 -> 18, of which waited for: 6 -> 9; matrix products, arithmetic and copies ran while one was open for 31% -> 6% of each run, Pallas kernels for 0% -> 22%
where the time goes in v1:
time: 91.1 us; the launch traced here: 89.9 us
  waiting for transfers between devices  33.4 us (37%)
  Pallas kernels  25.8 us (28%)
  starting transfers between devices  17.8 us (20%)
  local copies, waits for them, and re-layouts  7.69 us (8%)
  other arithmetic  2.77 us (3%)
  matrix products  1.6 us (2%)
    pallas_call x6, Pallas kernels, call(): pl.pallas_call(kernel, name=name, out_shape=outs, in_specs=[pl.BlockSpec(...  25.8 us
    ppermute x7, waiting for transfers between devices, swap(): return lax.ppermute(x, both, [(i, i ^ distance) for i in range(groups)])  22.5 us
    ppermute x5, waiting for transfers between devices, relay(): return lax.ppermute(x, both, [(i, target(i)) for i in range(groups)])  8.22 us
    ppermute x6, starting transfers between devices, ring(): return lax.ppermute(x, 'head', [(i, (i + 1) % ranks) for i in range(ranks)])  7.99 us
    ppermute x7, starting transfers between devices, swap(): return lax.ppermute(x, both, [(i, i ^ distance) for i in range(groups)])  7.51 us
    unnamed x19, local copies, waits for them, and re-layouts  5.76 us
    ppermute x6, waiting for transfers between devices, ring(): return lax.ppermute(x, 'head', [(i, (i + 1) % ranks) for i in range(ranks)])  2.73 us
    ppermute x5, starting transfers between devices, relay(): return lax.ppermute(x, both, [(i, target(i)) for i in range(groups)])  2.3 us
  transfers between devices with their start and end apart: 18, of which 9 were waited for; matrix products, arithmetic and copies ran while one was open for 6% of the time, Pallas kernels for 22%

profile of v1, /device:TPU:0, one launch (start us, length us, event | category | flops | bytes accessed | tf_op | source)
XLA Modules:
  0.0 89.9 jit_solution(10840473093744966033)
XLA Ops:
  1.7 3.1 %collective-permute-start.7 = (bf16[128,768]{1,0:T(8,128)(2,1)S(1)}, bf16[128,768]{1,0:T(8,128)(2,1)S(1)}, u32[]{:S(2)}, u32[]{:S(2)}) collective-permute-start(bf16[128,768]{1,0:T(8,128)(2,1)S(1)} %get-tuple-element.25.refs_0_), channel_id=1, source_target_pairs={{0,2},{2,4},{4,6},{6,0},{1,3},{3,5},{5,7},{7,1},{8,10},{10,12},{12... | collective-permute-start | bytes 589832 | tf_op jit(solution)/shard_map/ppermute | solution.py:253
  4.8 1.6 %collective-permute-start.4 = (bf16[128,768]{1,0:T(8,128)(2,1)S(1)}, bf16[128,768]{1,0:T(8,128)(2,1)S(1)}, u32[]{:S(2)}, u32[]{:S(2)}) collective-permute-start(bf16[128,768]{1,0:T(8,128)(2,1)S(1)} %get-tuple-element.26.refs_0_), channel_id=1, source_target_pairs={{0,2},{2,4},{4,6},{6,0},{1,3},{3,5},{5,7},{7,1},{8,10},{10,12},{12... | collective-permute-start | bytes 589832 | tf_op jit(solution)/shard_map/ppermute | solution.py:253
  6.3 1.5 %collective-permute-start.10 = (bf16[256,768]{1,0:T(8,128)(2,1)}, bf16[256,768]{1,0:T(8,128)(2,1)}, u32[]{:S(2)}, u32[]{:S(2)}) collective-permute-start(bf16[256,768]{1,0:T(8,128)(2,1)} %q0.1), channel_id=1, source_target_pairs={{0,1},{1,0},{8,9},{9,8},{16,17},{17,16},{24,25},{25,24},{2,3},{3,2... | collective-permute-start | bytes 1179656 | tf_op jit(solution)/shard_map/ppermute | solution.py:242
  8.4 1.5 %collective-permute-start.2 = (bf16[256,768]{1,0:T(8,128)(2,1)}, bf16[256,768]{1,0:T(8,128)(2,1)S(1)}, u32[]{:S(2)}, u32[]{:S(2)}) collective-permute-start(bf16[256,768]{1,0:T(8,128)(2,1)} %v.3), channel_id=1, source_target_pairs={{0,1},{1,0},{8,9},{9,8},{16,17},{17,16},{24,25},{25,24},{2,3},{3,2... | collective-permute-start | bytes 1179656 | tf_op jit(solution)/shard_map/ppermute | solution.py:242
  12.5 1.4 %collective-permute-start.8 = (bf16[128,768]{1,0:T(8,128)(2,1)S(1)}, bf16[128,768]{1,0:T(8,128)(2,1)S(1)}, u32[]{:S(2)}, u32[]{:S(2)}) collective-permute-start(bf16[128,768]{1,0:T(8,128)(2,1)S(1)} %collective-permute-done.7.refs_1_), channel_id=1, source_target_pairs={{0,2},{2,4},{4,6},{6,0},{1,3},{3,5},{5,7},{7,1},{8,10},{10,12},{12... | collective-permute-start | bytes 589832 | tf_op jit(solution)/shard_map/ppermute | solution.py:253
  13.9 2.5 %collective-permute-done.4.refs_1_ = bf16[128,768]{1,0:T(8,128)(2,1)S(1)} collective-permute-done((bf16[128,768]{1,0:T(8,128)(2,1)S(1)}, bf16[128,768]{1,0:T(8,128)(2,1)S(1)}, u32[]{:S(2)}, u32[]{:S(2)}) %collective-permute-start.4) | collective-permute-done | bytes 196640 | tf_op jit(solution)/shard_map/ppermute | solution.py:253
  16.4 10.7 %collective-permute-done.k1 = bf16[256,768]{1,0:T(8,128)(2,1)S(1)} collective-permute-done((bf16[256,768]{1,0:T(8,128)(2,1)}, bf16[256,768]{1,0:T(8,128)(2,1)S(1)}, u32[]{:S(2)}, u32[]{:S(2)}) %collective-permute-start) | collective-permute-done | bytes 393248 | tf_op jit(solution)/shard_map/ppermute | solution.py:242
  27.0 6.7 %collective-permute-done.2.v1 = bf16[256,768]{1,0:T(8,128)(2,1)S(1)} collective-permute-done((bf16[256,768]{1,0:T(8,128)(2,1)}, bf16[256,768]{1,0:T(8,128)(2,1)S(1)}, u32[]{:S(2)}, u32[]{:S(2)}) %collective-permute-start.2) | collective-permute-done | bytes 393248 | tf_op jit(solution)/shard_map/ppermute | solution.py:242
  33.7 1.3 %fusion.sv = bf16[256,768]{1,0:T(8,128)(2,1)S(1)} fusion(bf16[256,768]{1,0:T(8,128)(2,1)} %tv.3, s32[256]{0:T(256)S(1)} %multiply_add_fusion, s32[256]{0:T(256)S(1)} %add.29), kind=kOutput, calls=%fused_computation.2 | convolution fusion | flops 100728832 | bytes 788480 | tf_op jit(solution)/shard_map/dot_general | solution.py:284
  35.0 1.6 %collective-permute-start.6 = (bf16[128,768]{1,0:T(8,128)(2,1)S(1)}, bf16[128,768]{1,0:T(8,128)(2,1)S(1)}, u32[]{:S(2)}, u32[]{:S(2)}) collective-permute-start(bf16[128,768]{1,0:T(8,128)(2,1)S(1)} %collective-permute-done.5.refs_2_), channel_id=1, source_target_pairs={{0,2},{2,4},{4,6},{6,0},{1,3},{3,5},{5,7},{7,1},{8,10},{10,12},{12... | collective-permute-start | bytes 589832 | tf_op jit(solution)/shard_map/ppermute | solution.py:253
  38.0 4.1 %collective-permute-done.3.v2 = bf16[256,768]{1,0:T(8,128)(2,1)S(1)} collective-permute-done((bf16[256,768]{1,0:T(8,128)(2,1)S(1)}, bf16[256,768]{1,0:T(8,128)(2,1)S(1)}, u32[]{:S(2)}, u32[]{:S(2)}) %collective-permute-start.3) | collective-permute-done | bytes 393248 | tf_op jit(solution)/shard_map/ppermute | solution.py:250
  47.1 2.6 %attend.1 = (f32[256,768]{1,0:T(8,128)S(1)}, f32[16,768]{1,0:T(8,128)S(1)}) custom-call(s32[4]{0:T(128)S(1)} %pad_add_fusion.place, s32[16,3]{1,0:T(8,128)S(1)} %copy.20.lists, bf16[256,768]{1,0:T(8,128)(2,1)S(1)} %copy-done.8, bf16[256,768]{1,0:T(8,128)(2,1)S(1)} %copy-done.4, bf16[256,768]{1,0:T(8,128)(2,1)S(1)} %collective-permute-done.k1, ...), custom_call_target="tpu_custom_call" | custom-call | flops 503316480 | bytes 5242880 | tf_op jit(solution)/shard_map/attend/pallas_call | solution.py:215
  49.7 4.1 %grad_heads_0.1.m0.a0 = bf16[144,768]{1,0:T(8,128)(2,1)S(1)} custom-call(s32[4]{0:T(128)S(1)} %pad_add_fusion.place, bf16[128,768]{1,0:T(8,128)(2,1)S(1)} %get-tuple-element.26.refs_0_, bf16[128,768]{1,0:T(8,128)(2,1)S(1)} %collective-permute-done.4.refs_1_, bf16[128,768]{1,0:T(8,128)(2,1)S(1)} %collective-permute-done.5.refs_2_, ...), custom_call_target="tpu_custom_call" | custom-call | flops 603979776 | bytes 7340032 | tf_op jit(solution)/shard_map/grad_heads_0/pallas_call | solution.py:215
  54.0 4.2 %grad_heads_1.1.m1.a1 = bf16[144,768]{1,0:T(8,128)(2,1)S(1)} custom-call(s32[4]{0:T(128)S(1)} %pad_add_fusion.place, bf16[128,768]{1,0:T(8,128)(2,1)S(1)} %get-tuple-element.25.refs_0_, bf16[128,768]{1,0:T(8,128)(2,1)S(1)} %collective-permute-done.7.refs_1_, bf16[128,768]{1,0:T(8,128)(2,1)S(1)} %collective-permute-done.8.refs_2_, ...), custom_call_target="tpu_custom_call" | custom-call | flops 603979776 | bytes 7340032 | tf_op jit(solution)/shard_map/grad_heads_1/pallas_call | solution.py:215
  58.2 2.0 %collective-permute-start.14 = (bf16[144,768]{1,0:T(8,128)(2,1)S(1)}, bf16[144,768]{1,0:T(8,128)(2,1)S(1)}, u32[]{:S(2)}, u32[]{:S(2)}) collective-permute-start(bf16[144,768]{1,0:T(8,128)(2,1)S(1)} %grad_heads_1.1.m1.a1), channel_id=1, source_target_pairs={{0,1},{1,0},{8,9},{9,8},{16,17},{17,16},{24,25},{25,24},{2,3},{3,2... | collective-permute-start | bytes 663560 | tf_op jit(solution)/shard_map/ppermute | solution.py:242
  60.6 1.2 %collective-permute-done.12.b0 = bf16[144,768]{1,0:T(8,128)(2,1)S(1)} collective-permute-done((bf16[144,768]{1,0:T(8,128)(2,1)S(1)}, bf16[144,768]{1,0:T(8,128)(2,1)S(1)}, u32[]{:S(2)}, u32[]{:S(2)}) %collective-permute-start.12) | collective-permute-done | bytes 221216 | tf_op jit(solution)/shard_map/ppermute | solution.py:242
  61.8 3.9 %collective-permute-done.14.b1 = bf16[144,768]{1,0:T(8,128)(2,1)S(1)} collective-permute-done((bf16[144,768]{1,0:T(8,128)(2,1)S(1)}, bf16[144,768]{1,0:T(8,128)(2,1)S(1)}, u32[]{:S(2)}, u32[]{:S(2)}) %collective-permute-start.14) | collective-permute-done | bytes 221216 | tf_op jit(solution)/shard_map/ppermute | solution.py:242
  65.8 6.0 %near_keys.1 = (f32[256,768]{1,0:T(8,128)S(1)}, f32[256,768]{1,0:T(8,128)S(1)}, f32[128,768]{1,0:T(8,128)S(1)}, f32[128,768]{1,0:T(8,128)S(1)}, bf16[128,768]{1,...) custom-call(s32[4]{0:T(128)S(1)} %pad_add_fusion.place, s32[16,3]{1,0:T(8,128)S(1)} %copy.20.lists, ...), custom_call_target="tpu_custom_call" | custom-call | flops 1610612736 | bytes 8388608 | tf_op jit(solution)/shard_map/near_keys/pallas_call | solution.py:215
  72.7 1.8 %collective-permute-start.13 = (bf16[144,768]{1,0:T(8,128)(2,1)S(1)}, bf16[144,768]{1,0:T(8,128)(2,1)S(1)}, u32[]{:S(2)}, u32[]{:S(2)}) collective-permute-start(bf16[144,768]{1,0:T(8,128)(2,1)S(1)} %collective-permute-done.12.b0), channel_id=1, source_target_pairs={{0,8},{1,0},{8,16},{9,1},{16,24},{17,9},{24,25},{25,17},{2,10},{3,... | collective-permute-start | bytes 663560 | tf_op jit(solution)/shard_map/ppermute | solution.py:250
  75.0 1.2 %collective-permute-start.17 = (bf16[64,1536]{1,0:T(8,128)(2,1)S(1)}, bf16[64,1536]{1,0:T(8,128)(2,1)S(1)}, u32[]{:S(2)}, u32[]{:S(2)}) collective-permute-start(bf16[64,1536]{1,0:T(8,128)(2,1)S(1)} %slice.33), channel_id=1, source_target_pairs={{0,16},{1,17},{8,24},{9,25},{16,0},{17,1},{24,8},{25,9},{2,18},{3,... | collective-permute-start | bytes 589832 | tf_op jit(solution)/shard_map/ppermute | solution.py:242
  76.2 5.0 %query_grads.1 = bf16[256,768]{1,0:T(8,128)(2,1)} custom-call(s32[4]{0:T(128)S(1)} %pad_add_fusion.place, s32[16,3]{1,0:T(8,128)S(1)} %copy.20.lists, bf16[256,768]{1,0:T(8,128)(2,1)S(1)} %copy-done.8, bf16[256,768]{1,0:T(8,128)(2,1)S(1)} %copy-done.5, bf16[256,768]{1,0:T(8,128)(2,1)S(1)} %collective-permute-done.k1, ...), custom_call_target="tpu_custom_call" | custom-call | flops 754974720 | bytes 5242880 | tf_op jit(solution)/shard_map/query_grads/pallas_call | solution.py:215
  81.2 1.7 %collective-permute-done.13.m0 = bf16[144,768]{1,0:T(8,128)(2,1)S(1)} collective-permute-done((bf16[144,768]{1,0:T(8,128)(2,1)S(1)}, bf16[144,768]{1,0:T(8,128)(2,1)S(1)}, u32[]{:S(2)}, u32[]{:S(2)}) %collective-permute-start.13) | collective-permute-done | bytes 221216 | tf_op jit(solution)/shard_map/ppermute | solution.py:250
  83.0 2.4 %collective-permute-done.15.m1 = bf16[144,768]{1,0:T(8,128)(2,1)S(1)} collective-permute-done((bf16[144,768]{1,0:T(8,128)(2,1)S(1)}, bf16[144,768]{1,0:T(8,128)(2,1)S(1)}, u32[]{:S(2)}, u32[]{:S(2)}) %collective-permute-start.15) | collective-permute-done | bytes 221216 | tf_op jit(solution)/shard_map/ppermute | solution.py:250
  85.3 3.8 %far_keys.1 = (bf16[256,768]{1,0:T(8,128)(2,1)}, bf16[256,768]{1,0:T(8,128)(2,1)}) custom-call(s32[4]{0:T(128)S(1)} %pad_add_fusion.place, s32[16,3]{1,0:T(8,128)S(1)} %copy.20.lists, bf16[256,768]{1,0:T(8,128)(2,1)S(1)} %copy-done.5, bf16[256,768]{1,0:T(8,128)(2,1)S(1)} %copy-done.7, bf16[256,768]{1,0:T(8,128)(2,1)S(1)} %collective-permute-done.11.q, ...), custom_call_target="tpu_custom_call" | custom-call | flops 402653184 | bytes 5242880 | tf_op jit(solution)/shard_map/far_keys/pallas_call | solution.py:215
  (54 shorter events, 13.2 us)
Async XLA Ops:
  1.7 10.8 %collective-permute-start.7 = (bf16[128,768]{1,0:T(8,128)(2,1)S(1)}, bf16[128,768]{1,0:T(8,128)(2,1)S(1)}, u32[]{:S(2)}, u32[]{:S(2)}) collective-permute-start(bf16[128,768]{1,0:T(8,128)(2,1)S(1)} %get-tuple-element.25.refs_0_), channel_id=1, source_target_pairs={{0,2},{2,4},{4,6},{6,0},{1,3},{3,5},{5,7},{7,1},{8,10},{10,12},{12... | collective-permute-start | bytes 589832 | tf_op jit(solution)/shard_map/ppermute | solution.py:253
  4.8 11.6 %collective-permute-start.4 = (bf16[128,768]{1,0:T(8,128)(2,1)S(1)}, bf16[128,768]{1,0:T(8,128)(2,1)S(1)}, u32[]{:S(2)}, u32[]{:S(2)}) collective-permute-start(bf16[128,768]{1,0:T(8,128)(2,1)S(1)} %get-tuple-element.26.refs_0_), channel_id=1, source_target_pairs={{0,2},{2,4},{4,6},{6,0},{1,3},{3,5},{5,7},{7,1},{8,10},{10,12},{12... | collective-permute-start | bytes 589832 | tf_op jit(solution)/shard_map/ppermute | solution.py:253
  6.3 54.2 %collective-permute-start.10 = (bf16[256,768]{1,0:T(8,128)(2,1)}, bf16[256,768]{1,0:T(8,128)(2,1)}, u32[]{:S(2)}, u32[]{:S(2)}) collective-permute-start(bf16[256,768]{1,0:T(8,128)(2,1)} %q0.1), channel_id=1, source_target_pairs={{0,1},{1,0},{8,9},{9,8},{16,17},{17,16},{24,25},{25,24},{2,3},{3,2... | collective-permute-start | bytes 1179656 | tf_op jit(solution)/shard_map/ppermute | solution.py:242
  7.8 19.2 %collective-permute-start = (bf16[256,768]{1,0:T(8,128)(2,1)}, bf16[256,768]{1,0:T(8,128)(2,1)S(1)}, u32[]{:S(2)}, u32[]{:S(2)}) collective-permute-start(bf16[256,768]{1,0:T(8,128)(2,1)} %k.3), channel_id=1, source_target_pairs={{0,1},{1,0},{8,9},{9,8},{16,17},{17,16},{24,25},{25,24},{2,3},{3,2... | collective-permute-start | bytes 1179656 | tf_op jit(solution)/shard_map/ppermute | solution.py:242
  8.4 25.3 %collective-permute-start.2 = (bf16[256,768]{1,0:T(8,128)(2,1)}, bf16[256,768]{1,0:T(8,128)(2,1)S(1)}, u32[]{:S(2)}, u32[]{:S(2)}) collective-permute-start(bf16[256,768]{1,0:T(8,128)(2,1)} %v.3), channel_id=1, source_target_pairs={{0,1},{1,0},{8,9},{9,8},{16,17},{17,16},{24,25},{25,24},{2,3},{3,2... | collective-permute-start | bytes 1179656 | tf_op jit(solution)/shard_map/ppermute | solution.py:242
  12.5 25.1 %collective-permute-start.8 = (bf16[128,768]{1,0:T(8,128)(2,1)S(1)}, bf16[128,768]{1,0:T(8,128)(2,1)S(1)}, u32[]{:S(2)}, u32[]{:S(2)}) collective-permute-start(bf16[128,768]{1,0:T(8,128)(2,1)S(1)} %collective-permute-done.7.refs_1_), channel_id=1, source_target_pairs={{0,2},{2,4},{4,6},{6,0},{1,3},{3,5},{5,7},{7,1},{8,10},{10,12},{12... | collective-permute-start | bytes 589832 | tf_op jit(solution)/shard_map/ppermute | solution.py:253
  16.4 18.6 %collective-permute-start.5 = (bf16[128,768]{1,0:T(8,128)(2,1)S(1)}, bf16[128,768]{1,0:T(8,128)(2,1)S(1)}, u32[]{:S(2)}, u32[]{:S(2)}) collective-permute-start(bf16[128,768]{1,0:T(8,128)(2,1)S(1)} %collective-permute-done.4.refs_1_), channel_id=1, source_target_pairs={{0,2},{2,4},{4,6},{6,0},{1,3},{3,5},{5,7},{7,1},{8,10},{10,12},{12... | collective-permute-start | bytes 589832 | tf_op jit(solution)/shard_map/ppermute | solution.py:253
  27.0 11.0 %collective-permute-start.1 = (bf16[256,768]{1,0:T(8,128)(2,1)S(1)}, bf16[256,768]{1,0:T(8,128)(2,1)S(1)}, u32[]{:S(2)}, u32[]{:S(2)}) collective-permute-start(bf16[256,768]{1,0:T(8,128)(2,1)S(1)} %collective-permute-done.k1), channel_id=1, source_target_pairs={{0,8},{1,0},{8,16},{9,1},{16,24},{17,9},{24,25},{25,17},{2,10},{3,... | collective-permute-start | bytes 1179656 | tf_op jit(solution)/shard_map/ppermute | solution.py:250
  33.7 8.4 %collective-permute-start.3 = (bf16[256,768]{1,0:T(8,128)(2,1)S(1)}, bf16[256,768]{1,0:T(8,128)(2,1)S(1)}, u32[]{:S(2)}, u32[]{:S(2)}) collective-permute-start(bf16[256,768]{1,0:T(8,128)(2,1)S(1)} %collective-permute-done.2.v1), channel_id=1, source_target_pairs={{0,8},{1,0},{8,16},{9,1},{16,24},{17,9},{24,25},{25,17},{2,10},{3,... | collective-permute-start | bytes 1179656 | tf_op jit(solution)/shard_map/ppermute | solution.py:250
  35.0 14.7 %collective-permute-start.6 = (bf16[128,768]{1,0:T(8,128)(2,1)S(1)}, bf16[128,768]{1,0:T(8,128)(2,1)S(1)}, u32[]{:S(2)}, u32[]{:S(2)}) collective-permute-start(bf16[128,768]{1,0:T(8,128)(2,1)S(1)} %collective-permute-done.5.refs_2_), channel_id=1, source_target_pairs={{0,2},{2,4},{4,6},{6,0},{1,3},{3,5},{5,7},{7,1},{8,10},{10,12},{12... | collective-permute-start | bytes 589832 | tf_op jit(solution)/shard_map/ppermute | solution.py:253
  37.6 16.4 %collective-permute-start.9 = (bf16[128,768]{1,0:T(8,128)(2,1)S(1)}, bf16[128,768]{1,0:T(8,128)(2,1)S(1)}, u32[]{:S(2)}, u32[]{:S(2)}) collective-permute-start(bf16[128,768]{1,0:T(8,128)(2,1)S(1)} %collective-permute-done.8.refs_2_), channel_id=1, source_target_pairs={{0,2},{2,4},{4,6},{6,0},{1,3},{3,5},{5,7},{7,1},{8,10},{10,12},{12... | collective-permute-start | bytes 589832 | tf_op jit(solution)/shard_map/ppermute | solution.py:253
  42.1 1.0 %copy-start = (bf16[256,768]{1,0:T(8,128)(2,1)S(1)}, bf16[256,768]{1,0:T(8,128)(2,1)}, u32[]{:S(2)}) copy-start(bf16[256,768]{1,0:T(8,128)(2,1)} %tk.3) | copy-start | bytes 1179652
  43.1 1.0 %copy-start.2 = (bf16[256,768]{1,0:T(8,128)(2,1)S(1)}, bf16[256,768]{1,0:T(8,128)(2,1)}, u32[]{:S(2)}) copy-start(bf16[256,768]{1,0:T(8,128)(2,1)} %tv.3) | copy-start | bytes 1179652
  53.9 11.9 %copy-start.5 = (bf16[256,768]{1,0:T(8,128)(2,1)S(1)}, bf16[256,768]{1,0:T(8,128)(2,1)}, u32[]{:S(2)}) copy-start(bf16[256,768]{1,0:T(8,128)(2,1)} %k.3) | copy-start | bytes 1179652
  53.9 11.9 %copy-start.7 = (bf16[256,768]{1,0:T(8,128)(2,1)S(1)}, bf16[256,768]{1,0:T(8,128)(2,1)}, u32[]{:S(2)}) copy-start(bf16[256,768]{1,0:T(8,128)(2,1)} %v.3) | copy-start | bytes 1179652
  53.9 7.9 %collective-permute-start.12 = (bf16[144,768]{1,0:T(8,128)(2,1)S(1)}, bf16[144,768]{1,0:T(8,128)(2,1)S(1)}, u32[]{:S(2)}, u32[]{:S(2)}) collective-permute-start(bf16[144,768]{1,0:T(8,128)(2,1)S(1)} %grad_heads_0.1.m0.a0), channel_id=1, source_target_pairs={{0,1},{1,0},{8,9},{9,8},{16,17},{17,16},{24,25},{25,24},{2,3},{3,2... | collective-permute-start | bytes 663560 | tf_op jit(solution)/shard_map/ppermute | solution.py:242
  58.2 7.5 %collective-permute-start.14 = (bf16[144,768]{1,0:T(8,128)(2,1)S(1)}, bf16[144,768]{1,0:T(8,128)(2,1)S(1)}, u32[]{:S(2)}, u32[]{:S(2)}) collective-permute-start(bf16[144,768]{1,0:T(8,128)(2,1)S(1)} %grad_heads_1.1.m1.a1), channel_id=1, source_target_pairs={{0,1},{1,0},{8,9},{9,8},{16,17},{17,16},{24,25},{25,24},{2,3},{3,2... | collective-permute-start | bytes 663560 | tf_op jit(solution)/shard_map/ppermute | solution.py:242
  60.5 15.6 %copy-start.1 = (bf16[256,768]{1,0:T(8,128)(2,1)S(1)}, bf16[256,768]{1,0:T(8,128)(2,1)}, u32[]{:S(2)}) copy-start(bf16[256,768]{1,0:T(8,128)(2,1)} %tk.3) | copy-start | bytes 1179652
  60.5 15.6 %copy-start.3 = (bf16[256,768]{1,0:T(8,128)(2,1)S(1)}, bf16[256,768]{1,0:T(8,128)(2,1)}, u32[]{:S(2)}) copy-start(bf16[256,768]{1,0:T(8,128)(2,1)} %tv.3) | copy-start | bytes 1179652
  71.8 3.0 %collective-permute-start.16 = (bf16[128,1536]{1,0:T(8,128)(2,1)S(1)}, bf16[128,1536]{1,0:T(8,128)(2,1)S(1)}, u32[]{:S(2)}, u32[]{:S(2)}) collective-permute-start(bf16[128,1536]{1,0:T(8,128)(2,1)S(1)} %pad_maximum_fusion), channel_id=1, source_target_pairs={{0,8},{1,9},{8,0},{9,1},{16,24},{17,25},{24,16},{25,17},{2,10},{3,... | collective-permute-start | bytes 1179656 | tf_op jit(solution)/shard_map/ppermute | solution.py:242
  72.6 8.6 %collective-permute-start.11 = (bf16[256,768]{1,0:T(8,128)(2,1)}, bf16[256,768]{1,0:T(8,128)(2,1)S(1)}, u32[]{:S(2)}, u32[]{:S(2)}) collective-permute-start(bf16[256,768]{1,0:T(8,128)(2,1)} %collective-permute-done.10.q1), channel_id=1, source_target_pairs={{0,8},{1,0},{8,16},{9,1},{16,24},{17,9},{24,25},{25,17},{2,10},{3,... | collective-permute-start | bytes 1179656 | tf_op jit(solution)/shard_map/ppermute | solution.py:250
  72.7 10.3 %collective-permute-start.13 = (bf16[144,768]{1,0:T(8,128)(2,1)S(1)}, bf16[144,768]{1,0:T(8,128)(2,1)S(1)}, u32[]{:S(2)}, u32[]{:S(2)}) collective-permute-start(bf16[144,768]{1,0:T(8,128)(2,1)S(1)} %collective-permute-done.12.b0), channel_id=1, source_target_pairs={{0,8},{1,0},{8,16},{9,1},{16,24},{17,9},{24,25},{25,17},{2,10},{3,... | collective-permute-start | bytes 663560 | tf_op jit(solution)/shard_map/ppermute | solution.py:250
  74.5 10.9 %collective-permute-start.15 = (bf16[144,768]{1,0:T(8,128)(2,1)S(1)}, bf16[144,768]{1,0:T(8,128)(2,1)S(1)}, u32[]{:S(2)}, u32[]{:S(2)}) collective-permute-start(bf16[144,768]{1,0:T(8,128)(2,1)S(1)} %collective-permute-done.14.b1), channel_id=1, source_target_pairs={{0,8},{1,0},{8,16},{9,1},{16,24},{17,9},{24,25},{25,17},{2,10},{3,... | collective-permute-start | bytes 663560 | tf_op jit(solution)/shard_map/ppermute | solution.py:250
  75.0 14.2 %collective-permute-start.17 = (bf16[64,1536]{1,0:T(8,128)(2,1)S(1)}, bf16[64,1536]{1,0:T(8,128)(2,1)S(1)}, u32[]{:S(2)}, u32[]{:S(2)}) collective-permute-start(bf16[64,1536]{1,0:T(8,128)(2,1)S(1)} %slice.33), channel_id=1, source_target_pairs={{0,16},{1,17},{8,24},{9,25},{16,0},{17,1},{24,8},{25,9},{2,18},{3,... | collective-permute-start | bytes 589832 | tf_op jit(solution)/shard_map/ppermute | solution.py:242
  (3 other events, 3.0 us)

commit v2 on v1

v2 whole, which is shorter than its diff:
```python
import functools
import math

import jax
import jax.numpy as jnp
from jax import lax
from jax.experimental import pallas as pl
from jax.experimental.pallas import tpu as pltpu
from jax.sharding import PartitionSpec as P

HD = 128
TILE = 128
AUX = 16
SCALE = HD ** (-0.5)
SCALE2 = SCALE * math.log2(math.e)
OFF = 1e30
BF = jnp.bfloat16
F32 = jnp.float32
LIMIT = 16 << 20


def nt(a, b):
    return lax.dot_general(a, b, (((1,), (1,)), ((), ())), preferred_element_type=F32)


def nn(a, b):
    return lax.dot_general(a, b, (((1,), (0,)), ((), ())), preferred_element_type=F32)


def tn(a, b):
    return lax.dot_general(a, b, (((0,), (0,)), ((), ())), preferred_element_type=F32)


def lanes(h):
    return slice(h * HD, (h + 1) * HD)


def source_tile(place, lists, tile, entry):
    slab, mate = place[0], place[1]
    listed = lists[tile, entry]
    owner = lax.shift_right_logical(listed, 1)
    source = jnp.where(owner == slab, 0, jnp.where(owner == mate, 1, 2))
    return pl.multiple_of((source * 2 + (listed & 1)) * TILE, TILE)


def stack_tiles(parts, wide):
    frame = parts[0].shape[0]
    for i, part in enumerate(parts):
        wide[i * frame : (i + 1) * frame, :] = part[...]


def slot_kernel(capacity, place, owner, tk, tv, sk, sv, valid):
    count = owner.shape[1]
    slots = sk.shape[0]
    across = jnp.broadcast_to(owner[...], (count, count))
    down = across.astype(F32).T.astype(jnp.int32)
    line = lax.broadcasted_iota(jnp.int32, (count, count), 0)
    lane = lax.broadcasted_iota(jnp.int32, (count, count), 1)
    rank = jnp.sum(
        jnp.where((across == down) & (line < lane), 1, 0), axis=0, keepdims=True
    )
    slot = owner[...] * capacity + rank
    row = lax.broadcasted_iota(jnp.int32, (slots, count), 0)
    group, inside = row // capacity, row % capacity
    bits = (slots // capacity).bit_length() - 1
    offset = jnp.zeros_like(row)
    for bit in range(bits):
        offset = offset + (((group >> (bits - 1 - bit)) & 1) << (bit + 1))
    wanted = (place[0] ^ offset) * capacity + inside
    chosen = jnp.where(wanted == jnp.broadcast_to(slot, (slots, count)), 1.0, 0.0)
    live = jnp.sum(chosen, axis=1, keepdims=True)
    chosen = chosen.astype(BF)
    sk[...] = nn(chosen, tk[...]).astype(BF)
    sv[...] = nn(chosen, tv[...]).astype(BF)
    valid[...] = jnp.broadcast_to(live, valid.shape)


def gathered(wide, text, starts, cols):
    return jnp.concatenate(
        [wide[pl.ds(a, TILE), cols] for a in starts] + [text[:, cols]], axis=0
    )


def split(x, count):
    parts = []
    for _ in range(count):
        head = x.astype(BF).astype(F32)
        parts.append(head)
        x = x - head
    return parts


def first_kernel(n, place, *refs):
    parts, weights, out = refs[: 2 * n], refs[2 * n : 3 * n], refs[3 * n]
    for chunk in range(2):
        total = None
        for part, weight in zip(parts[chunk * n : (chunk + 1) * n], weights):
            term = nt(part[...], weight[...])
            total = term if total is None else total + term
        out[chunk * TILE : (chunk + 1) * TILE, :] = total


def middle_kernel(place, a_before, a_last, b_before, first, w_before, w_last, out, partial):
    total = first[:TILE, :] + nt(a_before[...], w_before[...])
    out[...] = (total + nt(a_last[...], w_last[...])).astype(BF)
    partial[...] = first[TILE:, :] + nt(b_before[...], w_before[...])


def last_kernel(place, b_last, partial, w_last, out):
    out[...] = (partial[...] + nt(b_last[...], w_last[...])).astype(BF)


def softmax_kernel(
    place, lists, q, k0, k1, k2, v0, v1, v2, tk, tv, m0, m1, aux, dscores, wide_k, wide_v
):
    stack_tiles((k0, k1, k2), wide_k)
    stack_tiles((v0, v1, v2), wide_v)
    row = lax.broadcasted_iota(jnp.int32, (AUX, TILE), 0)
    size = dscores.shape[0] // 2
    for tile, message in enumerate((m0, m1)):
        starts = [source_tile(place, lists, place[0] * 2 + tile, e) for e in range(3)]
        rows = slice(tile * TILE, (tile + 1) * TILE)
        for h in range(q.shape[1] // HD):
            cols = lanes(h)
            score = nt(gathered(wide_k, tk, starts, cols), q[rows, cols])
            top = jnp.max(score, axis=0, keepdims=True)
            weight = jnp.exp2((score - top) * SCALE2)
            total = jnp.sum(weight, axis=0, keepdims=True)
            prob = weight * (1.0 / total)
            dprob = nt(gathered(wide_v, tv, starts, cols), message[:, cols])
            delta = jnp.sum(prob * dprob, axis=0, keepdims=True)
            dscores[tile * size : (tile + 1) * size, cols] = (prob * (dprob - delta)).astype(BF)
            lse = top * SCALE2 + jnp.log2(total)
            block = jnp.zeros((AUX, TILE), F32)
            for i, line in enumerate(split(delta, 2) + split(lse, 3)):
                block = jnp.where(row == i, jnp.broadcast_to(line, (AUX, TILE)), block)
            aux[tile * AUX : (tile + 1) * AUX, cols] = block.astype(BF)


def query_kernel(place, lists, k0, k1, k2, tk, dscores, out, wide_k):
    stack_tiles((k0, k1, k2), wide_k)
    size = dscores.shape[0] // 2
    for tile in range(2):
        starts = [source_tile(place, lists, place[0] * 2 + tile, e) for e in range(3)]
        rows = slice(tile * TILE, (tile + 1) * TILE)
        for h in range(out.shape[1] // HD):
            cols = lanes(h)
            dscore = dscores[tile * size : (tile + 1) * size, cols]
            keys = gathered(wide_k, tk, starts, cols)
            out[rows, cols] = (SCALE * tn(dscore, keys)).astype(BF)


def read_lines(aux, chunk, cols):
    lines = aux[chunk * AUX : (chunk + 1) * AUX, cols].astype(F32)
    return lines[0:1] + lines[1:2], (lines[2:3] + lines[3:4]) + lines[4:5]


def off_by(place, lists, slab, tile, key_tile):
    count = lists.shape[0]
    query_tile = slab * 2 + tile
    row = jnp.clip(query_tile, 0, count - 1)
    wanted = place[0] * 2 + key_tile
    found = (lists[row, 0] == wanted) | (lists[row, 1] == wanted) | (lists[row, 2] == wanted)
    found = found & (query_tile >= 0) & (query_tile < count)
    return jnp.where(found, 0.0, OFF)


def key_terms(offs, keys, values, q, m0, m1, aux, cols):
    lines = [read_lines(aux, i, cols) for i in range(2)]
    delta = jnp.concatenate([d for d, _ in lines], axis=1)
    lse = [l for _, l in lines]
    g = jnp.concatenate([m0[:, cols], m1[:, cols]], axis=0)
    score = nt(keys, q) * SCALE2
    pieces = []
    for i in range(2):
        line = jnp.concatenate([lse[t] + offs[t][i] for t in range(2)], axis=1)
        pieces.append(score[i * TILE : (i + 1) * TILE] - line)
    if keys.shape[0] > 2 * TILE:
        pieces.append(score[2 * TILE :] - jnp.concatenate(lse, axis=1))
    prob = jnp.exp2(jnp.concatenate(pieces, axis=0))
    dscore = (prob * (nt(values, g) - delta)).astype(BF)
    return nn(dscore, q), nn(prob.astype(BF), g)


def all_offs(place, lists, slab):
    return [[off_by(place, lists, slab, t, i) for i in range(2)] for t in range(2)]


def own_kernel(
    place, lists, k, v, sk, sv, q, m0, m1, aux, key_acc, value_acc, text_k, text_v
):
    frame = k.shape[0]
    offs = all_offs(place, lists, place[0])
    for h in range(k.shape[1] // HD):
        cols = lanes(h)
        keys = jnp.concatenate([k[:, cols], sk[:, cols]], axis=0)
        values = jnp.concatenate([v[:, cols], sv[:, cols]], axis=0)
        dk, dv = key_terms(offs, keys, values, q[:, cols], m0, m1, aux, cols)
        key_acc[:, cols] = dk[:frame]
        value_acc[:, cols] = dv[:frame]
        text_k[:, cols] = dk[frame:]
        text_v[:, cols] = dv[frame:]


def mate_kernel(
    place, lists, k, v, sk, sv, valid, q, m0, m1, aux, key_in, value_in, text_k, text_v,
    key_acc, value_acc, keep, send,
):
    frame, width = k.shape
    half = keep.shape[0]
    live = valid[...] > 0
    offs = all_offs(place, lists, place[1])
    for h in range(width // HD):
        cols = lanes(h)
        more = slice(width + h * HD, width + (h + 1) * HD)
        keys = jnp.concatenate([k[:, cols], sk[:, cols]], axis=0)
        values = jnp.concatenate([v[:, cols], sv[:, cols]], axis=0)
        dk, dv = key_terms(offs, keys, values, q[:, cols], m0, m1, aux, cols)
        key_acc[:, cols] = key_in[:, cols] + dk[:frame]
        value_acc[:, cols] = value_in[:, cols] + dv[:frame]
        part_k = jnp.where(live, (text_k[:, cols] + dk[frame:]) * SCALE, 0.0)
        part_v = jnp.where(live, text_v[:, cols] + dv[frame:], 0.0)
        keep[:, cols] = part_k[:half]
        keep[:, more] = part_v[:half]
        send[:, cols] = part_k[half:].astype(BF)
        send[:, more] = part_v[half:].astype(BF)


def far_kernel(place, lists, k, v, q, m0, m1, aux, key_acc, value_acc, key_out, value_out):
    offs = all_offs(place, lists, place[3])
    for h in range(k.shape[1] // HD):
        cols = lanes(h)
        dk, dv = key_terms(offs, k[:, cols], v[:, cols], q[:, cols], m0, m1, aux, cols)
        key_out[:, cols] = ((key_acc[:, cols] + dk) * SCALE).astype(BF)
        value_out[:, cols] = (value_acc[:, cols] + dv).astype(BF)


VMEM = pl.BlockSpec(memory_space=pltpu.VMEM)
SMEM = pl.BlockSpec(memory_space=pltpu.SMEM)


def call(kernel, name, outs, scalars, arrays, scratch=()):
    return pl.pallas_call(
        kernel,
        name=name,
        out_shape=outs,
        in_specs=[SMEM] * scalars + [VMEM] * (len(arrays) - scalars),
        out_specs=jax.tree.map(lambda _: VMEM, outs),
        scratch_shapes=list(scratch),
        compiler_params=pltpu.CompilerParams(vmem_limit_bytes=LIMIT),
    )(*arrays)


def call_blocks(kernel, name, outs, place, arrays, weight, steps):
    rows, depth = weight.shape[0], arrays[0].shape[1]
    ranks = weight.shape[1] // depth

    def block(step):
        return pl.BlockSpec(
            (rows, depth), lambda i, place: (0, lax.rem(place[2] - step + ranks, ranks))
        )

    return pl.pallas_call(
        kernel,
        name=name,
        out_shape=outs,
        grid_spec=pltpu.PrefetchScalarGridSpec(
            num_scalar_prefetch=1,
            grid=(1,),
            in_specs=[VMEM] * len(arrays) + [block(step) for step in steps],
            out_specs=jax.tree.map(lambda _: VMEM, outs),
        ),
        compiler_params=pltpu.CompilerParams(vmem_limit_bytes=LIMIT),
    )(place, *arrays, *([weight] * len(steps)))


def together(*arrays):
    return lax.optimization_barrier(arrays)


def local(
    queries, keys, values, grad_output, out_weight, text_keys, text_values, mask_lists, text_owner
):
    frame, width = queries.shape
    text_count = text_keys.shape[0]
    both = ("seq", "rep")
    seqs, reps, ranks = lax.axis_size("seq"), lax.axis_size("rep"), lax.axis_size("head")
    groups = seqs * reps
    slab = lax.axis_index(both)
    mate = slab ^ 1
    other = jnp.where(slab & 1, slab + 1, slab - 1)
    place = jnp.stack([slab, mate, lax.axis_index("head"), other]).astype(jnp.int32)

    def swap(x, distance=1):
        return lax.ppermute(x, both, [(i, i ^ distance) for i in range(groups)])

    def relay(x):
        def target(i):
            if i % 2 == 0:
                return i + 2 if i + 2 < groups else i + 1
            return i - 2 if i >= 2 else i - 1

        return lax.ppermute(x, both, [(i, target(i)) for i in range(groups)])

    def ring(x):
        return lax.ppermute(x, "head", [(i, (i + 1) % ranks) for i in range(ranks)])

    capacity = 2 * text_count // groups
    slots = groups // 2 * capacity
    sds = jax.ShapeDtypeStruct
    sk, sv, valid = call(
        functools.partial(slot_kernel, capacity),
        "slots",
        (sds((slots, width), BF),) * 2 + (sds((slots, HD), F32),),
        1,
        (place, text_owner.reshape(1, text_count), text_keys, text_values),
    )
    part_a, part_b = [grad_output[:TILE]], [grad_output[TILE:]]
    part_a.append(ring(part_a[0]))
    part_b.append(ring(part_b[0]))
    mate_v = swap(values)
    late_k, part_a[1] = together(keys, part_a[1])
    mate_k = swap(late_k)
    for _ in range(ranks - 2):
        part_a.append(ring(part_a[-1]))
        part_b.append(ring(part_b[-1]))
    late_q, part_b[1] = together(queries, part_b[1])
    mate_q = swap(late_q)
    first = call_blocks(
        functools.partial(first_kernel, ranks - 2),
        "first_blocks",
        sds((frame, width), F32),
        place,
        (*part_a[:-2], *part_b[:-2]),
        out_weight,
        range(ranks - 2),
    )
    late_v, part_a[-2] = together(mate_v, part_a[-2])
    far_v = relay(late_v)
    late_k, part_a[-1] = together(mate_k, part_a[-1])
    far_k = relay(late_k)
    late_q, part_b[-1] = together(mate_q, part_b[-1])
    far_q = relay(late_q)

    grad_a, partial = call_blocks(
        middle_kernel,
        "grad_heads_a",
        (sds((TILE, width), BF), sds((TILE, width), F32)),
        place,
        (part_a[-2], part_a[-1], part_b[-2], first),
        out_weight,
        (ranks - 2, ranks - 1),
    )
    mate_a = swap(grad_a)
    grad_b = call_blocks(
        last_kernel,
        "grad_heads_b",
        sds((TILE, width), BF),
        place,
        (part_b[-1], partial),
        out_weight,
        (ranks - 1,),
    )
    mate_b = swap(grad_b)
    wide = pltpu.VMEM((3 * frame, width), BF)
    aux, dscores = call(
        softmax_kernel,
        "softmax",
        (sds((2 * AUX, width), BF), sds((2 * (3 * TILE + text_count), width), BF)),
        2,
        (
            place, mask_lists, queries, keys, mate_k, far_k, values, mate_v, far_v,
            text_keys, text_values, grad_a, grad_b,
        ),
        (wide, wide),
    )
    mate_aux = swap(aux)
    far_a, far_b, far_aux = relay(mate_a), relay(mate_b), relay(mate_aux)
    acc = sds((frame, width), F32)
    text_acc = sds((slots, width), F32)
    accs = call(
        own_kernel,
        "own_keys",
        (acc, acc, text_acc, text_acc),
        2,
        (place, mask_lists, keys, values, sk, sv, queries, grad_a, grad_b, aux),
    )
    late_aux, far_a = together(mate_aux, far_a)
    key_acc, value_acc, keep, send = call(
        mate_kernel,
        "mate_keys",
        (acc, acc, sds((slots // 2, 2 * width), F32), sds((slots // 2, 2 * width), BF)),
        2,
        (place, mask_lists, keys, values, sk, sv, valid, mate_q, mate_a, mate_b, late_aux, *accs),
    )
    query_grads = call(
        query_kernel,
        "query_grads",
        sds((frame, width), BF),
        2,
        (place, mask_lists, keys, mate_k, far_k, text_keys, dscores),
        (wide,),
    )
    key_grads, value_grads = call(
        far_kernel,
        "far_keys",
        (sds((frame, width), BF),) * 2,
        2,
        (place, mask_lists, keys, values, far_q, far_a, far_b, far_aux, key_acc, value_acc),
    )
    stages = []
    distance = 2
    while distance < groups:
        stages.append(distance)
        distance *= 2
    for i, d in enumerate(stages):
        total = keep + swap(send, d).astype(F32)
        if i + 1 < len(stages):
            rows = total.shape[0] // 2
            keep, send = total[:rows], total[rows:].astype(BF)
    total = total.astype(BF)
    return query_grads, key_grads, value_grads, total[:, :width], total[:, width:]


def solution(mesh):
    rows = P(("seq", "rep"), "head")
    return jax.shard_map(
        local,
        mesh=mesh,
        in_specs=(rows, rows, rows, rows, P("head", None), P(None, "head"), P(None, "head"), P(), P()),
        out_specs=(rows,) * 5,
        check_vma=False,
    )
```

time: 91.1 us -> 78.6 us (0.86)
  the two profiles are of different devices: /device:TPU:0 before, /device:TPU:27 now
where the time goes in v2:
time: 78.6 us; the launch traced here: 78.3 us
  starting transfers between devices  27.6 us (35%)
  waiting for transfers between devices  23.9 us (30%)
  Pallas kernels  20.9 us (27%)
  local copies, waits for them, and re-layouts  4.89 us (6%)
  between operations  0.83 us (1%)
    pallas_call x6, Pallas kernels, call(): pl.pallas_call(kernel, name=name, out_shape=outs, in_specs=[SMEM] * scala...  15.7 us
    ppermute x6, starting transfers between devices, ring(): return lax.ppermute(x, 'head', [(i, (i + 1) % ranks) for i in range(ranks)])  11.6 us
    ppermute x6, waiting for transfers between devices, ring(): return lax.ppermute(x, 'head', [(i, (i + 1) % ranks) for i in range(ranks)])  9.39 us
    ppermute x6, waiting for transfers between devices, relay(): return lax.ppermute(x, both, [(i, target(i)) for i in range(groups)])  9.33 us
    ppermute x8, starting transfers between devices, swap(): return lax.ppermute(x, both, [(i, i ^ distance) for i in range(groups)])  8.19 us
    ppermute x6, starting transfers between devices, relay(): return lax.ppermute(x, both, [(i, target(i)) for i in range(groups)])  7.84 us
    ppermute x8, waiting for transfers between devices, swap(): return lax.ppermute(x, both, [(i, i ^ distance) for i in range(groups)])  5.17 us
    pallas_call x3, Pallas kernels, call_blocks(): pl.pallas_call(kernel, name=name, out_shape=outs, grid_spec=pltpu.Prefetc...  5.13 us
  transfers between devices with their start and end apart: 20, of which 9 were waited for; matrix products, arithmetic and copies ran while one was open for 1% of the time, Pallas kernels for 23%

profile of v2, /device:TPU:27, one launch (start us, length us, event | category | flops | bytes accessed | tf_op | source)
XLA Modules:
  0.0 78.3 jit_solution(3197615770819313044)
XLA Ops:
  2.1 5.5 %collective-permute-done.refs_1_ = bf16[128,768]{1,0:T(8,128)(2,1)S(1)} collective-permute-done((bf16[128,768]{1,0:T(8,128)(2,1)S(1)}, bf16[128,768]{1,0:T(8,128)(2,1)S(1)}, u32[]{:S(2)}, u32[]{:S(2)}) %collective-permute-start) | collective-permute-done | bytes 196640 | tf_op jit(solution)/shard_map/ppermute | solution.py:306
  7.6 1.8 %collective-permute-start.2 = (bf16[128,768]{1,0:T(8,128)(2,1)S(1)}, bf16[128,768]{1,0:T(8,128)(2,1)S(1)}, u32[]{:S(2)}, u32[]{:S(2)}) collective-permute-start(bf16[128,768]{1,0:T(8,128)(2,1)S(1)} %collective-permute-done.refs_1_), channel_id=1, source_target_pairs={{0,2},{2,4},{4,6},{6,0},{1,3},{3,5},{5,7},{7,1},{8,10},{10,12},{12... | collective-permute-start | bytes 589832 | tf_op jit(solution)/shard_map/ppermute | solution.py:306
  9.9 2.8 %collective-permute-done.2.a_before = bf16[128,768]{1,0:T(8,128)(2,1)S(1)} collective-permute-done((bf16[128,768]{1,0:T(8,128)(2,1)S(1)}, bf16[128,768]{1,0:T(8,128)(2,1)S(1)}, u32[]{:S(2)}, u32[]{:S(2)}) %collective-permute-start.2) | collective-permute-done | bytes 196640 | tf_op jit(solution)/shard_map/ppermute | solution.py:306
  12.7 3.4 %collective-permute-start.3 = (bf16[128,768]{1,0:T(8,128)(2,1)S(1)}, bf16[128,768]{1,0:T(8,128)(2,1)S(1)}, u32[]{:S(2)}, u32[]{:S(2)}) collective-permute-start(bf16[128,768]{1,0:T(8,128)(2,1)S(1)} %collective-permute-done.2.a_before), channel_id=1, source_target_pairs={{0,2},{2,4},{4,6},{6,0},{1,3},{3,5},{5,7},{7,1},{8,10},{10,12},{12... | collective-permute-start | bytes 589832 | tf_op jit(solution)/shard_map/ppermute | solution.py:306
  16.8 3.5 %collective-permute-start.8 = (bf16[128,768]{1,0:T(8,128)(2,1)S(1)}, bf16[128,768]{1,0:T(8,128)(2,1)S(1)}, u32[]{:S(2)}, u32[]{:S(2)}) collective-permute-start(bf16[128,768]{1,0:T(8,128)(2,1)S(1)} %collective-permute-done.7.refs_3_), channel_id=1, source_target_pairs={{0,2},{2,4},{4,6},{6,0},{1,3},{3,5},{5,7},{7,1},{8,10},{10,12},{12... | collective-permute-start | bytes 589832 | tf_op jit(solution)/shard_map/ppermute | solution.py:306
  21.1 4.1 %collective-permute-start.6 = (bf16[256,768]{1,0:T(8,128)(2,1)}, bf16[256,768]{1,0:T(8,128)(2,1)}, u32[]{:S(2)}, u32[]{:S(2)}) collective-permute-start(bf16[256,768]{1,0:T(8,128)(2,1)} %collective-permute-done.5.v1), channel_id=1, source_target_pairs={{0,8},{1,0},{8,16},{9,1},{16,24},{17,9},{24,25},{25,17},{2,10},{3,... | collective-permute-start | bytes 1179656 | tf_op jit(solution)/shard_map/ppermute | solution.py:303
  25.2 1.5 %collective-permute-start.4 = (bf16[256,768]{1,0:T(8,128)(2,1)S(1)}, bf16[256,768]{1,0:T(8,128)(2,1)S(1)}, u32[]{:S(2)}, u32[]{:S(2)}) collective-permute-start(bf16[256,768]{1,0:T(8,128)(2,1)S(1)} %collective-permute-done.1.k1), channel_id=1, source_target_pairs={{0,8},{1,0},{8,16},{9,1},{16,24},{17,9},{24,25},{25,17},{2,10},{3,... | collective-permute-start | bytes 1179656 | tf_op jit(solution)/shard_map/ppermute | solution.py:303
  26.7 2.3 %copy-done = bf16[768,3072]{1,0:T(8,128)(2,1)S(1)} copy-done((bf16[768,3072]{1,0:T(8,128)(2,1)S(1)}, bf16[768,3072]{1,0:T(8,128)(2,1)}, u32[]{:S(2)}) %copy-start) | copy-done | bytes 4718616
  29.1 2.2 %first_blocks.1.first = f32[256,768]{1,0:T(8,128)S(1)} custom-call(s32[4]{0:T(128)S(1)} %pad_add_fusion.place, bf16[128,768]{1,0:T(8,128)(2,1)S(1)} %get-tuple-element.64.refs_0_, bf16[128,768]{1,0:T(8,128)(2,1)S(1)} %collective-permute-done.refs_1_, bf16[128,768]{1,0:T(8,128)(2,1)S(1)} %get-tuple-element.63.refs_2_, ...), custom_call_target="tpu_custom_call" | custom-call | tf_op jit(solution)/shard_map/first_blocks/pallas_call | solution.py:263
  31.3 2.8 %collective-permute-start.10 = (bf16[128,768]{1,0:T(8,128)(2,1)S(1)}, bf16[128,768]{1,0:T(8,128)(2,1)S(1)}, u32[]{:S(2)}, u32[]{:S(2)}) collective-permute-start(bf16[128,768]{1,0:T(8,128)(2,1)S(1)} %collective-permute-done.8.b_before), channel_id=1, source_target_pairs={{0,2},{2,4},{4,6},{6,0},{1,3},{3,5},{5,7},{7,1},{8,10},{10,12},{12... | collective-permute-start | bytes 589832 | tf_op jit(solution)/shard_map/ppermute | solution.py:306
  34.1 1.8 %grad_heads_a.1 = (bf16[128,768]{1,0:T(8,128)(2,1)S(1)}, f32[128,768]{1,0:T(8,128)S(1)}) custom-call(s32[4]{0:T(128)S(1)} %pad_add_fusion.place, bf16[128,768]{1,0:T(8,128)(2,1)S(1)} %collective-permute-done.2.a_before, bf16[128,768]{1,0:T(8,128)(2,1)S(1)} %collective-permute-done.3.a_last, bf16[128,768]{1,0:T(8,128)(2,1)S(1)} %collective-permute-done.8.b_before, ...), custom_call_target="tpu_custom_call" | custom-call | tf_op jit(solution)/shard_map/grad_heads_a/pallas_call | solution.py:263
  36.0 1.4 %collective-permute-start.13 = (bf16[128,768]{1,0:T(8,128)(2,1)S(1)}, bf16[128,768]{1,0:T(8,128)(2,1)}, u32[]{:S(2)}, u32[]{:S(2)}) collective-permute-start(bf16[128,768]{1,0:T(8,128)(2,1)S(1)} %get-tuple-element.41.m0), channel_id=1, source_target_pairs={{0,1},{1,0},{8,9},{9,8},{16,17},{17,16},{24,25},{25,24},{2,3},{3,2... | collective-permute-start | bytes 589832 | tf_op jit(solution)/shard_map/ppermute | solution.py:295
  37.8 4.4 %collective-permute-done.13.m0 = bf16[128,768]{1,0:T(8,128)(2,1)} collective-permute-done((bf16[128,768]{1,0:T(8,128)(2,1)S(1)}, bf16[128,768]{1,0:T(8,128)(2,1)}, u32[]{:S(2)}, u32[]{:S(2)}) %collective-permute-start.13) | collective-permute-done | bytes 196640 | tf_op jit(solution)/shard_map/ppermute | solution.py:295
  42.3 1.3 %collective-permute-start.14 = (bf16[128,768]{1,0:T(8,128)(2,1)}, bf16[128,768]{1,0:T(8,128)(2,1)}, u32[]{:S(2)}, u32[]{:S(2)}) collective-permute-start(bf16[128,768]{1,0:T(8,128)(2,1)} %collective-permute-done.13.m0), channel_id=1, source_target_pairs={{0,8},{1,0},{8,16},{9,1},{16,24},{17,9},{24,25},{25,17},{2,10},{3,... | collective-permute-start | bytes 589832 | tf_op jit(solution)/shard_map/ppermute | solution.py:303
  44.6 1.2 %collective-permute-start.15 = (bf16[128,768]{1,0:T(8,128)(2,1)S(1)}, bf16[128,768]{1,0:T(8,128)(2,1)}, u32[]{:S(2)}, u32[]{:S(2)}) collective-permute-start(bf16[128,768]{1,0:T(8,128)(2,1)S(1)} %grad_heads_b.1.m1), channel_id=1, source_target_pairs={{0,1},{1,0},{8,9},{9,8},{16,17},{17,16},{24,25},{25,24},{2,3},{3,2... | collective-permute-start | bytes 589832 | tf_op jit(solution)/shard_map/ppermute | solution.py:295
  46.6 3.8 %softmax.1 = (bf16[32,768]{1,0:T(8,128)(2,1)S(1)}, bf16[1280,768]{1,0:T(8,128)(2,1)S(1)}) custom-call(s32[4]{0:T(128)S(1)} %pad_add_fusion.place, s32[16,3]{1,0:T(8,128)S(1)} %copy.15.lists, bf16[256,768]{1,0:T(8,128)(2,1)S(1)} %copy-done.6, bf16[256,768]{1,0:T(8,128)(2,1)S(1)} %copy-done.2, bf16[256,768]{1,0:T(8,128)(2,1)S(1)} %collective-permute-done.1.k1, ...), custom_call_target="tpu_custom_call" | custom-call | tf_op jit(solution)/shard_map/softmax/pallas_call | solution.py:243
  51.8 2.5 %own_keys.1 = (f32[256,768]{1,0:T(8,128)S(1)}, f32[256,768]{1,0:T(8,128)S(1)}, f32[256,768]{1,0:T(8,128)S(1)}, f32[256,768]{1,0:T(8,128)S(1)}) custom-call(s32[4]{0:T(128)S(1)} %pad_add_fusion.place, s32[16,3]{1,0:T(8,128)S(1)} %copy.15.lists, bf16[256,768]{1,0:T(8,128)(2,1)S(1)} %copy-done.2, bf16[256,768]{1,0:T(8,128)(2,1)S(1)} %copy-done.3, ...), custom_call_target="tpu_custom_call" | custom-call | tf_op jit(solution)/shard_map/own_keys/pallas_call | solution.py:243
  54.3 2.9 %mate_keys.1 = (f32[256,768]{1,0:T(8,128)S(1)}, f32[256,768]{1,0:T(8,128)S(1)}, f32[128,1536]{1,0:T(8,128)S(1)}, bf16[128,1536]{1,0:T(8,128)(2,1)S(1)}) custom-call(s32[4]{0:T(128)S(1)} %pad_add_fusion.place, s32[16,3]{1,0:T(8,128)S(1)} %copy.15.lists, bf16[256,768]{1,0:T(8,128)(2,1)S(1)} %copy-done.2, bf16[256,768]{1,0:T(8,128)(2,1)S(1)} %copy-done.3, ...), custom_call_target="tpu_custom_call" | custom-call | tf_op jit(solution)/shard_map/mate_keys/pallas_call | solution.py:243
  57.2 3.0 %collective-permute-start.18 = (bf16[128,1536]{1,0:T(8,128)(2,1)S(1)}, bf16[128,1536]{1,0:T(8,128)(2,1)S(1)}, u32[]{:S(2)}, u32[]{:S(2)}) collective-permute-start(bf16[128,1536]{1,0:T(8,128)(2,1)S(1)} %get-tuple-element.62), channel_id=1, source_target_pairs={{0,8},{1,9},{8,0},{9,1},{16,24},{17,25},{24,16},{25,17},{2,10},{3,... | collective-permute-start | bytes 1179656 | tf_op jit(solution)/shard_map/ppermute | solution.py:295
  62.6 2.3 %query_grads.1 = bf16[256,768]{1,0:T(8,128)(2,1)} custom-call(s32[4]{0:T(128)S(1)} %pad_add_fusion.place, s32[16,3]{1,0:T(8,128)S(1)} %copy.15.lists, bf16[256,768]{1,0:T(8,128)(2,1)S(1)} %copy-done.2, bf16[256,768]{1,0:T(8,128)(2,1)S(1)} %collective-permute-done.1.k1, bf16[256,768]{1,0:T(8,128)(2,1)S(1)} %collective-permute-done.4.k2, ...), custom_call_target="tpu_custom_call" | custom-call | tf_op jit(solution)/shard_map/query_grads/pallas_call | solution.py:243
  64.9 4.6 %collective-permute-done.11.q = bf16[256,768]{1,0:T(8,128)(2,1)S(1)} collective-permute-done((bf16[256,768]{1,0:T(8,128)(2,1)S(1)}, bf16[256,768]{1,0:T(8,128)(2,1)S(1)}, u32[]{:S(2)}, u32[]{:S(2)}) %collective-permute-start.11) | collective-permute-done | bytes 393248 | tf_op jit(solution)/shard_map/ppermute | solution.py:303
  69.5 2.1 %collective-permute-done.16.m1 = bf16[128,768]{1,0:T(8,128)(2,1)S(1)} collective-permute-done((bf16[128,768]{1,0:T(8,128)(2,1)}, bf16[128,768]{1,0:T(8,128)(2,1)S(1)}, u32[]{:S(2)}, u32[]{:S(2)}) %collective-permute-start.16) | collective-permute-done | bytes 196640 | tf_op jit(solution)/shard_map/ppermute | solution.py:303
  71.6 2.6 %collective-permute-done.17.aux = bf16[32,768]{1,0:T(8,128)(2,1)S(1)} collective-permute-done((bf16[32,768]{1,0:T(8,128)(2,1)S(1)}, bf16[32,768]{1,0:T(8,128)(2,1)S(1)}, u32[]{:S(2)}, u32[]{:S(2)}) %collective-permute-start.17) | collective-permute-done | bytes 49184 | tf_op jit(solution)/shard_map/ppermute | solution.py:303
  74.3 3.3 %far_keys.1 = (bf16[256,768]{1,0:T(8,128)(2,1)}, bf16[256,768]{1,0:T(8,128)(2,1)}) custom-call(s32[4]{0:T(128)S(1)} %pad_add_fusion.place, s32[16,3]{1,0:T(8,128)S(1)} %copy.15.lists, bf16[256,768]{1,0:T(8,128)(2,1)S(1)} %copy-done.2, bf16[256,768]{1,0:T(8,128)(2,1)S(1)} %copy-done.3, bf16[256,768]{1,0:T(8,128)(2,1)S(1)} %collective-permute-done.11.q, ...), custom_call_target="tpu_custom_call" | custom-call | tf_op jit(solution)/shard_map/far_keys/pallas_call | solution.py:243
  (48 shorter events, 10.3 us)
Async XLA Ops:
  1.7 5.9 %collective-permute-start = (bf16[128,768]{1,0:T(8,128)(2,1)S(1)}, bf16[128,768]{1,0:T(8,128)(2,1)S(1)}, u32[]{:S(2)}, u32[]{:S(2)}) collective-permute-start(bf16[128,768]{1,0:T(8,128)(2,1)S(1)} %get-tuple-element.64.refs_0_), channel_id=1, source_target_pairs={{0,2},{2,4},{4,6},{6,0},{1,3},{3,5},{5,7},{7,1},{8,10},{10,12},{12... | collective-permute-start | bytes 589832 | tf_op jit(solution)/shard_map/ppermute | solution.py:306
  1.7 19.3 %collective-permute-start.5 = (bf16[256,768]{1,0:T(8,128)(2,1)}, bf16[256,768]{1,0:T(8,128)(2,1)}, u32[]{:S(2)}, u32[]{:S(2)}) collective-permute-start(bf16[256,768]{1,0:T(8,128)(2,1)} %v.5), channel_id=1, source_target_pairs={{0,1},{1,0},{8,9},{9,8},{16,17},{17,16},{24,25},{25,24},{2,3},{3,2... | collective-permute-start | bytes 1179656 | tf_op jit(solution)/shard_map/ppermute | solution.py:295
  7.6 5.1 %collective-permute-start.2 = (bf16[128,768]{1,0:T(8,128)(2,1)S(1)}, bf16[128,768]{1,0:T(8,128)(2,1)S(1)}, u32[]{:S(2)}, u32[]{:S(2)}) collective-permute-start(bf16[128,768]{1,0:T(8,128)(2,1)S(1)} %collective-permute-done.refs_1_), channel_id=1, source_target_pairs={{0,2},{2,4},{4,6},{6,0},{1,3},{3,5},{5,7},{7,1},{8,10},{10,12},{12... | collective-permute-start | bytes 589832 | tf_op jit(solution)/shard_map/ppermute | solution.py:306
  9.4 15.8 %collective-permute-start.1 = (bf16[256,768]{1,0:T(8,128)(2,1)}, bf16[256,768]{1,0:T(8,128)(2,1)S(1)}, u32[]{:S(2)}, u32[]{:S(2)}) collective-permute-start(bf16[256,768]{1,0:T(8,128)(2,1)} %k.5), channel_id=1, source_target_pairs={{0,1},{1,0},{8,9},{9,8},{16,17},{17,16},{24,25},{25,24},{2,3},{3,2... | collective-permute-start | bytes 1179656 | tf_op jit(solution)/shard_map/ppermute | solution.py:295
  9.9 6.9 %collective-permute-start.7 = (bf16[128,768]{1,0:T(8,128)(2,1)S(1)}, bf16[128,768]{1,0:T(8,128)(2,1)S(1)}, u32[]{:S(2)}, u32[]{:S(2)}) collective-permute-start(bf16[128,768]{1,0:T(8,128)(2,1)S(1)} %get-tuple-element.63.refs_2_), channel_id=1, source_target_pairs={{0,2},{2,4},{4,6},{6,0},{1,3},{3,5},{5,7},{7,1},{8,10},{10,12},{12... | collective-permute-start | bytes 589832 | tf_op jit(solution)/shard_map/ppermute | solution.py:306
  12.7 12.5 %collective-permute-start.3 = (bf16[128,768]{1,0:T(8,128)(2,1)S(1)}, bf16[128,768]{1,0:T(8,128)(2,1)S(1)}, u32[]{:S(2)}, u32[]{:S(2)}) collective-permute-start(bf16[128,768]{1,0:T(8,128)(2,1)S(1)} %collective-permute-done.2.a_before), channel_id=1, source_target_pairs={{0,2},{2,4},{4,6},{6,0},{1,3},{3,5},{5,7},{7,1},{8,10},{10,12},{12... | collective-permute-start | bytes 589832 | tf_op jit(solution)/shard_map/ppermute | solution.py:306
  16.8 14.5 %collective-permute-start.8 = (bf16[128,768]{1,0:T(8,128)(2,1)S(1)}, bf16[128,768]{1,0:T(8,128)(2,1)S(1)}, u32[]{:S(2)}, u32[]{:S(2)}) collective-permute-start(bf16[128,768]{1,0:T(8,128)(2,1)S(1)} %collective-permute-done.7.refs_3_), channel_id=1, source_target_pairs={{0,2},{2,4},{4,6},{6,0},{1,3},{3,5},{5,7},{7,1},{8,10},{10,12},{12... | collective-permute-start | bytes 589832 | tf_op jit(solution)/shard_map/ppermute | solution.py:306
  20.3 17.5 %collective-permute-start.9 = (bf16[256,768]{1,0:T(8,128)(2,1)}, bf16[256,768]{1,0:T(8,128)(2,1)S(1)}, u32[]{:S(2)}, u32[]{:S(2)}) collective-permute-start(bf16[256,768]{1,0:T(8,128)(2,1)} %q.3), channel_id=1, source_target_pairs={{0,1},{1,0},{8,9},{9,8},{16,17},{17,16},{24,25},{25,24},{2,3},{3,2... | collective-permute-start | bytes 1179656 | tf_op jit(solution)/shard_map/ppermute | solution.py:295
  21.1 25.5 %collective-permute-start.6 = (bf16[256,768]{1,0:T(8,128)(2,1)}, bf16[256,768]{1,0:T(8,128)(2,1)}, u32[]{:S(2)}, u32[]{:S(2)}) collective-permute-start(bf16[256,768]{1,0:T(8,128)(2,1)} %collective-permute-done.5.v1), channel_id=1, source_target_pairs={{0,8},{1,0},{8,16},{9,1},{16,24},{17,9},{24,25},{25,17},{2,10},{3,... | collective-permute-start | bytes 1179656 | tf_op jit(solution)/shard_map/ppermute | solution.py:303
  25.2 21.4 %collective-permute-start.4 = (bf16[256,768]{1,0:T(8,128)(2,1)S(1)}, bf16[256,768]{1,0:T(8,128)(2,1)S(1)}, u32[]{:S(2)}, u32[]{:S(2)}) collective-permute-start(bf16[256,768]{1,0:T(8,128)(2,1)S(1)} %collective-permute-done.1.k1), channel_id=1, source_target_pairs={{0,8},{1,0},{8,16},{9,1},{16,24},{17,9},{24,25},{25,17},{2,10},{3,... | collective-permute-start | bytes 1179656 | tf_op jit(solution)/shard_map/ppermute | solution.py:303
  31.3 6.5 %collective-permute-start.10 = (bf16[128,768]{1,0:T(8,128)(2,1)S(1)}, bf16[128,768]{1,0:T(8,128)(2,1)S(1)}, u32[]{:S(2)}, u32[]{:S(2)}) collective-permute-start(bf16[128,768]{1,0:T(8,128)(2,1)S(1)} %collective-permute-done.8.b_before), channel_id=1, source_target_pairs={{0,2},{2,4},{4,6},{6,0},{1,3},{3,5},{5,7},{7,1},{8,10},{10,12},{12... | collective-permute-start | bytes 589832 | tf_op jit(solution)/shard_map/ppermute | solution.py:306
  36.0 10.6 %copy-start.2 = (bf16[256,768]{1,0:T(8,128)(2,1)S(1)}, bf16[256,768]{1,0:T(8,128)(2,1)}, u32[]{:S(2)}) copy-start(bf16[256,768]{1,0:T(8,128)(2,1)} %k.5) | copy-start | bytes 1179652
  36.0 10.6 %copy-start.3 = (bf16[256,768]{1,0:T(8,128)(2,1)S(1)}, bf16[256,768]{1,0:T(8,128)(2,1)}, u32[]{:S(2)}) copy-start(bf16[256,768]{1,0:T(8,128)(2,1)} %v.5) | copy-start | bytes 1179652
  36.0 10.6 %copy-start.4 = (bf16[256,768]{1,0:T(8,128)(2,1)S(1)}, bf16[256,768]{1,0:T(8,128)(2,1)}, u32[]{:S(2)}) copy-start(bf16[256,768]{1,0:T(8,128)(2,1)} %tk.5) | copy-start | bytes 1179652
  36.0 10.6 %copy-start.5 = (bf16[256,768]{1,0:T(8,128)(2,1)S(1)}, bf16[256,768]{1,0:T(8,128)(2,1)}, u32[]{:S(2)}) copy-start(bf16[256,768]{1,0:T(8,128)(2,1)} %tv.3) | copy-start | bytes 1179652
  36.0 6.2 %collective-permute-start.13 = (bf16[128,768]{1,0:T(8,128)(2,1)S(1)}, bf16[128,768]{1,0:T(8,128)(2,1)}, u32[]{:S(2)}, u32[]{:S(2)}) collective-permute-start(bf16[128,768]{1,0:T(8,128)(2,1)S(1)} %get-tuple-element.41.m0), channel_id=1, source_target_pairs={{0,1},{1,0},{8,9},{9,8},{16,17},{17,16},{24,25},{25,24},{2,3},{3,2... | collective-permute-start | bytes 589832 | tf_op jit(solution)/shard_map/ppermute | solution.py:295
  42.3 12.0 %collective-permute-start.14 = (bf16[128,768]{1,0:T(8,128)(2,1)}, bf16[128,768]{1,0:T(8,128)(2,1)}, u32[]{:S(2)}, u32[]{:S(2)}) collective-permute-start(bf16[128,768]{1,0:T(8,128)(2,1)} %collective-permute-done.13.m0), channel_id=1, source_target_pairs={{0,8},{1,0},{8,16},{9,1},{16,24},{17,9},{24,25},{25,17},{2,10},{3,... | collective-permute-start | bytes 589832 | tf_op jit(solution)/shard_map/ppermute | solution.py:303
  44.6 9.7 %collective-permute-start.15 = (bf16[128,768]{1,0:T(8,128)(2,1)S(1)}, bf16[128,768]{1,0:T(8,128)(2,1)}, u32[]{:S(2)}, u32[]{:S(2)}) collective-permute-start(bf16[128,768]{1,0:T(8,128)(2,1)S(1)} %grad_heads_b.1.m1), channel_id=1, source_target_pairs={{0,1},{1,0},{8,9},{9,8},{16,17},{17,16},{24,25},{25,24},{2,3},{3,2... | collective-permute-start | bytes 589832 | tf_op jit(solution)/shard_map/ppermute | solution.py:295
  50.4 3.9 %collective-permute-start.12 = (bf16[32,768]{1,0:T(8,128)(2,1)S(1)}, bf16[32,768]{1,0:T(8,128)(2,1)S(1)}, u32[]{:S(2)}, u32[]{:S(2)}) collective-permute-start(bf16[32,768]{1,0:T(8,128)(2,1)S(1)} %get-tuple-element.47.aux), channel_id=1, source_target_pairs={{0,1},{1,0},{8,9},{9,8},{16,17},{17,16},{24,25},{25,24},{2,3},{3,2... | collective-permute-start | bytes 147464 | tf_op jit(solution)/shard_map/ppermute | solution.py:295
  57.2 4.4 %collective-permute-start.18 = (bf16[128,1536]{1,0:T(8,128)(2,1)S(1)}, bf16[128,1536]{1,0:T(8,128)(2,1)S(1)}, u32[]{:S(2)}, u32[]{:S(2)}) collective-permute-start(bf16[128,1536]{1,0:T(8,128)(2,1)S(1)} %get-tuple-element.62), channel_id=1, source_target_pairs={{0,8},{1,9},{8,0},{9,1},{16,24},{17,25},{24,16},{25,17},{2,10},{3,... | collective-permute-start | bytes 1179656 | tf_op jit(solution)/shard_map/ppermute | solution.py:295
  60.2 9.3 %collective-permute-start.11 = (bf16[256,768]{1,0:T(8,128)(2,1)S(1)}, bf16[256,768]{1,0:T(8,128)(2,1)S(1)}, u32[]{:S(2)}, u32[]{:S(2)}) collective-permute-start(bf16[256,768]{1,0:T(8,128)(2,1)S(1)} %collective-permute-done.9.q), channel_id=1, source_target_pairs={{0,8},{1,0},{8,16},{9,1},{16,24},{17,9},{24,25},{25,17},{2,10},{3,... | collective-permute-start | bytes 1179656 | tf_op jit(solution)/shard_map/ppermute | solution.py:303
  60.3 11.3 %collective-permute-start.16 = (bf16[128,768]{1,0:T(8,128)(2,1)}, bf16[128,768]{1,0:T(8,128)(2,1)S(1)}, u32[]{:S(2)}, u32[]{:S(2)}) collective-permute-start(bf16[128,768]{1,0:T(8,128)(2,1)} %collective-permute-done.15.m1), channel_id=1, source_target_pairs={{0,8},{1,0},{8,16},{9,1},{16,24},{17,9},{24,25},{25,17},{2,10},{3,... | collective-permute-start | bytes 589832 | tf_op jit(solution)/shard_map/ppermute | solution.py:303
  61.7 15.9 %collective-permute-start.19 = (bf16[64,1536]{1,0:T(8,128)(2,1)S(1)}, bf16[64,1536]{1,0:T(8,128)(2,1)S(1)}, u32[]{:S(2)}, u32[]{:S(2)}) collective-permute-start(bf16[64,1536]{1,0:T(8,128)(2,1)S(1)} %slice.33), channel_id=1, source_target_pairs={{0,16},{1,17},{8,24},{9,25},{16,0},{17,1},{24,8},{25,9},{2,18},{3,... | collective-permute-start | bytes 589832 | tf_op jit(solution)/shard_map/ppermute | solution.py:295
  62.3 12.0 %collective-permute-start.17 = (bf16[32,768]{1,0:T(8,128)(2,1)S(1)}, bf16[32,768]{1,0:T(8,128)(2,1)S(1)}, u32[]{:S(2)}, u32[]{:S(2)}) collective-permute-start(bf16[32,768]{1,0:T(8,128)(2,1)S(1)} %collective-permute-done.12.aux), channel_id=1, source_target_pairs={{0,8},{1,0},{8,16},{9,1},{16,24},{17,9},{24,25},{25,17},{2,10},{3,... | collective-permute-start | bytes 147464 | tf_op jit(solution)/shard_map/ppermute | solution.py:303
  (4 other events, 25.2 us)

commit v3 on v2

--- a/solution.py
+++ b/solution.py
@@ -90,34 +90,41 @@
     return parts
 
 
-def first_kernel(n, place, *refs):
-    parts, weights, out = refs[: 2 * n], refs[2 * n : 3 * n], refs[3 * n]
+def block_of(place, weight, depth, step):
+    ranks = weight.shape[1] // depth
+    source = lax.rem(place[2] - step + ranks, ranks)
+    return weight[:, pl.ds(pl.multiple_of(source * depth, 128), depth)]
+
+
+def first_kernel(place, *refs):
+    n = len(refs) // 2 - 1
+    weight, out = refs[2 * n :]
+    depth = refs[0].shape[1]
     for chunk in range(2):
         total = None
-        for part, weight in zip(parts[chunk * n : (chunk + 1) * n], weights):
-            term = nt(part[...], weight[...])
+        for step in range(n):
+            term = nt(refs[chunk * n + step][...], block_of(place, weight, depth, step))
             total = term if total is None else total + term
         out[chunk * TILE : (chunk + 1) * TILE, :] = total
 
 
-def middle_kernel(place, a_before, a_last, b_before, first, w_before, w_last, out, partial):
-    total = first[:TILE, :] + nt(a_before[...], w_before[...])
-    out[...] = (total + nt(a_last[...], w_last[...])).astype(BF)
-    partial[...] = first[TILE:, :] + nt(b_before[...], w_before[...])
-
-
-def last_kernel(place, b_last, partial, w_last, out):
-    out[...] = (partial[...] + nt(b_last[...], w_last[...])).astype(BF)
+def last_kernel(step, place, a_before, a_last, b_before, b_last, weight, first, out):
+    depth = a_last.shape[1]
+    before, last = (block_of(place, weight, depth, i) for i in (step - 1, step))
+    for chunk, parts in enumerate(((a_before, a_last), (b_before, b_last))):
+        rows = slice(chunk * TILE, (chunk + 1) * TILE)
+        total = first[rows, :] + nt(parts[0][...], before)
+        out[rows, :] = (total + nt(parts[1][...], last)).astype(BF)
 
 
 def softmax_kernel(
-    place, lists, q, k0, k1, k2, v0, v1, v2, tk, tv, m0, m1, aux, dscores, wide_k, wide_v
+    place, lists, q, k0, k1, k2, v0, v1, v2, tk, tv, g, aux, dscores, wide_k, wide_v
 ):
     stack_tiles((k0, k1, k2), wide_k)
     stack_tiles((v0, v1, v2), wide_v)
     row = lax.broadcasted_iota(jnp.int32, (AUX, TILE), 0)
     size = dscores.shape[0] // 2
-    for tile, message in enumerate((m0, m1)):
+    for tile in range(2):
         starts = [source_tile(place, lists, place[0] * 2 + tile, e) for e in range(3)]
         rows = slice(tile * TILE, (tile + 1) * TILE)
         for h in range(q.shape[1] // HD):
@@ -127,7 +134,7 @@
             weight = jnp.exp2((score - top) * SCALE2)
             total = jnp.sum(weight, axis=0, keepdims=True)
             prob = weight * (1.0 / total)
-            dprob = nt(gathered(wide_v, tv, starts, cols), message[:, cols])
+            dprob = nt(gathered(wide_v, tv, starts, cols), g[rows, cols])
             delta = jnp.sum(prob * dprob, axis=0, keepdims=True)
             dscores[tile * size : (tile + 1) * size, cols] = (prob * (dprob - delta)).astype(BF)
             lse = top * SCALE2 + jnp.log2(total)
@@ -165,11 +172,10 @@
     return jnp.where(found, 0.0, OFF)
 
 
-def key_terms(offs, keys, values, q, m0, m1, aux, cols):
+def key_terms(offs, keys, values, q, g, aux, cols):
     lines = [read_lines(aux, i, cols) for i in range(2)]
     delta = jnp.concatenate([d for d, _ in lines], axis=1)
     lse = [l for _, l in lines]
-    g = jnp.concatenate([m0[:, cols], m1[:, cols]], axis=0)
     score = nt(keys, q) * SCALE2
     pieces = []
     for i in range(2):
@@ -187,7 +193,7 @@
 
 
 def own_kernel(
-    place, lists, k, v, sk, sv, q, m0, m1, aux, key_acc, value_acc, text_k, text_v
+    place, lists, k, v, sk, sv, q, g, aux, key_acc, value_acc, text_k, text_v
 ):
     frame = k.shape[0]
     offs = all_offs(place, lists, place[0])
@@ -195,7 +201,7 @@
         cols = lanes(h)
         keys = jnp.concatenate([k[:, cols], sk[:, cols]], axis=0)
         values = jnp.concatenate([v[:, cols], sv[:, cols]], axis=0)
-        dk, dv = key_terms(offs, keys, values, q[:, cols], m0, m1, aux, cols)
+        dk, dv = key_terms(offs, keys, values, q[:, cols], g[:, cols], aux, cols)
         key_acc[:, cols] = dk[:frame]
         value_acc[:, cols] = dv[:frame]
         text_k[:, cols] = dk[frame:]
@@ -203,7 +209,7 @@
 
 
 def mate_kernel(
-    place, lists, k, v, sk, sv, valid, q, m0, m1, aux, key_in, value_in, text_k, text_v,
+    place, lists, k, v, sk, sv, valid, q, g, aux, key_in, value_in, text_k, text_v,
     key_acc, value_acc, keep, send,
 ):
     frame, width = k.shape
@@ -215,7 +221,7 @@
         more = slice(width + h * HD, width + (h + 1) * HD)
         keys = jnp.concatenate([k[:, cols], sk[:, cols]], axis=0)
         values = jnp.concatenate([v[:, cols], sv[:, cols]], axis=0)
-        dk, dv = key_terms(offs, keys, values, q[:, cols], m0, m1, aux, cols)
+        dk, dv = key_terms(offs, keys, values, q[:, cols], g[:, cols], aux, cols)
         key_acc[:, cols] = key_in[:, cols] + dk[:frame]
         value_acc[:, cols] = value_in[:, cols] + dv[:frame]
         part_k = jnp.where(live, (text_k[:, cols] + dk[frame:]) * SCALE, 0.0)
@@ -226,11 +232,11 @@
         send[:, more] = part_v[half:].astype(BF)
 
 
-def far_kernel(place, lists, k, v, q, m0, m1, aux, key_acc, value_acc, key_out, value_out):
+def far_kernel(place, lists, k, v, q, g, aux, key_acc, value_acc, key_out, value_out):
     offs = all_offs(place, lists, place[3])
     for h in range(k.shape[1] // HD):
         cols = lanes(h)
-        dk, dv = key_terms(offs, k[:, cols], v[:, cols], q[:, cols], m0, m1, aux, cols)
+        dk, dv = key_terms(offs, k[:, cols], v[:, cols], q[:, cols], g[:, cols], aux, cols)
         key_out[:, cols] = ((key_acc[:, cols] + dk) * SCALE).astype(BF)
         value_out[:, cols] = (value_acc[:, cols] + dv).astype(BF)
 
@@ -249,29 +255,6 @@
         scratch_shapes=list(scratch),
         compiler_params=pltpu.CompilerParams(vmem_limit_bytes=LIMIT),
     )(*arrays)
-
-
-def call_blocks(kernel, name, outs, place, arrays, weight, steps):
-    rows, depth = weight.shape[0], arrays[0].shape[1]
-    ranks = weight.shape[1] // depth
-
-    def block(step):
-        return pl.BlockSpec(
-            (rows, depth), lambda i, place: (0, lax.rem(place[2] - step + ranks, ranks))
-        )
-
-    return pl.pallas_call(
-        kernel,
-        name=name,
-        out_shape=outs,
-        grid_spec=pltpu.PrefetchScalarGridSpec(
-            num_scalar_prefetch=1,
-            grid=(1,),
-            in_specs=[VMEM] * len(arrays) + [block(step) for step in steps],
-            out_specs=jax.tree.map(lambda _: VMEM, outs),
-        ),
-        compiler_params=pltpu.CompilerParams(vmem_limit_bytes=LIMIT),
-    )(place, *arrays, *([weight] * len(steps)))
 
 
 def together(*arrays):
@@ -295,15 +278,11 @@
         return lax.ppermute(x, both, [(i, i ^ distance) for i in range(groups)])
 
     def relay(x):
-        def target(i):
-            if i % 2 == 0:
-                return i + 2 if i + 2 < groups else i + 1
-            return i - 2 if i >= 2 else i - 1
-
-        return lax.ppermute(x, both, [(i, target(i)) for i in range(groups)])
-
-    def ring(x):
-        return lax.ppermute(x, "head", [(i, (i + 1) % ranks) for i in range(ranks)])
+        turns = [(i, (i + 2 - 4 * (i % 2)) % groups) for i in range(groups)]
+        return lax.ppermute(x, both, turns)
+
+    def ring(x, way=1):
+        return lax.ppermute(x, "head", [(i, (i + way) % ranks) for i in range(ranks)])
 
     capacity = 2 * text_count // groups
     slots = groups // 2 * capacity
@@ -316,52 +295,35 @@
         (place, text_owner.reshape(1, text_count), text_keys, text_values),
     )
     part_a, part_b = [grad_output[:TILE]], [grad_output[TILE:]]
+    mate_v, mate_k, mate_q = swap(values), swap(keys), swap(queries)
     part_a.append(ring(part_a[0]))
     part_b.append(ring(part_b[0]))
-    mate_v = swap(values)
-    late_k, part_a[1] = together(keys, part_a[1])
-    mate_k = swap(late_k)
-    for _ in range(ranks - 2):
+    for step in range(ranks - 2):
+        if step == ranks - 3:
+            first = call(
+                first_kernel,
+                "first_blocks",
+                sds((frame, width), F32),
+                1,
+                (place, *part_a[:-1], *part_b[:-1], out_weight),
+            )
+            part_a[-1], mate_v = together(part_a[-1], mate_v)
+            part_b[-1], mate_k, first = together(part_b[-1], mate_k, first)
         part_a.append(ring(part_a[-1]))
         part_b.append(ring(part_b[-1]))
-    late_q, part_b[1] = together(queries, part_b[1])
-    mate_q = swap(late_q)
-    first = call_blocks(
-        functools.partial(first_kernel, ranks - 2),
-        "first_blocks",
-        sds((frame, width), F32),
-        place,
-        (*part_a[:-2], *part_b[:-2]),
-        out_weight,
-        range(ranks - 2),
-    )
-    late_v, part_a[-2] = together(mate_v, part_a[-2])
-    far_v = relay(late_v)
-    late_k, part_a[-1] = together(mate_k, part_a[-1])
-    far_k = relay(late_k)
-    late_q, part_b[-1] = together(mate_q, part_b[-1])
-    far_q = relay(late_q)
-
-    grad_a, partial = call_blocks(
-        middle_kernel,
-        "grad_heads_a",
-        (sds((TILE, width), BF), sds((TILE, width), F32)),
-        place,
-        (part_a[-2], part_a[-1], part_b[-2], first),
-        out_weight,
-        (ranks - 2, ranks - 1),
-    )
-    mate_a = swap(grad_a)
-    grad_b = call_blocks(
-        last_kernel,
-        "grad_heads_b",
-        sds((TILE, width), BF),
-        place,
-        (part_b[-1], partial),
-        out_weight,
-        (ranks - 1,),
-    )
-    mate_b = swap(grad_b)
+    part_a[-1], mate_v, mate_k = together(part_a[-1], mate_v, mate_k)
+    far_v, far_k = relay(mate_v), relay(mate_k)
+
+    grad = call(
+        functools.partial(last_kernel, ranks - 1),
+        "grad_heads",
+        sds((frame, width), BF),
+        1,
+        (place, *part_a[-2:], *part_b[-2:], out_weight, first),
+    )
+    late_grad, mate_q = together(grad, mate_q)
+    mate_g = swap(late_grad)
+    far_q = relay(mate_q)
     wide = pltpu.VMEM((3 * frame, width), BF)
     aux, dscores = call(
         softmax_kernel,
@@ -370,12 +332,13 @@
         2,
         (
             place, mask_lists, queries, keys, mate_k, far_k, values, mate_v, far_v,
-            text_keys, text_values, grad_a, grad_b,
+            text_keys, text_values, grad,
         ),
         (wide, wide),
     )
     mate_aux = swap(aux)
-    far_a, far_b, far_aux = relay(mate_a), relay(mate_b), relay(mate_aux)
+    far_g, far_aux = relay(mate_g), relay(mate_aux)
+    own_aux, far_q = together(aux, far_q)
     acc = sds((frame, width), F32)
     text_acc = sds((slots, width), F32)
     accs = call(
@@ -383,15 +346,14 @@
         "own_keys",
         (acc, acc, text_acc, text_acc),
         2,
-        (place, mask_lists, keys, values, sk, sv, queries, grad_a, grad_b, aux),
-    )
-    late_aux, far_a = together(mate_aux, far_a)
+        (place, mask_lists, keys, values, sk, sv, queries, grad, own_aux),
+    )
     key_acc, value_acc, keep, send = call(
         mate_kernel,
         "mate_keys",
         (acc, acc, sds((slots // 2, 2 * width), F32), sds((slots // 2, 2 * width), BF)),
         2,
-        (place, mask_lists, keys, values, sk, sv, valid, mate_q, mate_a, mate_b, late_aux, *accs),
+        (place, mask_lists, keys, values, sk, sv, valid, mate_q, mate_g, mate_aux, *accs),
     )
     query_grads = call(
         query_kernel,
@@ -406,7 +368,7 @@
         "far_keys",
         (sds((frame, width), BF),) * 2,
         2,
-        (place, mask_lists, keys, values, far_q, far_a, far_b, far_aux, key_acc, value_acc),
+        (place, mask_lists, keys, values, far_q, far_g, far_aux, key_acc, value_acc),
     )
     stages = []
     distance = 2

time: 78.6 us -> 69.9 us (0.89)
  the two profiles are of different devices: /device:TPU:27 before, /device:TPU:0 now
where the time goes in v3:
time: 69.9 us; the launch traced here: 69.6 us
  waiting for transfers between devices  25.5 us (36%)
  Pallas kernels  20.7 us (30%)
  starting transfers between devices  16.5 us (24%)
  local copies, waits for them, and re-layouts  5.82 us (8%)
  between operations  0.82 us (1%)
    pallas_call x8, Pallas kernels, call(): pl.pallas_call(kernel, name=name, out_shape=outs, in_specs=[SMEM] * scala...  20.7 us
    ppermute x6, waiting for transfers between devices, ring(): lax.ppermute(x, 'head', [(i, (i + way) % ranks) for i in range(ranks)])  15.3 us
    ppermute x7, starting transfers between devices, swap(): return lax.ppermute(x, both, [(i, i ^ distance) for i in range(groups)])  7.78 us
    ppermute x5, waiting for transfers between devices, relay(): return lax.ppermute(x, both, turns)  7.34 us
    ppermute x6, starting transfers between devices, ring(): lax.ppermute(x, 'head', [(i, (i + way) % ranks) for i in range(ranks)])  6.7 us
    unnamed x21, local copies, waits for them, and re-layouts  4.07 us
    ppermute x7, waiting for transfers between devices, swap(): return lax.ppermute(x, both, [(i, i ^ distance) for i in range(groups)])  2.94 us
    ppermute x5, starting transfers between devices, relay(): return lax.ppermute(x, both, turns)  2 us
  transfers between devices with their start and end apart: 18, of which 11 were waited for; matrix products, arithmetic and copies ran while one was open for 1% of the time, Pallas kernels for 26%

profile of v3, /device:TPU:0, one launch (start us, length us, event | category | flops | bytes accessed | tf_op | source)
XLA Modules:
  0.0 69.6 jit_solution(1616418756189956998)
XLA Ops:
  0.6 1.0 %fusion.1 = (bf16[128,768]{1,0:T(8,128)(2,1)S(1)}, bf16[128,768]{1,0:T(8,128)(2,1)S(1)}) fusion(bf16[256,768]{1,0:T(8,128)(2,1)} %param.12), kind=kLoop, calls=%fused_computation.5 | loop fusion | bytes 786432 | tf_op jit(solution)/shard_map/slice | solution.py:297
  1.7 3.1 %collective-permute-start = (bf16[128,768]{1,0:T(8,128)(2,1)S(1)}, bf16[128,768]{1,0:T(8,128)(2,1)S(1)}, u32[]{:S(2)}, u32[]{:S(2)}) collective-permute-start(bf16[128,768]{1,0:T(8,128)(2,1)S(1)} %get-tuple-element.60.refs_0_), channel_id=1, source_target_pairs={{0,2},{2,4},{4,6},{6,0},{1,3},{3,5},{5,7},{7,1},{8,10},{10,12},{12... | collective-permute-start | bytes 589832 | tf_op jit(solution)/shard_map/ppermute | solution.py:285
  4.8 1.5 %collective-permute-start.2 = (bf16[256,768]{1,0:T(8,128)(2,1)}, bf16[256,768]{1,0:T(8,128)(2,1)}, u32[]{:S(2)}, u32[]{:S(2)}) collective-permute-start(bf16[256,768]{1,0:T(8,128)(2,1)} %v.5), channel_id=1, source_target_pairs={{0,1},{1,0},{8,9},{9,8},{16,17},{17,16},{24,25},{25,24},{2,3},{3,2... | collective-permute-start | bytes 1179656 | tf_op jit(solution)/shard_map/ppermute | solution.py:278
  6.3 1.6 %collective-permute-start.4 = (bf16[128,768]{1,0:T(8,128)(2,1)S(1)}, bf16[128,768]{1,0:T(8,128)(2,1)S(1)}, u32[]{:S(2)}, u32[]{:S(2)}) collective-permute-start(bf16[128,768]{1,0:T(8,128)(2,1)S(1)} %get-tuple-element.59.refs_2_), channel_id=1, source_target_pairs={{0,2},{2,4},{4,6},{6,0},{1,3},{3,5},{5,7},{7,1},{8,10},{10,12},{12... | collective-permute-start | bytes 589832 | tf_op jit(solution)/shard_map/ppermute | solution.py:285
  8.4 4.2 %collective-permute-done.refs_1_ = bf16[128,768]{1,0:T(8,128)(2,1)S(1)} collective-permute-done((bf16[128,768]{1,0:T(8,128)(2,1)S(1)}, bf16[128,768]{1,0:T(8,128)(2,1)S(1)}, u32[]{:S(2)}, u32[]{:S(2)}) %collective-permute-start) | collective-permute-done | bytes 196640 | tf_op jit(solution)/shard_map/ppermute | solution.py:285
  12.5 3.8 %collective-permute-done.4.refs_3_ = bf16[128,768]{1,0:T(8,128)(2,1)S(1)} collective-permute-done((bf16[128,768]{1,0:T(8,128)(2,1)S(1)}, bf16[128,768]{1,0:T(8,128)(2,1)S(1)}, u32[]{:S(2)}, u32[]{:S(2)}) %collective-permute-start.4) | collective-permute-done | bytes 196640 | tf_op jit(solution)/shard_map/ppermute | solution.py:285
  16.8 1.5 %collective-permute-start.10 = (bf16[256,768]{1,0:T(8,128)(2,1)}, bf16[256,768]{1,0:T(8,128)(2,1)S(1)}, u32[]{:S(2)}, u32[]{:S(2)}) collective-permute-start(bf16[256,768]{1,0:T(8,128)(2,1)} %q.3), channel_id=1, source_target_pairs={{0,1},{1,0},{8,9},{9,8},{16,17},{17,16},{24,25},{25,24},{2,3},{3,2... | collective-permute-start | bytes 1179656 | tf_op jit(solution)/shard_map/ppermute | solution.py:278
  18.3 2.3 %collective-permute-done.1.a_before = bf16[128,768]{1,0:T(8,128)(2,1)S(1)} collective-permute-done((bf16[128,768]{1,0:T(8,128)(2,1)S(1)}, bf16[128,768]{1,0:T(8,128)(2,1)S(1)}, u32[]{:S(2)}, u32[]{:S(2)}) %collective-permute-start.1) | collective-permute-done | bytes 196640 | tf_op jit(solution)/shard_map/ppermute | solution.py:285
  21.1 2.3 %copy-done = bf16[768,3072]{1,0:T(8,128)(2,1)S(1)} copy-done((bf16[768,3072]{1,0:T(8,128)(2,1)S(1)}, bf16[768,3072]{1,0:T(8,128)(2,1)}, u32[]{:S(2)}) %copy-start) | copy-done | bytes 4718616
  23.4 2.3 %first_blocks.1.first = f32[256,768]{1,0:T(8,128)S(1)} custom-call(s32[4]{0:T(128)S(1)} %pad_add_fusion.place, bf16[128,768]{1,0:T(8,128)(2,1)S(1)} %get-tuple-element.60.refs_0_, bf16[128,768]{1,0:T(8,128)(2,1)S(1)} %collective-permute-done.refs_1_, bf16[128,768]{1,0:T(8,128)(2,1)S(1)} %get-tuple-element.59.refs_2_, ...), custom_call_target="tpu_custom_call" | custom-call | tf_op jit(solution)/shard_map/first_blocks/pallas_call | solution.py:249
  26.1 1.2 %collective-permute-start.9 = (bf16[128,768]{1,0:T(8,128)(2,1)}, bf16[128,768]{1,0:T(8,128)(2,1)S(1)}, u32[]{:S(2)}, u32[]{:S(2)}) collective-permute-start(bf16[128,768]{1,0:T(8,128)(2,1)} %collective-permute-done.5.b_before), channel_id=1, source_target_pairs={{0,2},{2,4},{4,6},{6,0},{1,3},{3,5},{5,7},{7,1},{8,10},{10,12},{12... | collective-permute-start | bytes 589832 | tf_op jit(solution)/shard_map/ppermute | solution.py:285
  27.4 1.7 %collective-permute-done.3.a_last = bf16[128,768]{1,0:T(8,128)(2,1)S(1)} collective-permute-done((bf16[128,768]{1,0:T(8,128)(2,1)S(1)}, bf16[128,768]{1,0:T(8,128)(2,1)S(1)}, u32[]{:S(2)}, u32[]{:S(2)}) %collective-permute-start.3) | collective-permute-done | bytes 196640 | tf_op jit(solution)/shard_map/ppermute | solution.py:285
  29.1 1.9 %collective-permute-start.7 = (bf16[256,768]{1,0:T(8,128)(2,1)S(1)}, bf16[256,768]{1,0:T(8,128)(2,1)S(1)}, u32[]{:S(2)}, u32[]{:S(2)}) collective-permute-start(bf16[256,768]{1,0:T(8,128)(2,1)S(1)} %collective-permute-done.6.k1), channel_id=1, source_target_pairs={{0,8},{1,25},{8,16},{9,1},{16,24},{17,9},{24,0},{25,17},{2,10},{3,... | collective-permute-start | bytes 1179656 | tf_op jit(solution)/shard_map/ppermute | solution.py:282
  30.9 2.9 %collective-permute-done.9.b_last = bf16[128,768]{1,0:T(8,128)(2,1)S(1)} collective-permute-done((bf16[128,768]{1,0:T(8,128)(2,1)}, bf16[128,768]{1,0:T(8,128)(2,1)S(1)}, u32[]{:S(2)}, u32[]{:S(2)}) %collective-permute-start.9) | collective-permute-done | bytes 196640 | tf_op jit(solution)/shard_map/ppermute | solution.py:285
  34.7 2.6 %grad_heads.1.g = bf16[256,768]{1,0:T(8,128)(2,1)S(1)} custom-call(s32[4]{0:T(128)S(1)} %pad_add_fusion.place, bf16[128,768]{1,0:T(8,128)(2,1)S(1)} %copy-done.8, bf16[128,768]{1,0:T(8,128)(2,1)S(1)} %collective-permute-done.3.a_last, bf16[128,768]{1,0:T(8,128)(2,1)} %collective-permute-done.5.b_before, bf16[128,768]{1,0:T(8,128)(2,1)S(1)} %collective-permute-done.9.b_last, ...), custom_call_target="tpu_custom_call" | custom-call | tf_op jit(solution)/shard_map/grad_heads/pallas_call | solution.py:249
  37.4 1.8 %collective-permute-start.12 = (bf16[256,768]{1,0:T(8,128)(2,1)S(1)}, bf16[256,768]{1,0:T(8,128)(2,1)}, u32[]{:S(2)}, u32[]{:S(2)}) collective-permute-start(bf16[256,768]{1,0:T(8,128)(2,1)S(1)} %grad_heads.1.g), channel_id=1, source_target_pairs={{0,1},{1,0},{8,9},{9,8},{16,17},{17,16},{24,25},{25,24},{2,3},{3,2... | collective-permute-start | bytes 1179656 | tf_op jit(solution)/shard_map/ppermute | solution.py:278
  40.7 3.8 %softmax.1 = (bf16[32,768]{1,0:T(8,128)(2,1)S(1)}, bf16[1280,768]{1,0:T(8,128)(2,1)S(1)}) custom-call(s32[4]{0:T(128)S(1)} %pad_add_fusion.place, s32[16,3]{1,0:T(8,128)S(1)} %copy.15.lists, bf16[256,768]{1,0:T(8,128)(2,1)S(1)} %copy-done.6, bf16[256,768]{1,0:T(8,128)(2,1)S(1)} %copy-done.2, bf16[256,768]{1,0:T(8,128)(2,1)S(1)} %collective-permute-done.6.k1, ...), custom_call_target="tpu_custom_call" | custom-call | tf_op jit(solution)/shard_map/softmax/pallas_call | solution.py:249
  45.6 2.5 %own_keys.1 = (f32[256,768]{1,0:T(8,128)S(1)}, f32[256,768]{1,0:T(8,128)S(1)}, f32[256,768]{1,0:T(8,128)S(1)}, f32[256,768]{1,0:T(8,128)S(1)}) custom-call(s32[4]{0:T(128)S(1)} %pad_add_fusion.place, s32[16,3]{1,0:T(8,128)S(1)} %copy.15.lists, bf16[256,768]{1,0:T(8,128)(2,1)S(1)} %copy-done.2, bf16[256,768]{1,0:T(8,128)(2,1)S(1)} %copy-done.3, ...), custom_call_target="tpu_custom_call" | custom-call | tf_op jit(solution)/shard_map/own_keys/pallas_call | solution.py:249
  49.7 2.8 %mate_keys.1 = (f32[256,768]{1,0:T(8,128)S(1)}, f32[256,768]{1,0:T(8,128)S(1)}, f32[128,1536]{1,0:T(8,128)S(1)}, bf16[128,1536]{1,0:T(8,128)(2,1)S(1)}) custom-call(s32[4]{0:T(128)S(1)} %pad_add_fusion.place, s32[16,3]{1,0:T(8,128)S(1)} %copy.15.lists, bf16[256,768]{1,0:T(8,128)(2,1)S(1)} %copy-done.2, bf16[256,768]{1,0:T(8,128)(2,1)S(1)} %copy-done.3, ...), custom_call_target="tpu_custom_call" | custom-call | tf_op jit(solution)/shard_map/mate_keys/pallas_call | solution.py:249
  53.3 1.3 %collective-permute-done.16 = bf16[128,1536]{1,0:T(8,128)(2,1)S(1)} collective-permute-done((bf16[128,1536]{1,0:T(8,128)(2,1)S(1)}, bf16[128,1536]{1,0:T(8,128)(2,1)S(1)}, u32[]{:S(2)}, u32[]{:S(2)}) %collective-permute-start.16) | collective-permute-done | bytes 393248 | tf_op jit(solution)/shard_map/ppermute | solution.py:278
  54.8 1.7 %collective-permute-start.17 = (bf16[64,1536]{1,0:T(8,128)(2,1)S(1)}, bf16[64,1536]{1,0:T(8,128)(2,1)S(1)}, u32[]{:S(2)}, u32[]{:S(2)}) collective-permute-start(bf16[64,1536]{1,0:T(8,128)(2,1)S(1)} %slice.33), channel_id=1, source_target_pairs={{0,16},{1,17},{8,24},{9,25},{16,0},{17,1},{24,8},{25,9},{2,18},{3,... | collective-permute-start | bytes 589832 | tf_op jit(solution)/shard_map/ppermute | solution.py:278
  56.5 2.3 %query_grads.1 = bf16[256,768]{1,0:T(8,128)(2,1)} custom-call(s32[4]{0:T(128)S(1)} %pad_add_fusion.place, s32[16,3]{1,0:T(8,128)S(1)} %copy.15.lists, bf16[256,768]{1,0:T(8,128)(2,1)S(1)} %copy-done.2, bf16[256,768]{1,0:T(8,128)(2,1)S(1)} %collective-permute-done.6.k1, bf16[256,768]{1,0:T(8,128)(2,1)S(1)} %collective-permute-done.7.k2, ...), custom_call_target="tpu_custom_call" | custom-call | tf_op jit(solution)/shard_map/query_grads/pallas_call | solution.py:249
  58.8 6.6 %collective-permute-done.15.aux = bf16[32,768]{1,0:T(8,128)(2,1)S(1)} collective-permute-done((bf16[32,768]{1,0:T(8,128)(2,1)S(1)}, bf16[32,768]{1,0:T(8,128)(2,1)S(1)}, u32[]{:S(2)}, u32[]{:S(2)}) %collective-permute-start.15) | collective-permute-done | bytes 49184 | tf_op jit(solution)/shard_map/ppermute | solution.py:282
  65.4 3.4 %far_keys.1 = (bf16[256,768]{1,0:T(8,128)(2,1)}, bf16[256,768]{1,0:T(8,128)(2,1)}) custom-call(s32[4]{0:T(128)S(1)} %pad_add_fusion.place, s32[16,3]{1,0:T(8,128)S(1)} %copy.15.lists, bf16[256,768]{1,0:T(8,128)(2,1)S(1)} %copy-done.2, bf16[256,768]{1,0:T(8,128)(2,1)S(1)} %copy-done.3, bf16[256,768]{1,0:T(8,128)(2,1)} %collective-permute-done.11.q, ...), custom_call_target="tpu_custom_call" | custom-call | tf_op jit(solution)/shard_map/far_keys/pallas_call | solution.py:249
  (47 shorter events, 8.6 us)
Async XLA Ops:
  1.7 10.8 %collective-permute-start = (bf16[128,768]{1,0:T(8,128)(2,1)S(1)}, bf16[128,768]{1,0:T(8,128)(2,1)S(1)}, u32[]{:S(2)}, u32[]{:S(2)}) collective-permute-start(bf16[128,768]{1,0:T(8,128)(2,1)S(1)} %get-tuple-element.60.refs_0_), channel_id=1, source_target_pairs={{0,2},{2,4},{4,6},{6,0},{1,3},{3,5},{5,7},{7,1},{8,10},{10,12},{12... | collective-permute-start | bytes 589832 | tf_op jit(solution)/shard_map/ppermute | solution.py:285
  4.8 15.8 %collective-permute-start.2 = (bf16[256,768]{1,0:T(8,128)(2,1)}, bf16[256,768]{1,0:T(8,128)(2,1)}, u32[]{:S(2)}, u32[]{:S(2)}) collective-permute-start(bf16[256,768]{1,0:T(8,128)(2,1)} %v.5), channel_id=1, source_target_pairs={{0,1},{1,0},{8,9},{9,8},{16,17},{17,16},{24,25},{25,24},{2,3},{3,2... | collective-permute-start | bytes 1179656 | tf_op jit(solution)/shard_map/ppermute | solution.py:278
  6.3 10.1 %collective-permute-start.4 = (bf16[128,768]{1,0:T(8,128)(2,1)S(1)}, bf16[128,768]{1,0:T(8,128)(2,1)S(1)}, u32[]{:S(2)}, u32[]{:S(2)}) collective-permute-start(bf16[128,768]{1,0:T(8,128)(2,1)S(1)} %get-tuple-element.59.refs_2_), channel_id=1, source_target_pairs={{0,2},{2,4},{4,6},{6,0},{1,3},{3,5},{5,7},{7,1},{8,10},{10,12},{12... | collective-permute-start | bytes 589832 | tf_op jit(solution)/shard_map/ppermute | solution.py:285
  7.8 18.3 %collective-permute-start.6 = (bf16[256,768]{1,0:T(8,128)(2,1)}, bf16[256,768]{1,0:T(8,128)(2,1)S(1)}, u32[]{:S(2)}, u32[]{:S(2)}) collective-permute-start(bf16[256,768]{1,0:T(8,128)(2,1)} %k.5), channel_id=1, source_target_pairs={{0,1},{1,0},{8,9},{9,8},{16,17},{17,16},{24,25},{25,24},{2,3},{3,2... | collective-permute-start | bytes 1179656 | tf_op jit(solution)/shard_map/ppermute | solution.py:278
  12.5 8.1 %collective-permute-start.1 = (bf16[128,768]{1,0:T(8,128)(2,1)S(1)}, bf16[128,768]{1,0:T(8,128)(2,1)S(1)}, u32[]{:S(2)}, u32[]{:S(2)}) collective-permute-start(bf16[128,768]{1,0:T(8,128)(2,1)S(1)} %collective-permute-done.refs_1_), channel_id=1, source_target_pairs={{0,2},{2,4},{4,6},{6,0},{1,3},{3,5},{5,7},{7,1},{8,10},{10,12},{12... | collective-permute-start | bytes 589832 | tf_op jit(solution)/shard_map/ppermute | solution.py:285
  16.4 9.7 %collective-permute-start.5 = (bf16[128,768]{1,0:T(8,128)(2,1)S(1)}, bf16[128,768]{1,0:T(8,128)(2,1)}, u32[]{:S(2)}, u32[]{:S(2)}) collective-permute-start(bf16[128,768]{1,0:T(8,128)(2,1)S(1)} %collective-permute-done.4.refs_3_), channel_id=1, source_target_pairs={{0,2},{2,4},{4,6},{6,0},{1,3},{3,5},{5,7},{7,1},{8,10},{10,12},{12... | collective-permute-start | bytes 589832 | tf_op jit(solution)/shard_map/ppermute | solution.py:285
  16.8 20.6 %collective-permute-start.10 = (bf16[256,768]{1,0:T(8,128)(2,1)}, bf16[256,768]{1,0:T(8,128)(2,1)S(1)}, u32[]{:S(2)}, u32[]{:S(2)}) collective-permute-start(bf16[256,768]{1,0:T(8,128)(2,1)} %q.3), channel_id=1, source_target_pairs={{0,1},{1,0},{8,9},{9,8},{16,17},{17,16},{24,25},{25,24},{2,3},{3,2... | collective-permute-start | bytes 1179656 | tf_op jit(solution)/shard_map/ppermute | solution.py:278
  20.6 8.5 %collective-permute-start.3 = (bf16[128,768]{1,0:T(8,128)(2,1)S(1)}, bf16[128,768]{1,0:T(8,128)(2,1)S(1)}, u32[]{:S(2)}, u32[]{:S(2)}) collective-permute-start(bf16[128,768]{1,0:T(8,128)(2,1)S(1)} %collective-permute-done.1.a_before), channel_id=1, source_target_pairs={{0,2},{2,4},{4,6},{6,0},{1,3},{3,5},{5,7},{7,1},{8,10},{10,12},{12... | collective-permute-start | bytes 589832 | tf_op jit(solution)/shard_map/ppermute | solution.py:285
  23.4 21.2 %copy-start.9 = (s32[256]{0:T(256)S(1)}, s32[256]{0:T(256)}, u32[]{:S(2)}) copy-start(s32[256]{0:T(256)} %param.17) | copy-start | bytes 3076
  25.7 15.0 %copy-start.2 = (bf16[256,768]{1,0:T(8,128)(2,1)S(1)}, bf16[256,768]{1,0:T(8,128)(2,1)}, u32[]{:S(2)}) copy-start(bf16[256,768]{1,0:T(8,128)(2,1)} %k.5) | copy-start | bytes 1179652
  25.7 15.0 %copy-start.3 = (bf16[256,768]{1,0:T(8,128)(2,1)S(1)}, bf16[256,768]{1,0:T(8,128)(2,1)}, u32[]{:S(2)}) copy-start(bf16[256,768]{1,0:T(8,128)(2,1)} %v.5) | copy-start | bytes 1179652
  25.7 15.0 %copy-start.4 = (bf16[256,768]{1,0:T(8,128)(2,1)S(1)}, bf16[256,768]{1,0:T(8,128)(2,1)}, u32[]{:S(2)}) copy-start(bf16[256,768]{1,0:T(8,128)(2,1)} %tk.5) | copy-start | bytes 1179652
  25.7 15.0 %copy-start.5 = (bf16[256,768]{1,0:T(8,128)(2,1)S(1)}, bf16[256,768]{1,0:T(8,128)(2,1)}, u32[]{:S(2)}) copy-start(bf16[256,768]{1,0:T(8,128)(2,1)} %tv.3) | copy-start | bytes 1179652
  25.7 15.0 %copy-start.6 = (bf16[256,768]{1,0:T(8,128)(2,1)S(1)}, bf16[256,768]{1,0:T(8,128)(2,1)}, u32[]{:S(2)}) copy-start(bf16[256,768]{1,0:T(8,128)(2,1)} %q.3) | copy-start | bytes 1179652
  26.1 7.7 %collective-permute-start.9 = (bf16[128,768]{1,0:T(8,128)(2,1)}, bf16[128,768]{1,0:T(8,128)(2,1)S(1)}, u32[]{:S(2)}, u32[]{:S(2)}) collective-permute-start(bf16[128,768]{1,0:T(8,128)(2,1)} %collective-permute-done.5.b_before), channel_id=1, source_target_pairs={{0,2},{2,4},{4,6},{6,0},{1,3},{3,5},{5,7},{7,1},{8,10},{10,12},{12... | collective-permute-start | bytes 589832 | tf_op jit(solution)/shard_map/ppermute | solution.py:285
  29.1 10.9 %collective-permute-start.8 = (bf16[256,768]{1,0:T(8,128)(2,1)}, bf16[256,768]{1,0:T(8,128)(2,1)}, u32[]{:S(2)}, u32[]{:S(2)}) collective-permute-start(bf16[256,768]{1,0:T(8,128)(2,1)} %collective-permute-done.2.v1), channel_id=1, source_target_pairs={{0,8},{1,25},{8,16},{9,1},{16,24},{17,9},{24,0},{25,17},{2,10},{3,... | collective-permute-start | bytes 1179656 | tf_op jit(solution)/shard_map/ppermute | solution.py:282
  29.1 11.6 %collective-permute-start.7 = (bf16[256,768]{1,0:T(8,128)(2,1)S(1)}, bf16[256,768]{1,0:T(8,128)(2,1)S(1)}, u32[]{:S(2)}, u32[]{:S(2)}) collective-permute-start(bf16[256,768]{1,0:T(8,128)(2,1)S(1)} %collective-permute-done.6.k1), channel_id=1, source_target_pairs={{0,8},{1,25},{8,16},{9,1},{16,24},{17,9},{24,0},{25,17},{2,10},{3,... | collective-permute-start | bytes 1179656 | tf_op jit(solution)/shard_map/ppermute | solution.py:282
  37.4 8.2 %collective-permute-start.11 = (bf16[256,768]{1,0:T(8,128)(2,1)S(1)}, bf16[256,768]{1,0:T(8,128)(2,1)}, u32[]{:S(2)}, u32[]{:S(2)}) collective-permute-start(bf16[256,768]{1,0:T(8,128)(2,1)S(1)} %collective-permute-done.10.q), channel_id=1, source_target_pairs={{0,8},{1,25},{8,16},{9,1},{16,24},{17,9},{24,0},{25,17},{2,10},{3,... | collective-permute-start | bytes 1179656 | tf_op jit(solution)/shard_map/ppermute | solution.py:282
  37.4 11.4 %collective-permute-start.12 = (bf16[256,768]{1,0:T(8,128)(2,1)S(1)}, bf16[256,768]{1,0:T(8,128)(2,1)}, u32[]{:S(2)}, u32[]{:S(2)}) collective-permute-start(bf16[256,768]{1,0:T(8,128)(2,1)S(1)} %grad_heads.1.g), channel_id=1, source_target_pairs={{0,1},{1,0},{8,9},{9,8},{16,17},{17,16},{24,25},{25,24},{2,3},{3,2... | collective-permute-start | bytes 1179656 | tf_op jit(solution)/shard_map/ppermute | solution.py:278
  44.5 5.2 %collective-permute-start.14 = (bf16[32,768]{1,0:T(8,128)(2,1)S(1)}, bf16[32,768]{1,0:T(8,128)(2,1)S(1)}, u32[]{:S(2)}, u32[]{:S(2)}) collective-permute-start(bf16[32,768]{1,0:T(8,128)(2,1)S(1)} %get-tuple-element.48.aux), channel_id=1, source_target_pairs={{0,1},{1,0},{8,9},{9,8},{16,17},{17,16},{24,25},{25,24},{2,3},{3,2... | collective-permute-start | bytes 147464 | tf_op jit(solution)/shard_map/ppermute | solution.py:278
  52.6 2.0 %collective-permute-start.16 = (bf16[128,1536]{1,0:T(8,128)(2,1)S(1)}, bf16[128,1536]{1,0:T(8,128)(2,1)S(1)}, u32[]{:S(2)}, u32[]{:S(2)}) collective-permute-start(bf16[128,1536]{1,0:T(8,128)(2,1)S(1)} %get-tuple-element.58), channel_id=1, source_target_pairs={{0,8},{1,9},{8,0},{9,1},{16,24},{17,25},{24,16},{25,17},{2,10},{3,... | collective-permute-start | bytes 1179656 | tf_op jit(solution)/shard_map/ppermute | solution.py:278
  53.3 12.2 %collective-permute-start.13 = (bf16[256,768]{1,0:T(8,128)(2,1)}, bf16[256,768]{1,0:T(8,128)(2,1)S(1)}, u32[]{:S(2)}, u32[]{:S(2)}) collective-permute-start(bf16[256,768]{1,0:T(8,128)(2,1)} %collective-permute-done.12.g), channel_id=1, source_target_pairs={{0,8},{1,25},{8,16},{9,1},{16,24},{17,9},{24,0},{25,17},{2,10},{3,... | collective-permute-start | bytes 1179656 | tf_op jit(solution)/shard_map/ppermute | solution.py:282
  54.8 14.1 %collective-permute-start.17 = (bf16[64,1536]{1,0:T(8,128)(2,1)S(1)}, bf16[64,1536]{1,0:T(8,128)(2,1)S(1)}, u32[]{:S(2)}, u32[]{:S(2)}) collective-permute-start(bf16[64,1536]{1,0:T(8,128)(2,1)S(1)} %slice.33), channel_id=1, source_target_pairs={{0,16},{1,17},{8,24},{9,25},{16,0},{17,1},{24,8},{25,9},{2,18},{3,... | collective-permute-start | bytes 589832 | tf_op jit(solution)/shard_map/ppermute | solution.py:278
  56.5 9.0 %collective-permute-start.15 = (bf16[32,768]{1,0:T(8,128)(2,1)S(1)}, bf16[32,768]{1,0:T(8,128)(2,1)S(1)}, u32[]{:S(2)}, u32[]{:S(2)}) collective-permute-start(bf16[32,768]{1,0:T(8,128)(2,1)S(1)} %collective-permute-done.14.aux), channel_id=1, source_target_pairs={{0,8},{1,25},{8,16},{9,1},{16,24},{17,9},{24,0},{25,17},{2,10},{3,... | collective-permute-start | bytes 147464 | tf_op jit(solution)/shard_map/ppermute | solution.py:282
  (4 other events, 24.0 us)

commit v4 on v3

--- a/solution.py
+++ b/solution.py
@@ -14,6 +14,8 @@
 SCALE = HD ** (-0.5)
 SCALE2 = SCALE * math.log2(math.e)
 OFF = 1e30
+GROUP = 3
+PAIRS = 3
 BF = jnp.bfloat16
 F32 = jnp.float32
 LIMIT = 16 << 20
@@ -37,7 +39,7 @@
 
 def source_tile(place, lists, tile, entry):
     slab, mate = place[0], place[1]
-    listed = lists[tile, entry]
+    listed = lists[entry, tile]
     owner = lax.shift_right_logical(listed, 1)
     source = jnp.where(owner == slab, 0, jnp.where(owner == mate, 1, 2))
     return pl.multiple_of((source * 2 + (listed & 1)) * TILE, TILE)
@@ -108,13 +110,18 @@
         out[chunk * TILE : (chunk + 1) * TILE, :] = total
 
 
-def last_kernel(step, place, a_before, a_last, b_before, b_last, weight, first, out):
-    depth = a_last.shape[1]
-    before, last = (block_of(place, weight, depth, i) for i in (step - 1, step))
-    for chunk, parts in enumerate(((a_before, a_last), (b_before, b_last))):
+def second_kernel(step, place, a_before, b_before, weight, first, out):
+    block = block_of(place, weight, a_before.shape[1], step)
+    for chunk, part in enumerate((a_before, b_before)):
         rows = slice(chunk * TILE, (chunk + 1) * TILE)
-        total = first[rows, :] + nt(parts[0][...], before)
-        out[rows, :] = (total + nt(parts[1][...], last)).astype(BF)
+        out[rows, :] = first[rows, :] + nt(part[...], block)
+
+
+def last_kernel(step, place, a_last, b_last, weight, second, out):
+    block = block_of(place, weight, a_last.shape[1], step)
+    for chunk, part in enumerate((a_last, b_last)):
+        rows = slice(chunk * TILE, (chunk + 1) * TILE)
+        out[rows, :] = (second[rows, :] + nt(part[...], block)).astype(BF)
 
 
 def softmax_kernel(
@@ -124,17 +131,20 @@
     stack_tiles((v0, v1, v2), wide_v)
     row = lax.broadcasted_iota(jnp.int32, (AUX, TILE), 0)
     size = dscores.shape[0] // 2
+    jobs = []
     for tile in range(2):
         starts = [source_tile(place, lists, place[0] * 2 + tile, e) for e in range(3)]
         rows = slice(tile * TILE, (tile + 1) * TILE)
-        for h in range(q.shape[1] // HD):
-            cols = lanes(h)
-            score = nt(gathered(wide_k, tk, starts, cols), q[rows, cols])
+        jobs += [(tile, rows, starts, lanes(h)) for h in range(q.shape[1] // HD)]
+    for first in range(0, len(jobs), PAIRS):
+        group = jobs[first : first + PAIRS]
+        scores = [nt(gathered(wide_k, tk, at, cols), q[rows, cols]) for _, rows, at, cols in group]
+        dprobs = [nt(gathered(wide_v, tv, at, cols), g[rows, cols]) for _, rows, at, cols in group]
+        for (tile, _, _, cols), score, dprob in zip(group, scores, dprobs):
             top = jnp.max(score, axis=0, keepdims=True)
             weight = jnp.exp2((score - top) * SCALE2)
             total = jnp.sum(weight, axis=0, keepdims=True)
             prob = weight * (1.0 / total)
-            dprob = nt(gathered(wide_v, tv, starts, cols), g[rows, cols])
             delta = jnp.sum(prob * dprob, axis=0, keepdims=True)
             dscores[tile * size : (tile + 1) * size, cols] = (prob * (dprob - delta)).astype(BF)
             lse = top * SCALE2 + jnp.log2(total)
@@ -163,82 +173,122 @@
 
 
 def off_by(place, lists, slab, tile, key_tile):
-    count = lists.shape[0]
+    count = lists.shape[1]
     query_tile = slab * 2 + tile
     row = jnp.clip(query_tile, 0, count - 1)
     wanted = place[0] * 2 + key_tile
-    found = (lists[row, 0] == wanted) | (lists[row, 1] == wanted) | (lists[row, 2] == wanted)
+    found = (lists[0, row] == wanted) | (lists[1, row] == wanted) | (lists[2, row] == wanted)
     found = found & (query_tile >= 0) & (query_tile < count)
     return jnp.where(found, 0.0, OFF)
 
 
-def key_terms(offs, keys, values, q, g, aux, cols):
-    lines = [read_lines(aux, i, cols) for i in range(2)]
-    delta = jnp.concatenate([d for d, _ in lines], axis=1)
-    lse = [l for _, l in lines]
-    score = nt(keys, q) * SCALE2
-    pieces = []
-    for i in range(2):
-        line = jnp.concatenate([lse[t] + offs[t][i] for t in range(2)], axis=1)
-        pieces.append(score[i * TILE : (i + 1) * TILE] - line)
-    if keys.shape[0] > 2 * TILE:
-        pieces.append(score[2 * TILE :] - jnp.concatenate(lse, axis=1))
-    prob = jnp.exp2(jnp.concatenate(pieces, axis=0))
-    dscore = (prob * (nt(values, g) - delta)).astype(BF)
-    return nn(dscore, q), nn(prob.astype(BF), g)
+def key_terms(offs, keys, values, q, g, aux, emit):
+    heads = [lanes(h) for h in range(q.shape[1] // HD)]
+    for first in range(0, len(heads), GROUP):
+        group = heads[first : first + GROUP]
+        q_rows = [q[:, cols] for cols in group]
+        g_rows = [g[:, cols] for cols in group]
+        scores = [nt(keys(cols), rows) for cols, rows in zip(group, q_rows)]
+        dprobs = [nt(values(cols), rows) for cols, rows in zip(group, g_rows)]
+        probs, dscores = [], []
+        for cols, score, dprob in zip(group, scores, dprobs):
+            lines = [read_lines(aux, i, cols) for i in range(2)]
+            delta = jnp.concatenate([d for d, _ in lines], axis=1)
+            lse = [l for _, l in lines]
+            score = score * SCALE2
+            pieces = []
+            if offs is not None:
+                for i in range(2):
+                    line = jnp.concatenate([lse[t] + offs[t][i] for t in range(2)], axis=1)
+                    pieces.append(score[i * TILE : (i + 1) * TILE] - line)
+            done = len(pieces) * TILE
+            if score.shape[0] > done:
+                pieces.append(score[done:] - jnp.concatenate(lse, axis=1))
+            prob = jnp.exp2(jnp.concatenate(pieces, axis=0))
+            probs.append(prob.astype(BF))
+            dscores.append((prob * (dprob - delta)).astype(BF))
+        sums_k = [nn(dscore, rows) for dscore, rows in zip(dscores, q_rows)]
+        sums_v = [nn(prob, rows) for prob, rows in zip(probs, g_rows)]
+        for cols, dk, dv in zip(group, sums_k, sums_v):
+            emit(cols, dk, dv)
 
 
 def all_offs(place, lists, slab):
     return [[off_by(place, lists, slab, t, i) for i in range(2)] for t in range(2)]
+
+
+def pair(top, low):
+    return lambda cols: jnp.concatenate([top[:, cols], low[:, cols]], axis=0)
 
 
 def own_kernel(
     place, lists, k, v, sk, sv, q, g, aux, key_acc, value_acc, text_k, text_v
 ):
     frame = k.shape[0]
-    offs = all_offs(place, lists, place[0])
-    for h in range(k.shape[1] // HD):
-        cols = lanes(h)
-        keys = jnp.concatenate([k[:, cols], sk[:, cols]], axis=0)
-        values = jnp.concatenate([v[:, cols], sv[:, cols]], axis=0)
-        dk, dv = key_terms(offs, keys, values, q[:, cols], g[:, cols], aux, cols)
+
+    def emit(cols, dk, dv):
         key_acc[:, cols] = dk[:frame]
         value_acc[:, cols] = dv[:frame]
         text_k[:, cols] = dk[frame:]
         text_v[:, cols] = dv[frame:]
 
-
-def mate_kernel(
-    place, lists, k, v, sk, sv, valid, q, g, aux, key_in, value_in, text_k, text_v,
-    key_acc, value_acc, keep, send,
-):
-    frame, width = k.shape
+    offs = all_offs(place, lists, place[0])
+    key_terms(offs, pair(k, sk), pair(v, sv), q, g, aux, emit)
+
+
+def whole(ref):
+    return lambda cols: ref[:, cols]
+
+
+def text_kernel(sk, sv, valid, q, g, aux, text_k, text_v, keep, send, message):
+    width = q.shape[1]
     half = keep.shape[0]
     live = valid[...] > 0
-    offs = all_offs(place, lists, place[1])
-    for h in range(width // HD):
-        cols = lanes(h)
-        more = slice(width + h * HD, width + (h + 1) * HD)
-        keys = jnp.concatenate([k[:, cols], sk[:, cols]], axis=0)
-        values = jnp.concatenate([v[:, cols], sv[:, cols]], axis=0)
-        dk, dv = key_terms(offs, keys, values, q[:, cols], g[:, cols], aux, cols)
-        key_acc[:, cols] = key_in[:, cols] + dk[:frame]
-        value_acc[:, cols] = value_in[:, cols] + dv[:frame]
-        part_k = jnp.where(live, (text_k[:, cols] + dk[frame:]) * SCALE, 0.0)
-        part_v = jnp.where(live, text_v[:, cols] + dv[frame:], 0.0)
+    message[: g.shape[0], :] = g[...]
+    message[g.shape[0] :, :] = aux[...]
+
+    def emit(cols, dk, dv):
+        more = slice(cols.start + width, cols.stop + width)
+        part_k = jnp.where(live, (text_k[:, cols] + dk) * SCALE, 0.0)
+        part_v = jnp.where(live, text_v[:, cols] + dv, 0.0)
         keep[:, cols] = part_k[:half]
         keep[:, more] = part_v[:half]
         send[:, cols] = part_k[half:].astype(BF)
         send[:, more] = part_v[half:].astype(BF)
 
-
-def far_kernel(place, lists, k, v, q, g, aux, key_acc, value_acc, key_out, value_out):
-    offs = all_offs(place, lists, place[3])
-    for h in range(k.shape[1] // HD):
-        cols = lanes(h)
-        dk, dv = key_terms(offs, k[:, cols], v[:, cols], q[:, cols], g[:, cols], aux, cols)
+    key_terms(None, whole(sk), whole(sv), q, g, aux, emit)
+
+
+def mate_kernel(place, lists, k, v, q, g, aux, key_in, value_in, key_acc, value_acc):
+    def emit(cols, dk, dv):
+        key_acc[:, cols] = key_in[:, cols] + dk
+        value_acc[:, cols] = value_in[:, cols] + dv
+
+    key_terms(all_offs(place, lists, place[1]), whole(k), whole(v), q, g, aux, emit)
+
+
+def far_kernel(place, lists, k, v, q, message, key_acc, value_acc, key_out, value_out):
+    rows = q.shape[0]
+    g, aux = message.at[:rows], message.at[rows:]
+
+    def emit(cols, dk, dv):
         key_out[:, cols] = ((key_acc[:, cols] + dk) * SCALE).astype(BF)
         value_out[:, cols] = (value_acc[:, cols] + dv).astype(BF)
+
+    key_terms(all_offs(place, lists, place[3]), whole(k), whole(v), q, g, aux, emit)
+
+
+def add_kernel(keep, arrived, more, send):
+    rows = more.shape[0]
+    more[...] = keep[:rows, :] + arrived[:rows, :].astype(F32)
+    send[...] = (keep[rows:, :] + arrived[rows:, :].astype(F32)).astype(BF)
+
+
+def finish_kernel(keep, arrived, key_out, value_out):
+    width = key_out.shape[1]
+    total = (keep[...] + arrived[...].astype(F32)).astype(BF)
+    key_out[...] = total[:, :width]
+    value_out[...] = total[:, width:]
 
 
 VMEM = pl.BlockSpec(memory_space=pltpu.VMEM)
@@ -269,6 +319,7 @@
     both = ("seq", "rep")
     seqs, reps, ranks = lax.axis_size("seq"), lax.axis_size("rep"), lax.axis_size("head")
     groups = seqs * reps
+    lists = mask_lists.T
     slab = lax.axis_index(both)
     mate = slab ^ 1
     other = jnp.where(slab & 1, slab + 1, slab - 1)
@@ -294,7 +345,8 @@
         1,
         (place, text_owner.reshape(1, text_count), text_keys, text_values),
     )
-    part_a, part_b = [grad_output[:TILE]], [grad_output[TILE:]]
+    start_a, late_grad = together(grad_output[:TILE], grad_output)
+    part_a, part_b = [start_a], [late_grad[TILE:]]
     mate_v, mate_k, mate_q = swap(values), swap(keys), swap(queries)
     part_a.append(ring(part_a[0]))
     part_b.append(ring(part_b[0]))
@@ -314,16 +366,24 @@
     part_a[-1], mate_v, mate_k = together(part_a[-1], mate_v, mate_k)
     far_v, far_k = relay(mate_v), relay(mate_k)
 
+    second = call(
+        functools.partial(second_kernel, ranks - 2),
+        "second_blocks",
+        sds((frame, width), F32),
+        1,
+        (place, part_a[-2], part_b[-2], out_weight, first),
+    )
     grad = call(
         functools.partial(last_kernel, ranks - 1),
         "grad_heads",
         sds((frame, width), BF),
         1,
-        (place, *part_a[-2:], *part_b[-2:], out_weight, first),
+        (place, part_a[-1], part_b[-1], out_weight, second),
     )
     late_grad, mate_q = together(grad, mate_q)
     mate_g = swap(late_grad)
     far_q = relay(mate_q)
+    far_k, sk = together(far_k, sk)
     wide = pltpu.VMEM((3 * frame, width), BF)
     aux, dscores = call(
         softmax_kernel,
@@ -331,13 +391,12 @@
         (sds((2 * AUX, width), BF), sds((2 * (3 * TILE + text_count), width), BF)),
         2,
         (
-            place, mask_lists, queries, keys, mate_k, far_k, values, mate_v, far_v,
+            place, lists, queries, keys, mate_k, far_k, values, mate_v, far_v,
             text_keys, text_values, grad,
         ),
         (wide, wide),
     )
     mate_aux = swap(aux)
-    far_g, far_aux = relay(mate_g), relay(mate_aux)
     own_aux, far_q = together(aux, far_q)
     acc = sds((frame, width), F32)
     text_acc = sds((slots, width), F32)
@@ -346,21 +405,34 @@
         "own_keys",
         (acc, acc, text_acc, text_acc),
         2,
-        (place, mask_lists, keys, values, sk, sv, queries, grad, own_aux),
-    )
-    key_acc, value_acc, keep, send = call(
+        (place, lists, keys, values, sk, sv, queries, grad, own_aux),
+    )
+    key_acc, value_acc, text_k, text_v = accs
+    keep, send, message = call(
+        text_kernel,
+        "text_slots",
+        (
+            sds((slots // 2, 2 * width), F32),
+            sds((slots // 2, 2 * width), BF),
+            sds((frame + 2 * AUX, width), BF),
+        ),
+        0,
+        (sk, sv, valid, mate_q, mate_g, mate_aux, text_k, text_v),
+    )
+    far_message = relay(message)
+    key_acc, value_acc = call(
         mate_kernel,
         "mate_keys",
-        (acc, acc, sds((slots // 2, 2 * width), F32), sds((slots // 2, 2 * width), BF)),
+        (acc, acc),
         2,
-        (place, mask_lists, keys, values, sk, sv, valid, mate_q, mate_g, mate_aux, *accs),
+        (place, lists, keys, values, mate_q, mate_g, mate_aux, key_acc, value_acc),
     )
     query_grads = call(
         query_kernel,
         "query_grads",
         sds((frame, width), BF),
         2,
-        (place, mask_lists, keys, mate_k, far_k, text_keys, dscores),
+        (place, lists, keys, mate_k, far_k, text_keys, dscores),
         (wide,),
     )
     key_grads, value_grads = call(
@@ -368,7 +440,7 @@
         "far_keys",
         (sds((frame, width), BF),) * 2,
         2,
-        (place, mask_lists, keys, values, far_q, far_g, far_aux, key_acc, value_acc),
+        (place, lists, keys, values, far_q, far_message, key_acc, value_acc),
     )
     stages = []
     distance = 2
@@ -376,12 +448,20 @@
         stages.append(distance)
         distance *= 2
     for i, d in enumerate(stages):
-        total = keep + swap(send, d).astype(F32)
+        arrived = swap(send, d)
+        rows = keep.shape[0] // 2
         if i + 1 < len(stages):
-            rows = total.shape[0] // 2
-            keep, send = total[:rows], total[rows:].astype(BF)
-    total = total.astype(BF)
-    return query_grads, key_grads, value_grads, total[:, :width], total[:, width:]
+            keep, send = call(
+                add_kernel,
+                f"add_slots_{i}",
+                (sds((rows, 2 * width), F32), sds((rows, 2 * width), BF)),
+                0,
+                (keep, arrived),
+            )
+    text_key_grads, text_value_grads = call(
+        finish_kernel, "finish_slots", (sds((2 * rows, width), BF),) * 2, 0, (keep, arrived)
+    )
+    return query_grads, key_grads, value_grads, text_key_grads, text_value_grads
 
 
 def solution(mesh):

time: 69.9 us -> 62.7 us (0.90)
  waiting for transfers between devices: 25.5 us -> 21.5 us
  local copies, waits for them, and re-layouts: 5.82 us -> 4.27 us
  starting transfers between devices: 16.5 us -> 15.8 us
    ppermute x6, waiting for transfers between devices: 15.3 us -> 12.9 us  [ring(): lax.ppermute(x, 'head', [(i, (i + way) % ranks) for i in range(ranks)])]
    unnamed x21 -> x18, local copies, waits for them, and re-layouts: 4.07 us -> 2.39 us
    ppermute x5 -> x4, waiting for transfers between devices: 7.34 us -> 6.44 us  [relay(): return lax.ppermute(x, both, turns)]
    ppermute x7, waiting for transfers between devices: 2.94 us -> 2.08 us  [swap(): return lax.ppermute(x, both, [(i, i ^ distance) for i in range(groups)])]
    pallas_call x8 -> x12, Pallas kernels: 20.7 us -> 20.1 us  [call(): pl.pallas_call(kernel, name=name, out_shape=outs, in_specs=[SMEM] * scala...]
    slice x3 -> x2, local copies, waits for them, and re-layouts: 1.76 us -> 1.88 us  [the longest x1 0.94 us: local(): start_a, late_grad = together(grad_output[:TILE], grad_output)]
    ppermute x5 -> x4, starting transfers between devices: 2 us -> 2.06 us  [relay(): return lax.ppermute(x, both, turns)]
  transfers between devices with their start and end apart: 18 -> 17, of which waited for: 11 -> 11; matrix products, arithmetic and copies ran while one was open for 1% -> 2% of each run, Pallas kernels for 26% -> 29%
where the time goes in v4:
time: 62.7 us; the launch traced here: 62.5 us
  waiting for transfers between devices  21.5 us (34%)
  Pallas kernels  20.1 us (32%)
  starting transfers between devices  15.8 us (25%)
  local copies, waits for them, and re-layouts  4.27 us (7%)
  between operations  0.82 us (1%)
    pallas_call x12, Pallas kernels, call(): pl.pallas_call(kernel, name=name, out_shape=outs, in_specs=[SMEM] * scala...  20.1 us
    ppermute x6, waiting for transfers between devices, ring(): lax.ppermute(x, 'head', [(i, (i + way) % ranks) for i in range(ranks)])  12.9 us
    ppermute x7, starting transfers between devices, swap(): return lax.ppermute(x, both, [(i, i ^ distance) for i in range(groups)])  7.34 us
    ppermute x4, waiting for transfers between devices, relay(): return lax.ppermute(x, both, turns)  6.44 us
    ppermute x6, starting transfers between devices, ring(): lax.ppermute(x, 'head', [(i, (i + way) % ranks) for i in range(ranks)])  6.37 us
    unnamed x18, local copies, waits for them, and re-layouts  2.39 us
    ppermute x7, waiting for transfers between devices, swap(): return lax.ppermute(x, both, [(i, i ^ distance) for i in range(groups)])  2.08 us
    ppermute x4, starting transfers between devices, relay(): return lax.ppermute(x, both, turns)  2.06 us
  transfers between devices with their start and end apart: 17, of which 11 were waited for; matrix products, arithmetic and copies ran while one was open for 2% of the time, Pallas kernels for 29%

profile of v4, /device:TPU:0, one launch (start us, length us, event | category | flops | bytes accessed | tf_op | source)
XLA Modules:
  0.0 62.5 jit_solution(17704061732806141407)
XLA Ops:
  1.6 3.1 %collective-permute-start = (bf16[128,768]{1,0:T(8,128)(2,1)S(1)}, bf16[128,768]{1,0:T(8,128)(2,1)S(1)}, u32[]{:S(2)}, u32[]{:S(2)}) collective-permute-start(bf16[128,768]{1,0:T(8,128)(2,1)S(1)} %slice.6.refs_0_), channel_id=1, source_target_pairs={{0,2},{2,4},{4,6},{6,0},{1,3},{3,5},{5,7},{7,1},{8,10},{10,12},{12... | collective-permute-start | bytes 589832 | tf_op jit(solution)/shard_map/ppermute | solution.py:336
  4.7 1.5 %collective-permute-start.2 = (bf16[256,768]{1,0:T(8,128)(2,1)}, bf16[256,768]{1,0:T(8,128)(2,1)S(1)}, u32[]{:S(2)}, u32[]{:S(2)}) collective-permute-start(bf16[256,768]{1,0:T(8,128)(2,1)} %v.5), channel_id=1, source_target_pairs={{0,1},{1,0},{8,9},{9,8},{16,17},{17,16},{24,25},{25,24},{2,3},{3,2... | collective-permute-start | bytes 1179656 | tf_op jit(solution)/shard_map/ppermute | solution.py:329
  7.1 1.6 %collective-permute-start.4 = (bf16[128,768]{1,0:T(8,128)(2,1)S(1)}, bf16[128,768]{1,0:T(8,128)(2,1)S(1)}, u32[]{:S(2)}, u32[]{:S(2)}) collective-permute-start(bf16[128,768]{1,0:T(8,128)(2,1)S(1)} %slice.7.refs_2_), channel_id=1, source_target_pairs={{0,2},{2,4},{4,6},{6,0},{1,3},{3,5},{5,7},{7,1},{8,10},{10,12},{12... | collective-permute-start | bytes 589832 | tf_op jit(solution)/shard_map/ppermute | solution.py:336
  9.3 3.0 %collective-permute-done.refs_1_ = bf16[128,768]{1,0:T(8,128)(2,1)S(1)} collective-permute-done((bf16[128,768]{1,0:T(8,128)(2,1)S(1)}, bf16[128,768]{1,0:T(8,128)(2,1)S(1)}, u32[]{:S(2)}, u32[]{:S(2)}) %collective-permute-start) | collective-permute-done | bytes 196640 | tf_op jit(solution)/shard_map/ppermute | solution.py:336
  12.3 4.0 %collective-permute-done.4.refs_3_ = bf16[128,768]{1,0:T(8,128)(2,1)S(1)} collective-permute-done((bf16[128,768]{1,0:T(8,128)(2,1)S(1)}, bf16[128,768]{1,0:T(8,128)(2,1)S(1)}, u32[]{:S(2)}, u32[]{:S(2)}) %collective-permute-start.4) | collective-permute-done | bytes 196640 | tf_op jit(solution)/shard_map/ppermute | solution.py:336
  16.6 1.6 %collective-permute-start.10 = (bf16[256,768]{1,0:T(8,128)(2,1)}, bf16[256,768]{1,0:T(8,128)(2,1)S(1)}, u32[]{:S(2)}, u32[]{:S(2)}) collective-permute-start(bf16[256,768]{1,0:T(8,128)(2,1)} %q.3), channel_id=1, source_target_pairs={{0,1},{1,0},{8,9},{9,8},{16,17},{17,16},{24,25},{25,24},{2,3},{3,2... | collective-permute-start | bytes 1179656 | tf_op jit(solution)/shard_map/ppermute | solution.py:329
  18.1 2.5 %collective-permute-done.1.a_before = bf16[128,768]{1,0:T(8,128)(2,1)S(1)} collective-permute-done((bf16[128,768]{1,0:T(8,128)(2,1)S(1)}, bf16[128,768]{1,0:T(8,128)(2,1)S(1)}, u32[]{:S(2)}, u32[]{:S(2)}) %collective-permute-start.1) | collective-permute-done | bytes 196640 | tf_op jit(solution)/shard_map/ppermute | solution.py:336
  20.9 2.3 %copy-done = bf16[768,3072]{1,0:T(8,128)(2,1)S(1)} copy-done((bf16[768,3072]{1,0:T(8,128)(2,1)S(1)}, bf16[768,3072]{1,0:T(8,128)(2,1)}, u32[]{:S(2)}) %copy-start) | copy-done | bytes 4718616
  23.2 2.3 %first_blocks.1.first = f32[256,768]{1,0:T(8,128)S(1)} custom-call(s32[4]{0:T(128)S(1)} %pad_add_fusion.place, bf16[128,768]{1,0:T(8,128)(2,1)S(1)} %slice.6.refs_0_, bf16[128,768]{1,0:T(8,128)(2,1)S(1)} %collective-permute-done.refs_1_, bf16[128,768]{1,0:T(8,128)(2,1)S(1)} %slice.7.refs_2_, bf16[128,768]{1,0:T(8,128)(2,1)S(1)} %collective-permute-done.4.refs_3_, ...), custom_call_target="tpu_custom_call" | custom-call | tf_op jit(solution)/shard_map/first_blocks/pallas_call | solution.py:299
  25.8 1.2 %collective-permute-start.9 = (bf16[128,768]{1,0:T(8,128)(2,1)S(1)}, bf16[128,768]{1,0:T(8,128)(2,1)S(1)}, u32[]{:S(2)}, u32[]{:S(2)}) collective-permute-start(bf16[128,768]{1,0:T(8,128)(2,1)S(1)} %collective-permute-done.5.b_before), channel_id=1, source_target_pairs={{0,2},{2,4},{4,6},{6,0},{1,3},{3,5},{5,7},{7,1},{8,10},{10,12},{12... | collective-permute-start | bytes 589832 | tf_op jit(solution)/shard_map/ppermute | solution.py:336
  27.1 2.1 %collective-permute-done.3.a_last = bf16[128,768]{1,0:T(8,128)(2,1)S(1)} collective-permute-done((bf16[128,768]{1,0:T(8,128)(2,1)S(1)}, bf16[128,768]{1,0:T(8,128)(2,1)S(1)}, u32[]{:S(2)}, u32[]{:S(2)}) %collective-permute-start.3) | collective-permute-done | bytes 196640 | tf_op jit(solution)/shard_map/ppermute | solution.py:336
  29.1 1.6 %collective-permute-start.8 = (bf16[256,768]{1,0:T(8,128)(2,1)S(1)}, bf16[256,768]{1,0:T(8,128)(2,1)S(1)}, u32[]{:S(2)}, u32[]{:S(2)}) collective-permute-start(bf16[256,768]{1,0:T(8,128)(2,1)S(1)} %collective-permute-done.2.v1), channel_id=1, source_target_pairs={{0,8},{1,25},{8,16},{9,1},{16,24},{17,9},{24,0},{25,17},{2,10},{3,... | collective-permute-start | bytes 1179656 | tf_op jit(solution)/shard_map/ppermute | solution.py:333
  30.8 1.5 %second_blocks.1.second = f32[256,768]{1,0:T(8,128)S(1)} custom-call(s32[4]{0:T(128)S(1)} %pad_add_fusion.place, bf16[128,768]{1,0:T(8,128)(2,1)S(1)} %collective-permute-done.1.a_before, bf16[128,768]{1,0:T(8,128)(2,1)S(1)} %collective-permute-done.5.b_before, bf16[768,3072]{1,0:T(8,128)(2,1)S(1)} %copy-done.1, f32[256,768]{1,0:T(8,128)S(1)} %first_blocks.1.first), custom_call_target="tpu_custom_call" | custom-call | tf_op jit(solution)/shard_map/second_blocks/pallas_call | solution.py:299
  33.3 1.5 %grad_heads.1.g = bf16[256,768]{1,0:T(8,128)(2,1)S(1)} custom-call(s32[4]{0:T(128)S(1)} %pad_add_fusion.place, bf16[128,768]{1,0:T(8,128)(2,1)S(1)} %collective-permute-done.3.a_last, bf16[128,768]{1,0:T(8,128)(2,1)S(1)} %collective-permute-done.9.b_last, bf16[768,3072]{1,0:T(8,128)(2,1)S(1)} %copy-done.1, f32[256,768]{1,0:T(8,128)S(1)} %second_blocks.1.second), custom_call_target="tpu_custom_call" | custom-call | tf_op jit(solution)/shard_map/grad_heads/pallas_call | solution.py:299
  34.9 1.9 %collective-permute-start.12 = (bf16[256,768]{1,0:T(8,128)(2,1)S(1)}, bf16[256,768]{1,0:T(8,128)(2,1)S(1)}, u32[]{:S(2)}, u32[]{:S(2)}) collective-permute-start(bf16[256,768]{1,0:T(8,128)(2,1)S(1)} %grad_heads.1.g), channel_id=1, source_target_pairs={{0,1},{1,0},{8,9},{9,8},{16,17},{17,16},{24,25},{25,24},{2,3},{3,2... | collective-permute-start | bytes 1179656 | tf_op jit(solution)/shard_map/ppermute | solution.py:329
  37.7 2.8 %collective-permute-done.8.v2 = bf16[256,768]{1,0:T(8,128)(2,1)S(1)} collective-permute-done((bf16[256,768]{1,0:T(8,128)(2,1)S(1)}, bf16[256,768]{1,0:T(8,128)(2,1)S(1)}, u32[]{:S(2)}, u32[]{:S(2)}) %collective-permute-start.8) | collective-permute-done | bytes 393248 | tf_op jit(solution)/shard_map/ppermute | solution.py:333
  40.6 3.3 %softmax.1 = (bf16[32,768]{1,0:T(8,128)(2,1)S(1)}, bf16[1280,768]{1,0:T(8,128)(2,1)S(1)}) custom-call(s32[4]{0:T(128)S(1)} %pad_add_fusion.place, s32[3,16]{1,0:T(4,128)S(1)} %bitcast.6, bf16[256,768]{1,0:T(8,128)(2,1)S(1)} %copy-done.5, bf16[256,768]{1,0:T(8,128)(2,1)S(1)} %copy-done.2, bf16[256,768]{1,0:T(8,128)(2,1)S(1)} %collective-permute-done.6.k1, ...), custom_call_target="tpu_custom_call" | custom-call | tf_op jit(solution)/shard_map/softmax/pallas_call | solution.py:299
  44.8 2.4 %own_keys.1 = (f32[256,768]{1,0:T(8,128)S(1)}, f32[256,768]{1,0:T(8,128)S(1)}, f32[256,768]{1,0:T(8,128)S(1)}, f32[256,768]{1,0:T(8,128)S(1)}) custom-call(s32[4]{0:T(128)S(1)} %pad_add_fusion.place, s32[3,16]{1,0:T(4,128)S(1)} %bitcast.7, bf16[256,768]{1,0:T(8,128)(2,1)S(1)} %copy-done.2, bf16[256,768]{1,0:T(8,128)(2,1)S(1)} %copy-done.3, ...), custom_call_target="tpu_custom_call" | custom-call | tf_op jit(solution)/shard_map/own_keys/pallas_call | solution.py:299
  49.8 1.2 %collective-permute-done.15.arrived = bf16[128,1536]{1,0:T(8,128)(2,1)S(1)} collective-permute-done((bf16[128,1536]{1,0:T(8,128)(2,1)S(1)}, bf16[128,1536]{1,0:T(8,128)(2,1)S(1)}, u32[]{:S(2)}, u32[]{:S(2)}) %collective-permute-start.15) | collective-permute-done | bytes 393248 | tf_op jit(solution)/shard_map/ppermute | solution.py:329
  51.1 1.6 %collective-permute-start.16 = (bf16[64,1536]{1,0:T(8,128)(2,1)S(1)}, bf16[64,1536]{1,0:T(8,128)(2,1)S(1)}, u32[]{:S(2)}, u32[]{:S(2)}) collective-permute-start(bf16[64,1536]{1,0:T(8,128)(2,1)S(1)} %get-tuple-element.74), channel_id=1, source_target_pairs={{0,16},{1,17},{8,24},{9,25},{16,0},{17,1},{24,8},{25,9},{2,18},{3,... | collective-permute-start | bytes 589832 | tf_op jit(solution)/shard_map/ppermute | solution.py:329
  52.6 2.2 %query_grads.1 = bf16[256,768]{1,0:T(8,128)(2,1)} custom-call(s32[4]{0:T(128)S(1)} %pad_add_fusion.place, s32[3,16]{1,0:T(4,128)S(1)} %bitcast.8, bf16[256,768]{1,0:T(8,128)(2,1)S(1)} %copy-done.2, bf16[256,768]{1,0:T(8,128)(2,1)S(1)} %collective-permute-done.6.k1, bf16[256,768]{1,0:T(8,128)(2,1)S(1)} %collective-permute-done.7.k2, ...), custom_call_target="tpu_custom_call" | custom-call | tf_op jit(solution)/shard_map/query_grads/pallas_call | solution.py:299
  54.8 1.6 %mate_keys.1 = (f32[256,768]{1,0:T(8,128)S(1)}, f32[256,768]{1,0:T(8,128)S(1)}) custom-call(s32[4]{0:T(128)S(1)} %pad_add_fusion.place, s32[3,16]{1,0:T(4,128)S(1)} %bitcast.9, bf16[256,768]{1,0:T(8,128)(2,1)S(1)} %copy-done.2, bf16[256,768]{1,0:T(8,128)(2,1)S(1)} %copy-done.3, bf16[256,768]{1,0:T(8,128)(2,1)S(1)} %collective-permute-done.10.q, ...), custom_call_target="tpu_custom_call" | custom-call | tf_op jit(solution)/shard_map/mate_keys/pallas_call | solution.py:299
  56.5 2.8 %collective-permute-done.14.message = bf16[288,768]{1,0:T(8,128)(2,1)S(1)} collective-permute-done((bf16[288,768]{1,0:T(8,128)(2,1)S(1)}, bf16[288,768]{1,0:T(8,128)(2,1)S(1)}, u32[]{:S(2)}, u32[]{:S(2)}) %collective-permute-start.14) | collective-permute-done | bytes 442400 | tf_op jit(solution)/shard_map/ppermute | solution.py:333
  59.3 2.4 %far_keys.1 = (bf16[256,768]{1,0:T(8,128)(2,1)}, bf16[256,768]{1,0:T(8,128)(2,1)}) custom-call(s32[4]{0:T(128)S(1)} %pad_add_fusion.place, s32[3,16]{1,0:T(4,128)S(1)} %bitcast.10, bf16[256,768]{1,0:T(8,128)(2,1)S(1)} %copy-done.2, bf16[256,768]{1,0:T(8,128)(2,1)S(1)} %copy-done.3, bf16[256,768]{1,0:T(8,128)(2,1)S(1)} %collective-permute-done.11.q, ...), custom_call_target="tpu_custom_call" | custom-call | tf_op jit(solution)/shard_map/far_keys/pallas_call | solution.py:299
  (43 shorter events, 9.6 us)
Async XLA Ops:
  1.6 10.7 %collective-permute-start = (bf16[128,768]{1,0:T(8,128)(2,1)S(1)}, bf16[128,768]{1,0:T(8,128)(2,1)S(1)}, u32[]{:S(2)}, u32[]{:S(2)}) collective-permute-start(bf16[128,768]{1,0:T(8,128)(2,1)S(1)} %slice.6.refs_0_), channel_id=1, source_target_pairs={{0,2},{2,4},{4,6},{6,0},{1,3},{3,5},{5,7},{7,1},{8,10},{10,12},{12... | collective-permute-start | bytes 589832 | tf_op jit(solution)/shard_map/ppermute | solution.py:336
  4.7 16.0 %collective-permute-start.2 = (bf16[256,768]{1,0:T(8,128)(2,1)}, bf16[256,768]{1,0:T(8,128)(2,1)S(1)}, u32[]{:S(2)}, u32[]{:S(2)}) collective-permute-start(bf16[256,768]{1,0:T(8,128)(2,1)} %v.5), channel_id=1, source_target_pairs={{0,1},{1,0},{8,9},{9,8},{16,17},{17,16},{24,25},{25,24},{2,3},{3,2... | collective-permute-start | bytes 1179656 | tf_op jit(solution)/shard_map/ppermute | solution.py:329
  7.1 9.2 %collective-permute-start.4 = (bf16[128,768]{1,0:T(8,128)(2,1)S(1)}, bf16[128,768]{1,0:T(8,128)(2,1)S(1)}, u32[]{:S(2)}, u32[]{:S(2)}) collective-permute-start(bf16[128,768]{1,0:T(8,128)(2,1)S(1)} %slice.7.refs_2_), channel_id=1, source_target_pairs={{0,2},{2,4},{4,6},{6,0},{1,3},{3,5},{5,7},{7,1},{8,10},{10,12},{12... | collective-permute-start | bytes 589832 | tf_op jit(solution)/shard_map/ppermute | solution.py:336
  8.7 17.1 %collective-permute-start.6 = (bf16[256,768]{1,0:T(8,128)(2,1)}, bf16[256,768]{1,0:T(8,128)(2,1)S(1)}, u32[]{:S(2)}, u32[]{:S(2)}) collective-permute-start(bf16[256,768]{1,0:T(8,128)(2,1)} %k.5), channel_id=1, source_target_pairs={{0,1},{1,0},{8,9},{9,8},{16,17},{17,16},{24,25},{25,24},{2,3},{3,2... | collective-permute-start | bytes 1179656 | tf_op jit(solution)/shard_map/ppermute | solution.py:329
  12.3 8.4 %collective-permute-start.1 = (bf16[128,768]{1,0:T(8,128)(2,1)S(1)}, bf16[128,768]{1,0:T(8,128)(2,1)S(1)}, u32[]{:S(2)}, u32[]{:S(2)}) collective-permute-start(bf16[128,768]{1,0:T(8,128)(2,1)S(1)} %collective-permute-done.refs_1_), channel_id=1, source_target_pairs={{0,2},{2,4},{4,6},{6,0},{1,3},{3,5},{5,7},{7,1},{8,10},{10,12},{12... | collective-permute-start | bytes 589832 | tf_op jit(solution)/shard_map/ppermute | solution.py:336
  16.3 9.6 %collective-permute-start.5 = (bf16[128,768]{1,0:T(8,128)(2,1)S(1)}, bf16[128,768]{1,0:T(8,128)(2,1)S(1)}, u32[]{:S(2)}, u32[]{:S(2)}) collective-permute-start(bf16[128,768]{1,0:T(8,128)(2,1)S(1)} %collective-permute-done.4.refs_3_), channel_id=1, source_target_pairs={{0,2},{2,4},{4,6},{6,0},{1,3},{3,5},{5,7},{7,1},{8,10},{10,12},{12... | collective-permute-start | bytes 589832 | tf_op jit(solution)/shard_map/ppermute | solution.py:336
  16.6 18.2 %collective-permute-start.10 = (bf16[256,768]{1,0:T(8,128)(2,1)}, bf16[256,768]{1,0:T(8,128)(2,1)S(1)}, u32[]{:S(2)}, u32[]{:S(2)}) collective-permute-start(bf16[256,768]{1,0:T(8,128)(2,1)} %q.3), channel_id=1, source_target_pairs={{0,1},{1,0},{8,9},{9,8},{16,17},{17,16},{24,25},{25,24},{2,3},{3,2... | collective-permute-start | bytes 1179656 | tf_op jit(solution)/shard_map/ppermute | solution.py:329
  20.6 8.5 %collective-permute-start.3 = (bf16[128,768]{1,0:T(8,128)(2,1)S(1)}, bf16[128,768]{1,0:T(8,128)(2,1)S(1)}, u32[]{:S(2)}, u32[]{:S(2)}) collective-permute-start(bf16[128,768]{1,0:T(8,128)(2,1)S(1)} %collective-permute-done.1.a_before), channel_id=1, source_target_pairs={{0,2},{2,4},{4,6},{6,0},{1,3},{3,5},{5,7},{7,1},{8,10},{10,12},{12... | collective-permute-start | bytes 589832 | tf_op jit(solution)/shard_map/ppermute | solution.py:336
  23.2 7.6 %copy-start.1 = (bf16[768,3072]{1,0:T(8,128)(2,1)S(1)}, bf16[768,3072]{1,0:T(8,128)(2,1)}, u32[]{:S(2)}) copy-start(bf16[768,3072]{1,0:T(8,128)(2,1)} %weight.3) | copy-start | bytes 14155780
  25.8 7.5 %collective-permute-start.9 = (bf16[128,768]{1,0:T(8,128)(2,1)S(1)}, bf16[128,768]{1,0:T(8,128)(2,1)S(1)}, u32[]{:S(2)}, u32[]{:S(2)}) collective-permute-start(bf16[128,768]{1,0:T(8,128)(2,1)S(1)} %collective-permute-done.5.b_before), channel_id=1, source_target_pairs={{0,2},{2,4},{4,6},{6,0},{1,3},{3,5},{5,7},{7,1},{8,10},{10,12},{12... | collective-permute-start | bytes 589832 | tf_op jit(solution)/shard_map/ppermute | solution.py:336
  29.1 8.6 %collective-permute-start.7 = (bf16[256,768]{1,0:T(8,128)(2,1)S(1)}, bf16[256,768]{1,0:T(8,128)(2,1)S(1)}, u32[]{:S(2)}, u32[]{:S(2)}) collective-permute-start(bf16[256,768]{1,0:T(8,128)(2,1)S(1)} %collective-permute-done.6.k1), channel_id=1, source_target_pairs={{0,8},{1,25},{8,16},{9,1},{16,24},{17,9},{24,0},{25,17},{2,10},{3,... | collective-permute-start | bytes 1179656 | tf_op jit(solution)/shard_map/ppermute | solution.py:333
  29.1 11.4 %collective-permute-start.8 = (bf16[256,768]{1,0:T(8,128)(2,1)S(1)}, bf16[256,768]{1,0:T(8,128)(2,1)S(1)}, u32[]{:S(2)}, u32[]{:S(2)}) collective-permute-start(bf16[256,768]{1,0:T(8,128)(2,1)S(1)} %collective-permute-done.2.v1), channel_id=1, source_target_pairs={{0,8},{1,25},{8,16},{9,1},{16,24},{17,9},{24,0},{25,17},{2,10},{3,... | collective-permute-start | bytes 1179656 | tf_op jit(solution)/shard_map/ppermute | solution.py:333
  32.2 4.5 %copy-start.4 = (bf16[256,768]{1,0:T(8,128)(2,1)S(1)}, bf16[256,768]{1,0:T(8,128)(2,1)}, u32[]{:S(2)}) copy-start(bf16[256,768]{1,0:T(8,128)(2,1)} %tk.5) | copy-start | bytes 1179652
  32.3 4.5 %copy-start.6 = (bf16[256,768]{1,0:T(8,128)(2,1)S(1)}, bf16[256,768]{1,0:T(8,128)(2,1)}, u32[]{:S(2)}) copy-start(bf16[256,768]{1,0:T(8,128)(2,1)} %tv.3) | copy-start | bytes 1179652
  32.3 8.3 %copy-start.2 = (bf16[256,768]{1,0:T(8,128)(2,1)S(1)}, bf16[256,768]{1,0:T(8,128)(2,1)}, u32[]{:S(2)}) copy-start(bf16[256,768]{1,0:T(8,128)(2,1)} %k.5) | copy-start | bytes 1179652
  32.3 8.3 %copy-start.3 = (bf16[256,768]{1,0:T(8,128)(2,1)S(1)}, bf16[256,768]{1,0:T(8,128)(2,1)}, u32[]{:S(2)}) copy-start(bf16[256,768]{1,0:T(8,128)(2,1)} %v.5) | copy-start | bytes 1179652
  32.3 8.3 %copy-start.5 = (bf16[256,768]{1,0:T(8,128)(2,1)S(1)}, bf16[256,768]{1,0:T(8,128)(2,1)}, u32[]{:S(2)}) copy-start(bf16[256,768]{1,0:T(8,128)(2,1)} %q.3) | copy-start | bytes 1179652
  32.3 8.3 %copy-start.7 = (s32[16,3]{0,1:T(4,128)S(1)}, s32[16,3]{0,1:T(4,128)}, u32[]{:S(2)}) copy-start(s32[16,3]{0,1:T(4,128)} %param.16) | copy-start | bytes 580
  34.8 10.0 %collective-permute-start.11 = (bf16[256,768]{1,0:T(8,128)(2,1)S(1)}, bf16[256,768]{1,0:T(8,128)(2,1)S(1)}, u32[]{:S(2)}, u32[]{:S(2)}) collective-permute-start(bf16[256,768]{1,0:T(8,128)(2,1)S(1)} %collective-permute-done.10.q), channel_id=1, source_target_pairs={{0,8},{1,25},{8,16},{9,1},{16,24},{17,9},{24,0},{25,17},{2,10},{3,... | collective-permute-start | bytes 1179656 | tf_op jit(solution)/shard_map/ppermute | solution.py:333
  34.9 12.4 %collective-permute-start.12 = (bf16[256,768]{1,0:T(8,128)(2,1)S(1)}, bf16[256,768]{1,0:T(8,128)(2,1)S(1)}, u32[]{:S(2)}, u32[]{:S(2)}) collective-permute-start(bf16[256,768]{1,0:T(8,128)(2,1)S(1)} %grad_heads.1.g), channel_id=1, source_target_pairs={{0,1},{1,0},{8,9},{9,8},{16,17},{17,16},{24,25},{25,24},{2,3},{3,2... | collective-permute-start | bytes 1179656 | tf_op jit(solution)/shard_map/ppermute | solution.py:329
  43.9 4.2 %collective-permute-start.13 = (bf16[32,768]{1,0:T(8,128)(2,1)S(1)}, bf16[32,768]{1,0:T(8,128)(2,1)S(1)}, u32[]{:S(2)}, u32[]{:S(2)}) collective-permute-start(bf16[32,768]{1,0:T(8,128)(2,1)S(1)} %get-tuple-element.61.aux), channel_id=1, source_target_pairs={{0,1},{1,0},{8,9},{9,8},{16,17},{17,16},{24,25},{25,24},{2,3},{3,2... | collective-permute-start | bytes 147464 | tf_op jit(solution)/shard_map/ppermute | solution.py:329
  49.2 1.8 %collective-permute-start.15 = (bf16[128,1536]{1,0:T(8,128)(2,1)S(1)}, bf16[128,1536]{1,0:T(8,128)(2,1)S(1)}, u32[]{:S(2)}, u32[]{:S(2)}) collective-permute-start(bf16[128,1536]{1,0:T(8,128)(2,1)S(1)} %get-tuple-element.72), channel_id=1, source_target_pairs={{0,8},{1,9},{8,0},{9,1},{16,24},{17,25},{24,16},{25,17},{2,10},{3,... | collective-permute-start | bytes 1179656 | tf_op jit(solution)/shard_map/ppermute | solution.py:329
  49.4 9.9 %collective-permute-start.14 = (bf16[288,768]{1,0:T(8,128)(2,1)S(1)}, bf16[288,768]{1,0:T(8,128)(2,1)S(1)}, u32[]{:S(2)}, u32[]{:S(2)}) collective-permute-start(bf16[288,768]{1,0:T(8,128)(2,1)S(1)} %get-tuple-element.64), channel_id=1, source_target_pairs={{0,8},{1,25},{8,16},{9,1},{16,24},{17,9},{24,0},{25,17},{2,10},{3,... | collective-permute-start | bytes 1327112 | tf_op jit(solution)/shard_map/ppermute | solution.py:333
  51.1 10.7 %collective-permute-start.16 = (bf16[64,1536]{1,0:T(8,128)(2,1)S(1)}, bf16[64,1536]{1,0:T(8,128)(2,1)S(1)}, u32[]{:S(2)}, u32[]{:S(2)}) collective-permute-start(bf16[64,1536]{1,0:T(8,128)(2,1)S(1)} %get-tuple-element.74), channel_id=1, source_target_pairs={{0,16},{1,17},{8,24},{9,25},{16,0},{17,1},{24,8},{25,9},{2,18},{3,... | collective-permute-start | bytes 589832 | tf_op jit(solution)/shard_map/ppermute | solution.py:329
  (2 other events, 6.8 us)

commit v5 on v4

--- a/solution.py
+++ b/solution.py
@@ -94,7 +94,7 @@
 
 def block_of(place, weight, depth, step):
     ranks = weight.shape[1] // depth
-    source = lax.rem(place[2] - step + ranks, ranks)
+    source = place[4 + lax.rem(place[2] - step + ranks, ranks)]
     return weight[:, pl.ds(pl.multiple_of(source * depth, 128), depth)]
 
 
@@ -117,15 +117,14 @@
         out[rows, :] = first[rows, :] + nt(part[...], block)
 
 
-def last_kernel(step, place, a_last, b_last, weight, second, out):
-    block = block_of(place, weight, a_last.shape[1], step)
-    for chunk, part in enumerate((a_last, b_last)):
-        rows = slice(chunk * TILE, (chunk + 1) * TILE)
-        out[rows, :] = (second[rows, :] + nt(part[...], block)).astype(BF)
+def last_kernel(step, chunk, place, last, weight, second, out):
+    block = block_of(place, weight, last.shape[1], step)
+    rows = slice(chunk * TILE, (chunk + 1) * TILE)
+    out[...] = (second[rows, :] + nt(last[...], block)).astype(BF)
 
 
 def softmax_kernel(
-    place, lists, q, k0, k1, k2, v0, v1, v2, tk, tv, g, aux, dscores, wide_k, wide_v
+    place, lists, q, k0, k1, k2, v0, v1, v2, tk, tv, ga, gb, aux, dscores, wide_k, wide_v
 ):
     stack_tiles((k0, k1, k2), wide_k)
     stack_tiles((v0, v1, v2), wide_v)
@@ -139,7 +138,7 @@
     for first in range(0, len(jobs), PAIRS):
         group = jobs[first : first + PAIRS]
         scores = [nt(gathered(wide_k, tk, at, cols), q[rows, cols]) for _, rows, at, cols in group]
-        dprobs = [nt(gathered(wide_v, tv, at, cols), g[rows, cols]) for _, rows, at, cols in group]
+        dprobs = [nt(gathered(wide_v, tv, at, cols), (ga, gb)[tile][:, cols]) for tile, _, at, cols in group]
         for (tile, _, _, cols), score, dprob in zip(group, scores, dprobs):
             top = jnp.max(score, axis=0, keepdims=True)
             weight = jnp.exp2((score - top) * SCALE2)
@@ -182,12 +181,12 @@
     return jnp.where(found, 0.0, OFF)
 
 
-def key_terms(offs, keys, values, q, g, aux, emit):
+def key_terms(offs, keys, values, q, ga, gb, aux, emit):
     heads = [lanes(h) for h in range(q.shape[1] // HD)]
     for first in range(0, len(heads), GROUP):
         group = heads[first : first + GROUP]
         q_rows = [q[:, cols] for cols in group]
-        g_rows = [g[:, cols] for cols in group]
+        g_rows = [jnp.concatenate([ga[:, cols], gb[:, cols]], axis=0) for cols in group]
         scores = [nt(keys(cols), rows) for cols, rows in zip(group, q_rows)]
         dprobs = [nt(values(cols), rows) for cols, rows in zip(group, g_rows)]
         probs, dscores = [], []
@@ -222,7 +221,7 @@
 
 
 def own_kernel(
-    place, lists, k, v, sk, sv, q, g, aux, key_acc, value_acc, text_k, text_v
+    place, lists, k, v, sk, sv, q, ga, gb, aux, key_acc, value_acc, text_k, text_v
 ):
     frame = k.shape[0]
 
@@ -233,19 +232,19 @@
         text_v[:, cols] = dv[frame:]
 
     offs = all_offs(place, lists, place[0])
-    key_terms(offs, pair(k, sk), pair(v, sv), q, g, aux, emit)
+    key_terms(offs, pair(k, sk), pair(v, sv), q, ga, gb, aux, emit)
 
 
 def whole(ref):
     return lambda cols: ref[:, cols]
 
 
-def text_kernel(sk, sv, valid, q, g, aux, text_k, text_v, keep, send, message):
+def text_kernel(sk, sv, valid, q, ga, gb, aux, text_k, text_v, keep, send, message):
     width = q.shape[1]
     half = keep.shape[0]
     live = valid[...] > 0
-    message[: g.shape[0], :] = g[...]
-    message[g.shape[0] :, :] = aux[...]
+    message[:TILE, :] = gb[...]
+    message[TILE:, :] = aux[...]
 
     def emit(cols, dk, dv):
         more = slice(cols.start + width, cols.stop + width)
@@ -256,26 +255,25 @@
         send[:, cols] = part_k[half:].astype(BF)
         send[:, more] = part_v[half:].astype(BF)
 
-    key_terms(None, whole(sk), whole(sv), q, g, aux, emit)
-
-
-def mate_kernel(place, lists, k, v, q, g, aux, key_in, value_in, key_acc, value_acc):
+    key_terms(None, whole(sk), whole(sv), q, ga, gb, aux, emit)
+
+
+def mate_kernel(place, lists, k, v, q, ga, gb, aux, key_in, value_in, key_acc, value_acc):
     def emit(cols, dk, dv):
         key_acc[:, cols] = key_in[:, cols] + dk
         value_acc[:, cols] = value_in[:, cols] + dv
 
-    key_terms(all_offs(place, lists, place[1]), whole(k), whole(v), q, g, aux, emit)
-
-
-def far_kernel(place, lists, k, v, q, message, key_acc, value_acc, key_out, value_out):
-    rows = q.shape[0]
-    g, aux = message.at[:rows], message.at[rows:]
+    key_terms(all_offs(place, lists, place[1]), whole(k), whole(v), q, ga, gb, aux, emit)
+
+
+def far_kernel(place, lists, k, v, q, ga, message, key_acc, value_acc, key_out, value_out):
+    gb, aux = message.at[:TILE], message.at[TILE:]
 
     def emit(cols, dk, dv):
         key_out[:, cols] = ((key_acc[:, cols] + dk) * SCALE).astype(BF)
         value_out[:, cols] = (value_acc[:, cols] + dv).astype(BF)
 
-    key_terms(all_offs(place, lists, place[3]), whole(k), whole(v), q, g, aux, emit)
+    key_terms(all_offs(place, lists, place[3]), whole(k), whole(v), q, ga, gb, aux, emit)
 
 
 def add_kernel(keep, arrived, more, send):
@@ -323,7 +321,11 @@
     slab = lax.axis_index(both)
     mate = slab ^ 1
     other = jnp.where(slab & 1, slab + 1, slab - 1)
-    place = jnp.stack([slab, mate, lax.axis_index("head"), other]).astype(jnp.int32)
+    order = list(range(0, ranks, 2)) + list(range(1, ranks, 2))[::-1]
+    seat = sum(
+        jnp.where(lax.axis_index("head") == rank, i, 0) for i, rank in enumerate(order)
+    )
+    place = jnp.stack([slab, mate, seat, other, *order]).astype(jnp.int32)
 
     def swap(x, distance=1):
         return lax.ppermute(x, both, [(i, i ^ distance) for i in range(groups)])
@@ -332,8 +334,9 @@
         turns = [(i, (i + 2 - 4 * (i % 2)) % groups) for i in range(groups)]
         return lax.ppermute(x, both, turns)
 
-    def ring(x, way=1):
-        return lax.ppermute(x, "head", [(i, (i + way) % ranks) for i in range(ranks)])
+    def ring(x):
+        turns = [(order[i], order[(i + 1) % ranks]) for i in range(ranks)]
+        return lax.ppermute(x, "head", turns)
 
     capacity = 2 * text_count // groups
     slots = groups // 2 * capacity
@@ -363,7 +366,6 @@
             part_b[-1], mate_k, first = together(part_b[-1], mate_k, first)
         part_a.append(ring(part_a[-1]))
         part_b.append(ring(part_b[-1]))
-    part_a[-1], mate_v, mate_k = together(part_a[-1], mate_v, mate_k)
     far_v, far_k = relay(mate_v), relay(mate_k)
 
     second = call(
@@ -373,17 +375,20 @@
         1,
         (place, part_a[-2], part_b[-2], out_weight, first),
     )
-    grad = call(
-        functools.partial(last_kernel, ranks - 1),
-        "grad_heads",
-        sds((frame, width), BF),
-        1,
-        (place, part_a[-1], part_b[-1], out_weight, second),
-    )
-    late_grad, mate_q = together(grad, mate_q)
-    mate_g = swap(late_grad)
+    grad_a, grad_b = (
+        call(
+            functools.partial(last_kernel, ranks - 1, chunk),
+            f"grad_heads_{chunk}",
+            sds((TILE, width), BF),
+            1,
+            (place, part, out_weight, second),
+        )
+        for chunk, part in enumerate((part_a[-1], part_b[-1]))
+    )
+    late_a, mate_q = together(grad_a, mate_q)
+    mate_a, mate_b = swap(late_a), swap(grad_b)
     far_q = relay(mate_q)
-    far_k, sk = together(far_k, sk)
+    far_k, sk, mate_a = together(far_k, sk, mate_a)
     wide = pltpu.VMEM((3 * frame, width), BF)
     aux, dscores = call(
         softmax_kernel,
@@ -392,12 +397,13 @@
         2,
         (
             place, lists, queries, keys, mate_k, far_k, values, mate_v, far_v,
-            text_keys, text_values, grad,
+            text_keys, text_values, grad_a, grad_b,
         ),
         (wide, wide),
     )
-    mate_aux = swap(aux)
-    own_aux, far_q = together(aux, far_q)
+    late_aux, mate_b = together(aux, mate_b)
+    mate_aux = swap(late_aux)
+    own_aux = aux
     acc = sds((frame, width), F32)
     text_acc = sds((slots, width), F32)
     accs = call(
@@ -405,19 +411,22 @@
         "own_keys",
         (acc, acc, text_acc, text_acc),
         2,
-        (place, lists, keys, values, sk, sv, queries, grad, own_aux),
+        (place, lists, keys, values, sk, sv, queries, grad_a, grad_b, own_aux),
     )
     key_acc, value_acc, text_k, text_v = accs
+    mate_aux, far_q = together(mate_aux, far_q)
+    far_a = relay(mate_a)
+    mate_aux, far_a = together(mate_aux, far_a)
     keep, send, message = call(
         text_kernel,
         "text_slots",
         (
             sds((slots // 2, 2 * width), F32),
             sds((slots // 2, 2 * width), BF),
-            sds((frame + 2 * AUX, width), BF),
+            sds((TILE + 2 * AUX, width), BF),
         ),
         0,
-        (sk, sv, valid, mate_q, mate_g, mate_aux, text_k, text_v),
+        (sk, sv, valid, mate_q, mate_a, mate_b, mate_aux, text_k, text_v),
     )
     far_message = relay(message)
     key_acc, value_acc = call(
@@ -425,7 +434,7 @@
         "mate_keys",
         (acc, acc),
         2,
-        (place, lists, keys, values, mate_q, mate_g, mate_aux, key_acc, value_acc),
+        (place, lists, keys, values, mate_q, mate_a, mate_b, mate_aux, key_acc, value_acc),
     )
     query_grads = call(
         query_kernel,
@@ -440,7 +449,7 @@
         "far_keys",
         (sds((frame, width), BF),) * 2,
         2,
-        (place, lists, keys, values, far_q, far_message, key_acc, value_acc),
+        (place, lists, keys, values, far_q, far_a, far_message, key_acc, value_acc),
     )
     stages = []
     distance = 2

time: 62.7 us -> 60.3 us (0.962)
  waiting for transfers between devices: 21.5 us -> 9.74 us
  starting transfers between devices: 15.8 us -> 24.3 us
  Pallas kernels: 20.1 us -> 20.8 us
    ppermute x6, waiting for transfers between devices: 12.9 us -> 3.07 us  [ring(): return lax.ppermute(x, 'head', turns)]
    ppermute x6, starting transfers between devices: 6.37 us -> 14.8 us  [ring(): return lax.ppermute(x, 'head', turns)]
    ppermute x4 -> x5, waiting for transfers between devices: 6.44 us -> 0.01 us  [relay(): return lax.ppermute(x, both, turns)]
    ppermute x7 -> x8, waiting for transfers between devices: 2.08 us -> 6.66 us  [swap(): return lax.ppermute(x, both, [(i, i ^ distance) for i in range(groups)])]
    pallas_call x12 -> x13, Pallas kernels: 20.1 us -> 20.8 us  [call(): pl.pallas_call(kernel, name=name, out_shape=outs, in_specs=[SMEM] * scala...]
    ppermute x4 -> x5, starting transfers between devices: 2.06 us -> 2.19 us  [relay(): return lax.ppermute(x, both, turns)]
    ppermute x7 -> x8, starting transfers between devices: 7.34 us -> 7.29 us  [swap(): return lax.ppermute(x, both, [(i, i ^ distance) for i in range(groups)])]
  transfers between devices with their start and end apart: 17 -> 19, of which waited for: 11 -> 10; matrix products, arithmetic and copies ran while one was open for 2% -> 2% of each run, Pallas kernels for 29% -> 32%
where the time goes in v5:
time: 60.3 us; the launch traced here: 60.1 us
  starting transfers between devices  24.3 us (40%)
  Pallas kernels  20.8 us (34%)
  waiting for transfers between devices  9.74 us (16%)
  local copies, waits for them, and re-layouts  4.35 us (7%)
  between operations  0.85 us (1%)
    pallas_call x13, Pallas kernels, call(): pl.pallas_call(kernel, name=name, out_shape=outs, in_specs=[SMEM] * scala...  20.8 us
    ppermute x6, starting transfers between devices, ring(): return lax.ppermute(x, 'head', turns)  14.8 us
    ppermute x8, starting transfers between devices, swap(): return lax.ppermute(x, both, [(i, i ^ distance) for i in range(groups)])  7.29 us
    ppermute x8, waiting for transfers between devices, swap(): return lax.ppermute(x, both, [(i, i ^ distance) for i in range(groups)])  6.66 us
    ppermute x6, waiting for transfers between devices, ring(): return lax.ppermute(x, 'head', turns)  3.07 us
    unnamed x18, local copies, waits for them, and re-layouts  2.38 us
    ppermute x5, starting transfers between devices, relay(): return lax.ppermute(x, both, turns)  2.19 us
  transfers between devices with their start and end apart: 19, of which 10 were waited for; matrix products, arithmetic and copies ran while one was open for 2% of the time, Pallas kernels for 32%

profile of v5, /device:TPU:0, one launch (start us, length us, event | category | flops | bytes accessed | tf_op | source)
XLA Modules:
  0.0 60.1 jit_solution(1944383042892124299)
XLA Ops:
  1.6 4.1 %collective-permute-start.3 = (bf16[128,768]{1,0:T(8,128)(2,1)S(1)}, bf16[128,768]{1,0:T(8,128)(2,1)S(1)}, u32[]{:S(2)}, u32[]{:S(2)}) collective-permute-start(bf16[128,768]{1,0:T(8,128)(2,1)S(1)} %slice.6.refs_0_), channel_id=1, source_target_pairs={{0,4},{4,6},{6,2},{2,0},{1,5},{5,7},{7,3},{3,1},{8,12},{12,14},{14... | collective-permute-start | bytes 589832 | tf_op jit(solution)/shard_map/ppermute | solution.py:339
  5.7 1.5 %collective-permute-start.6 = (bf16[256,768]{1,0:T(8,128)(2,1)}, bf16[256,768]{1,0:T(8,128)(2,1)S(1)}, u32[]{:S(2)}, u32[]{:S(2)}) collective-permute-start(bf16[256,768]{1,0:T(8,128)(2,1)} %v.5), channel_id=1, source_target_pairs={{0,1},{1,0},{8,9},{9,8},{16,17},{17,16},{24,25},{25,24},{2,3},{3,2... | collective-permute-start | bytes 1179656 | tf_op jit(solution)/shard_map/ppermute | solution.py:331
  8.1 1.6 %collective-permute-start = (bf16[128,768]{1,0:T(8,128)(2,1)S(1)}, bf16[128,768]{1,0:T(8,128)(2,1)S(1)}, u32[]{:S(2)}, u32[]{:S(2)}) collective-permute-start(bf16[128,768]{1,0:T(8,128)(2,1)S(1)} %slice.7.refs_2_), channel_id=1, source_target_pairs={{0,4},{4,6},{6,2},{2,0},{1,5},{5,7},{7,3},{3,1},{8,12},{12,14},{14... | collective-permute-start | bytes 589832 | tf_op jit(solution)/shard_map/ppermute | solution.py:339
  10.5 3.4 %collective-permute-start.5 = (bf16[128,768]{1,0:T(8,128)(2,1)S(1)}, bf16[128,768]{1,0:T(8,128)(2,1)S(1)}, u32[]{:S(2)}, u32[]{:S(2)}) collective-permute-start(bf16[128,768]{1,0:T(8,128)(2,1)S(1)} %collective-permute-done.3.refs_1_), channel_id=1, source_target_pairs={{0,4},{4,6},{6,2},{2,0},{1,5},{5,7},{7,3},{3,1},{8,12},{12,14},{14... | collective-permute-start | bytes 589832 | tf_op jit(solution)/shard_map/ppermute | solution.py:339
  13.8 2.0 %collective-permute-start.8 = (bf16[256,768]{1,0:T(8,128)(2,1)}, bf16[256,768]{1,0:T(8,128)(2,1)S(1)}, u32[]{:S(2)}, u32[]{:S(2)}) collective-permute-start(bf16[256,768]{1,0:T(8,128)(2,1)} %q.3), channel_id=1, source_target_pairs={{0,1},{1,0},{8,9},{9,8},{16,17},{17,16},{24,25},{25,24},{2,3},{3,2... | collective-permute-start | bytes 1179656 | tf_op jit(solution)/shard_map/ppermute | solution.py:331
  16.0 2.5 %collective-permute-start.1 = (bf16[128,768]{1,0:T(8,128)(2,1)S(1)}, bf16[128,768]{1,0:T(8,128)(2,1)S(1)}, u32[]{:S(2)}, u32[]{:S(2)}) collective-permute-start(bf16[128,768]{1,0:T(8,128)(2,1)S(1)} %collective-permute-done.refs_3_), channel_id=1, source_target_pairs={{0,4},{4,6},{6,2},{2,0},{1,5},{5,7},{7,3},{3,1},{8,12},{12,14},{14... | collective-permute-start | bytes 589832 | tf_op jit(solution)/shard_map/ppermute | solution.py:339
  18.6 1.7 %collective-permute-done.5.a_before = bf16[128,768]{1,0:T(8,128)(2,1)S(1)} collective-permute-done((bf16[128,768]{1,0:T(8,128)(2,1)S(1)}, bf16[128,768]{1,0:T(8,128)(2,1)S(1)}, u32[]{:S(2)}, u32[]{:S(2)}) %collective-permute-start.5) | collective-permute-done | bytes 196640 | tf_op jit(solution)/shard_map/ppermute | solution.py:339
  20.2 2.5 %collective-permute-start.7 = (bf16[128,768]{1,0:T(8,128)(2,1)S(1)}, bf16[128,768]{1,0:T(8,128)(2,1)S(1)}, u32[]{:S(2)}, u32[]{:S(2)}) collective-permute-start(bf16[128,768]{1,0:T(8,128)(2,1)S(1)} %collective-permute-done.5.a_before), channel_id=1, source_target_pairs={{0,4},{4,6},{6,2},{2,0},{1,5},{5,7},{7,3},{3,1},{8,12},{12,14},{14... | collective-permute-start | bytes 589832 | tf_op jit(solution)/shard_map/ppermute | solution.py:339
  22.7 2.3 %copy-done = bf16[768,3072]{1,0:T(8,128)(2,1)S(1)} copy-done((bf16[768,3072]{1,0:T(8,128)(2,1)S(1)}, bf16[768,3072]{1,0:T(8,128)(2,1)}, u32[]{:S(2)}) %copy-start) | copy-done | bytes 4718616
  25.0 2.2 %first_blocks.1.first = f32[256,768]{1,0:T(8,128)S(1)} custom-call(s32[8]{0:T(128)S(1)} %stack.19.place, bf16[128,768]{1,0:T(8,128)(2,1)S(1)} %slice.6.refs_0_, bf16[128,768]{1,0:T(8,128)(2,1)S(1)} %collective-permute-done.3.refs_1_, bf16[128,768]{1,0:T(8,128)(2,1)S(1)} %slice.7.refs_2_, bf16[128,768]{1,0:T(8,128)(2,1)S(1)} %collective-permute-done.refs_3_, ...), custom_call_target="tpu_custom_call" | custom-call | tf_op jit(solution)/shard_map/first_blocks/pallas_call | solution.py:297
  27.4 1.6 %collective-permute-start.10 = (bf16[256,768]{1,0:T(8,128)(2,1)S(1)}, bf16[256,768]{1,0:T(8,128)(2,1)S(1)}, u32[]{:S(2)}, u32[]{:S(2)}) collective-permute-start(bf16[256,768]{1,0:T(8,128)(2,1)S(1)} %collective-permute-done.6.v1), channel_id=1, source_target_pairs={{0,8},{1,25},{8,16},{9,1},{16,24},{17,9},{24,0},{25,17},{2,10},{3,... | collective-permute-start | bytes 1179656 | tf_op jit(solution)/shard_map/ppermute | solution.py:335
  29.8 1.5 %second_blocks.1.second = f32[256,768]{1,0:T(8,128)S(1)} custom-call(s32[8]{0:T(128)S(1)} %stack.19.place, bf16[128,768]{1,0:T(8,128)(2,1)S(1)} %collective-permute-done.5.a_before, bf16[128,768]{1,0:T(8,128)(2,1)S(1)} %collective-permute-done.1.b_before, bf16[768,3072]{1,0:T(8,128)(2,1)S(1)} %copy-done.1, f32[256,768]{1,0:T(8,128)S(1)} %first_blocks.1.first), custom_call_target="tpu_custom_call" | custom-call | tf_op jit(solution)/shard_map/second_blocks/pallas_call | solution.py:297
  31.3 1.1 %grad_heads_0.1.ga = bf16[128,768]{1,0:T(8,128)(2,1)S(1)} custom-call(s32[8]{0:T(128)S(1)} %stack.19.place, bf16[128,768]{1,0:T(8,128)(2,1)S(1)} %collective-permute-done.7.last, bf16[768,3072]{1,0:T(8,128)(2,1)S(1)} %copy-done.1, f32[256,768]{1,0:T(8,128)S(1)} %second_blocks.1.second), custom_call_target="tpu_custom_call" | custom-call | tf_op jit(solution)/shard_map/grad_heads_0/pallas_call | solution.py:297
  33.3 1.5 %collective-permute-start.9 = (bf16[128,768]{1,0:T(8,128)(2,1)S(1)}, bf16[128,768]{1,0:T(8,128)(2,1)S(1)}, u32[]{:S(2)}, u32[]{:S(2)}) collective-permute-start(bf16[128,768]{1,0:T(8,128)(2,1)S(1)} %grad_heads_0.1.ga), channel_id=1, source_target_pairs={{0,1},{1,0},{8,9},{9,8},{16,17},{17,16},{24,25},{25,24},{2,3},{3,2... | collective-permute-start | bytes 589832 | tf_op jit(solution)/shard_map/ppermute | solution.py:331
  35.9 1.1 %grad_heads_1.1.gb = bf16[128,768]{1,0:T(8,128)(2,1)S(1)} custom-call(s32[8]{0:T(128)S(1)} %stack.19.place, bf16[128,768]{1,0:T(8,128)(2,1)S(1)} %collective-permute-done.11.last, bf16[768,3072]{1,0:T(8,128)(2,1)S(1)} %copy-done.1, f32[256,768]{1,0:T(8,128)S(1)} %second_blocks.1.second), custom_call_target="tpu_custom_call" | custom-call | tf_op jit(solution)/shard_map/grad_heads_1/pallas_call | solution.py:297
  39.1 3.3 %softmax.1 = (bf16[32,768]{1,0:T(8,128)(2,1)S(1)}, bf16[1280,768]{1,0:T(8,128)(2,1)S(1)}) custom-call(s32[8]{0:T(128)S(1)} %stack.19.place, s32[3,16]{1,0:T(4,128)S(1)} %bitcast.6, bf16[256,768]{1,0:T(8,128)(2,1)S(1)} %copy-done.5, bf16[256,768]{1,0:T(8,128)(2,1)S(1)} %copy-done.2, bf16[256,768]{1,0:T(8,128)(2,1)S(1)} %collective-permute-done.2.k1, ...), custom_call_target="tpu_custom_call" | custom-call | tf_op jit(solution)/shard_map/softmax/pallas_call | solution.py:297
  42.5 1.9 %collective-permute-done.12.gb = bf16[128,768]{1,0:T(8,128)(2,1)S(1)} collective-permute-done((bf16[128,768]{1,0:T(8,128)(2,1)S(1)}, bf16[128,768]{1,0:T(8,128)(2,1)S(1)}, u32[]{:S(2)}, u32[]{:S(2)}) %collective-permute-start.12) | collective-permute-done | bytes 196640 | tf_op jit(solution)/shard_map/ppermute | solution.py:331
  44.7 2.5 %own_keys.1 = (f32[256,768]{1,0:T(8,128)S(1)}, f32[256,768]{1,0:T(8,128)S(1)}, f32[256,768]{1,0:T(8,128)S(1)}, f32[256,768]{1,0:T(8,128)S(1)}) custom-call(s32[8]{0:T(128)S(1)} %stack.19.place, s32[3,16]{1,0:T(4,128)S(1)} %bitcast.7, bf16[256,768]{1,0:T(8,128)(2,1)S(1)} %copy-done.2, bf16[256,768]{1,0:T(8,128)(2,1)S(1)} %copy-done.3, ...), custom_call_target="tpu_custom_call" | custom-call | tf_op jit(solution)/shard_map/own_keys/pallas_call | solution.py:297
  47.1 1.4 %collective-permute-done.13.aux = bf16[32,768]{1,0:T(8,128)(2,1)S(1)} collective-permute-done((bf16[32,768]{1,0:T(8,128)(2,1)S(1)}, bf16[32,768]{1,0:T(8,128)(2,1)S(1)}, u32[]{:S(2)}, u32[]{:S(2)}) %collective-permute-start.13) | collective-permute-done | bytes 49184 | tf_op jit(solution)/shard_map/ppermute | solution.py:331
  48.5 1.1 %text_slots.1 = (f32[128,1536]{1,0:T(8,128)S(1)}, bf16[128,1536]{1,0:T(8,128)(2,1)S(1)}, bf16[160,768]{1,0:T(8,128)(2,1)S(1)}) custom-call(bf16[256,768]{1,0:T(8,128)(2,1)S(1)} %get-tuple-element.61.sk, bf16[256,768]{1,0:T(8,128)(2,1)S(1)} %get-tuple-element.62.sv, f32[256,128]{1,0:T(8,128)S(1)} %get-tuple-element.63.valid, ...), custom_call_target="tpu_custom_call" | custom-call | tf_op jit(solution)/shard_map/text_slots/pallas_call | solution.py:297
  50.2 1.2 %collective-permute-done.17.arrived = bf16[128,1536]{1,0:T(8,128)(2,1)S(1)} collective-permute-done((bf16[128,1536]{1,0:T(8,128)(2,1)S(1)}, bf16[128,1536]{1,0:T(8,128)(2,1)S(1)}, u32[]{:S(2)}, u32[]{:S(2)}) %collective-permute-start.17) | collective-permute-done | bytes 393248 | tf_op jit(solution)/shard_map/ppermute | solution.py:331
  52.1 2.2 %query_grads.1 = bf16[256,768]{1,0:T(8,128)(2,1)} custom-call(s32[8]{0:T(128)S(1)} %stack.19.place, s32[3,16]{1,0:T(4,128)S(1)} %bitcast.8, bf16[256,768]{1,0:T(8,128)(2,1)S(1)} %copy-done.2, bf16[256,768]{1,0:T(8,128)(2,1)S(1)} %collective-permute-done.2.k1, bf16[256,768]{1,0:T(8,128)(2,1)S(1)} %collective-permute-done.4.k2, ...), custom_call_target="tpu_custom_call" | custom-call | tf_op jit(solution)/shard_map/query_grads/pallas_call | solution.py:297
  54.3 1.7 %mate_keys.1 = (f32[256,768]{1,0:T(8,128)S(1)}, f32[256,768]{1,0:T(8,128)S(1)}) custom-call(s32[8]{0:T(128)S(1)} %stack.19.place, s32[3,16]{1,0:T(4,128)S(1)} %bitcast.9, bf16[256,768]{1,0:T(8,128)(2,1)S(1)} %copy-done.2, bf16[256,768]{1,0:T(8,128)(2,1)S(1)} %copy-done.3, bf16[256,768]{1,0:T(8,128)(2,1)S(1)} %collective-permute-done.8.q, ...), custom_call_target="tpu_custom_call" | custom-call | tf_op jit(solution)/shard_map/mate_keys/pallas_call | solution.py:297
  55.9 2.4 %far_keys.1 = (bf16[256,768]{1,0:T(8,128)(2,1)}, bf16[256,768]{1,0:T(8,128)(2,1)}) custom-call(s32[8]{0:T(128)S(1)} %stack.19.place, s32[3,16]{1,0:T(4,128)S(1)} %bitcast.10, bf16[256,768]{1,0:T(8,128)(2,1)S(1)} %copy-done.2, bf16[256,768]{1,0:T(8,128)(2,1)S(1)} %copy-done.3, bf16[256,768]{1,0:T(8,128)(2,1)S(1)} %collective-permute-done.14.q, ...), custom_call_target="tpu_custom_call" | custom-call | tf_op jit(solution)/shard_map/far_keys/pallas_call | solution.py:297
  (48 shorter events, 11.1 us)
Async XLA Ops:
  1.6 8.9 %collective-permute-start.3 = (bf16[128,768]{1,0:T(8,128)(2,1)S(1)}, bf16[128,768]{1,0:T(8,128)(2,1)S(1)}, u32[]{:S(2)}, u32[]{:S(2)}) collective-permute-start(bf16[128,768]{1,0:T(8,128)(2,1)S(1)} %slice.6.refs_0_), channel_id=1, source_target_pairs={{0,4},{4,6},{6,2},{2,0},{1,5},{5,7},{7,3},{3,1},{8,12},{12,14},{14... | collective-permute-start | bytes 589832 | tf_op jit(solution)/shard_map/ppermute | solution.py:339
  5.7 14.5 %collective-permute-start.6 = (bf16[256,768]{1,0:T(8,128)(2,1)}, bf16[256,768]{1,0:T(8,128)(2,1)S(1)}, u32[]{:S(2)}, u32[]{:S(2)}) collective-permute-start(bf16[256,768]{1,0:T(8,128)(2,1)} %v.5), channel_id=1, source_target_pairs={{0,1},{1,0},{8,9},{9,8},{16,17},{17,16},{24,25},{25,24},{2,3},{3,2... | collective-permute-start | bytes 1179656 | tf_op jit(solution)/shard_map/ppermute | solution.py:331
  8.1 7.9 %collective-permute-start = (bf16[128,768]{1,0:T(8,128)(2,1)S(1)}, bf16[128,768]{1,0:T(8,128)(2,1)S(1)}, u32[]{:S(2)}, u32[]{:S(2)}) collective-permute-start(bf16[128,768]{1,0:T(8,128)(2,1)S(1)} %slice.7.refs_2_), channel_id=1, source_target_pairs={{0,4},{4,6},{6,2},{2,0},{1,5},{5,7},{7,3},{3,1},{8,12},{12,14},{14... | collective-permute-start | bytes 589832 | tf_op jit(solution)/shard_map/ppermute | solution.py:339
  9.7 17.6 %collective-permute-start.2 = (bf16[256,768]{1,0:T(8,128)(2,1)}, bf16[256,768]{1,0:T(8,128)(2,1)S(1)}, u32[]{:S(2)}, u32[]{:S(2)}) collective-permute-start(bf16[256,768]{1,0:T(8,128)(2,1)} %k.5), channel_id=1, source_target_pairs={{0,1},{1,0},{8,9},{9,8},{16,17},{17,16},{24,25},{25,24},{2,3},{3,2... | collective-permute-start | bytes 1179656 | tf_op jit(solution)/shard_map/ppermute | solution.py:331
  10.5 9.7 %collective-permute-start.5 = (bf16[128,768]{1,0:T(8,128)(2,1)S(1)}, bf16[128,768]{1,0:T(8,128)(2,1)S(1)}, u32[]{:S(2)}, u32[]{:S(2)}) collective-permute-start(bf16[128,768]{1,0:T(8,128)(2,1)S(1)} %collective-permute-done.3.refs_1_), channel_id=1, source_target_pairs={{0,4},{4,6},{6,2},{2,0},{1,5},{5,7},{7,3},{3,1},{8,12},{12,14},{14... | collective-permute-start | bytes 589832 | tf_op jit(solution)/shard_map/ppermute | solution.py:339
  13.8 19.5 %collective-permute-start.8 = (bf16[256,768]{1,0:T(8,128)(2,1)}, bf16[256,768]{1,0:T(8,128)(2,1)S(1)}, u32[]{:S(2)}, u32[]{:S(2)}) collective-permute-start(bf16[256,768]{1,0:T(8,128)(2,1)} %q.3), channel_id=1, source_target_pairs={{0,1},{1,0},{8,9},{9,8},{16,17},{17,16},{24,25},{25,24},{2,3},{3,2... | collective-permute-start | bytes 1179656 | tf_op jit(solution)/shard_map/ppermute | solution.py:331
  16.0 11.3 %collective-permute-start.1 = (bf16[128,768]{1,0:T(8,128)(2,1)S(1)}, bf16[128,768]{1,0:T(8,128)(2,1)S(1)}, u32[]{:S(2)}, u32[]{:S(2)}) collective-permute-start(bf16[128,768]{1,0:T(8,128)(2,1)S(1)} %collective-permute-done.refs_3_), channel_id=1, source_target_pairs={{0,4},{4,6},{6,2},{2,0},{1,5},{5,7},{7,3},{3,1},{8,12},{12,14},{14... | collective-permute-start | bytes 589832 | tf_op jit(solution)/shard_map/ppermute | solution.py:339
  20.2 11.1 %collective-permute-start.7 = (bf16[128,768]{1,0:T(8,128)(2,1)S(1)}, bf16[128,768]{1,0:T(8,128)(2,1)S(1)}, u32[]{:S(2)}, u32[]{:S(2)}) collective-permute-start(bf16[128,768]{1,0:T(8,128)(2,1)S(1)} %collective-permute-done.5.a_before), channel_id=1, source_target_pairs={{0,4},{4,6},{6,2},{2,0},{1,5},{5,7},{7,3},{3,1},{8,12},{12,14},{14... | collective-permute-start | bytes 589832 | tf_op jit(solution)/shard_map/ppermute | solution.py:339
  27.3 11.8 %collective-permute-start.4 = (bf16[256,768]{1,0:T(8,128)(2,1)S(1)}, bf16[256,768]{1,0:T(8,128)(2,1)S(1)}, u32[]{:S(2)}, u32[]{:S(2)}) collective-permute-start(bf16[256,768]{1,0:T(8,128)(2,1)S(1)} %collective-permute-done.2.k1), channel_id=1, source_target_pairs={{0,8},{1,25},{8,16},{9,1},{16,24},{17,9},{24,0},{25,17},{2,10},{3,... | collective-permute-start | bytes 1179656 | tf_op jit(solution)/shard_map/ppermute | solution.py:335
  27.4 11.7 %collective-permute-start.10 = (bf16[256,768]{1,0:T(8,128)(2,1)S(1)}, bf16[256,768]{1,0:T(8,128)(2,1)S(1)}, u32[]{:S(2)}, u32[]{:S(2)}) collective-permute-start(bf16[256,768]{1,0:T(8,128)(2,1)S(1)} %collective-permute-done.6.v1), channel_id=1, source_target_pairs={{0,8},{1,25},{8,16},{9,1},{16,24},{17,9},{24,0},{25,17},{2,10},{3,... | collective-permute-start | bytes 1179656 | tf_op jit(solution)/shard_map/ppermute | solution.py:335
  29.0 6.9 %collective-permute-start.11 = (bf16[128,768]{1,0:T(8,128)(2,1)S(1)}, bf16[128,768]{1,0:T(8,128)(2,1)S(1)}, u32[]{:S(2)}, u32[]{:S(2)}) collective-permute-start(bf16[128,768]{1,0:T(8,128)(2,1)S(1)} %collective-permute-done.1.b_before), channel_id=1, source_target_pairs={{0,4},{4,6},{6,2},{2,0},{1,5},{5,7},{7,3},{3,1},{8,12},{12,14},{14... | collective-permute-start | bytes 589832 | tf_op jit(solution)/shard_map/ppermute | solution.py:339
  31.2 6.6 %copy-start.4 = (bf16[256,768]{1,0:T(8,128)(2,1)S(1)}, bf16[256,768]{1,0:T(8,128)(2,1)}, u32[]{:S(2)}) copy-start(bf16[256,768]{1,0:T(8,128)(2,1)} %tk.5) | copy-start | bytes 1179652
  32.4 6.7 %copy-start.2 = (bf16[256,768]{1,0:T(8,128)(2,1)S(1)}, bf16[256,768]{1,0:T(8,128)(2,1)}, u32[]{:S(2)}) copy-start(bf16[256,768]{1,0:T(8,128)(2,1)} %k.5) | copy-start | bytes 1179652
  32.4 6.7 %copy-start.3 = (bf16[256,768]{1,0:T(8,128)(2,1)S(1)}, bf16[256,768]{1,0:T(8,128)(2,1)}, u32[]{:S(2)}) copy-start(bf16[256,768]{1,0:T(8,128)(2,1)} %v.5) | copy-start | bytes 1179652
  32.4 6.7 %copy-start.5 = (bf16[256,768]{1,0:T(8,128)(2,1)S(1)}, bf16[256,768]{1,0:T(8,128)(2,1)}, u32[]{:S(2)}) copy-start(bf16[256,768]{1,0:T(8,128)(2,1)} %q.3) | copy-start | bytes 1179652
  32.4 6.7 %copy-start.7 = (s32[16,3]{0,1:T(4,128)S(1)}, s32[16,3]{0,1:T(4,128)}, u32[]{:S(2)}) copy-start(s32[16,3]{0,1:T(4,128)} %param.16) | copy-start | bytes 580
  33.3 5.8 %collective-permute-start.9 = (bf16[128,768]{1,0:T(8,128)(2,1)S(1)}, bf16[128,768]{1,0:T(8,128)(2,1)S(1)}, u32[]{:S(2)}, u32[]{:S(2)}) collective-permute-start(bf16[128,768]{1,0:T(8,128)(2,1)S(1)} %grad_heads_0.1.ga), channel_id=1, source_target_pairs={{0,1},{1,0},{8,9},{9,8},{16,17},{17,16},{24,25},{25,24},{2,3},{3,2... | collective-permute-start | bytes 589832 | tf_op jit(solution)/shard_map/ppermute | solution.py:331
  34.8 13.7 %collective-permute-start.14 = (bf16[256,768]{1,0:T(8,128)(2,1)S(1)}, bf16[256,768]{1,0:T(8,128)(2,1)S(1)}, u32[]{:S(2)}, u32[]{:S(2)}) collective-permute-start(bf16[256,768]{1,0:T(8,128)(2,1)S(1)} %collective-permute-done.8.q), channel_id=1, source_target_pairs={{0,8},{1,25},{8,16},{9,1},{16,24},{17,9},{24,0},{25,17},{2,10},{3,... | collective-permute-start | bytes 1179656 | tf_op jit(solution)/shard_map/ppermute | solution.py:335
  36.9 7.4 %collective-permute-start.12 = (bf16[128,768]{1,0:T(8,128)(2,1)S(1)}, bf16[128,768]{1,0:T(8,128)(2,1)S(1)}, u32[]{:S(2)}, u32[]{:S(2)}) collective-permute-start(bf16[128,768]{1,0:T(8,128)(2,1)S(1)} %grad_heads_1.1.gb), channel_id=1, source_target_pairs={{0,1},{1,0},{8,9},{9,8},{16,17},{17,16},{24,25},{25,24},{2,3},{3,2... | collective-permute-start | bytes 589832 | tf_op jit(solution)/shard_map/ppermute | solution.py:331
  39.1 9.4 %collective-permute-start.15 = (bf16[128,768]{1,0:T(8,128)(2,1)S(1)}, bf16[128,768]{1,0:T(8,128)(2,1)S(1)}, u32[]{:S(2)}, u32[]{:S(2)}) collective-permute-start(bf16[128,768]{1,0:T(8,128)(2,1)S(1)} %collective-permute-done.9.ga), channel_id=1, source_target_pairs={{0,8},{1,25},{8,16},{9,1},{16,24},{17,9},{24,0},{25,17},{2,10},{3,... | collective-permute-start | bytes 589832 | tf_op jit(solution)/shard_map/ppermute | solution.py:335
  44.4 4.1 %collective-permute-start.13 = (bf16[32,768]{1,0:T(8,128)(2,1)S(1)}, bf16[32,768]{1,0:T(8,128)(2,1)S(1)}, u32[]{:S(2)}, u32[]{:S(2)}) collective-permute-start(bf16[32,768]{1,0:T(8,128)(2,1)S(1)} %get-tuple-element.55.aux), channel_id=1, source_target_pairs={{0,1},{1,0},{8,9},{9,8},{16,17},{17,16},{24,25},{25,24},{2,3},{3,2... | collective-permute-start | bytes 147464 | tf_op jit(solution)/shard_map/ppermute | solution.py:331
  49.6 1.8 %collective-permute-start.17 = (bf16[128,1536]{1,0:T(8,128)(2,1)S(1)}, bf16[128,1536]{1,0:T(8,128)(2,1)S(1)}, u32[]{:S(2)}, u32[]{:S(2)}) collective-permute-start(bf16[128,1536]{1,0:T(8,128)(2,1)S(1)} %get-tuple-element.76), channel_id=1, source_target_pairs={{0,8},{1,9},{8,0},{9,1},{16,24},{17,25},{24,16},{25,17},{2,10},{3,... | collective-permute-start | bytes 1179656 | tf_op jit(solution)/shard_map/ppermute | solution.py:331
  49.7 6.3 %collective-permute-start.16 = (bf16[160,768]{1,0:T(8,128)(2,1)S(1)}, bf16[160,768]{1,0:T(8,128)(2,1)S(1)}, u32[]{:S(2)}, u32[]{:S(2)}) collective-permute-start(bf16[160,768]{1,0:T(8,128)(2,1)S(1)} %get-tuple-element.68), channel_id=1, source_target_pairs={{0,8},{1,25},{8,16},{9,1},{16,24},{17,9},{24,0},{25,17},{2,10},{3,... | collective-permute-start | bytes 737288 | tf_op jit(solution)/shard_map/ppermute | solution.py:335
  51.5 7.9 %collective-permute-start.18 = (bf16[64,1536]{1,0:T(8,128)(2,1)S(1)}, bf16[64,1536]{1,0:T(8,128)(2,1)S(1)}, u32[]{:S(2)}, u32[]{:S(2)}) collective-permute-start(bf16[64,1536]{1,0:T(8,128)(2,1)S(1)} %get-tuple-element.78), channel_id=1, source_target_pairs={{0,16},{1,17},{8,24},{9,25},{16,0},{17,1},{24,8},{25,9},{2,18},{3,... | collective-permute-start | bytes 589832 | tf_op jit(solution)/shard_map/ppermute | solution.py:331
  (4 other events, 20.2 us)

commit v6 on v5

--- a/solution.py
+++ b/solution.py
@@ -216,27 +216,16 @@
     return [[off_by(place, lists, slab, t, i) for i in range(2)] for t in range(2)]
 
 
-def pair(top, low):
-    return lambda cols: jnp.concatenate([top[:, cols], low[:, cols]], axis=0)
-
-
-def own_kernel(
-    place, lists, k, v, sk, sv, q, ga, gb, aux, key_acc, value_acc, text_k, text_v
-):
-    frame = k.shape[0]
-
-    def emit(cols, dk, dv):
-        key_acc[:, cols] = dk[:frame]
-        value_acc[:, cols] = dv[:frame]
-        text_k[:, cols] = dk[frame:]
-        text_v[:, cols] = dv[frame:]
-
-    offs = all_offs(place, lists, place[0])
-    key_terms(offs, pair(k, sk), pair(v, sv), q, ga, gb, aux, emit)
-
-
 def whole(ref):
     return lambda cols: ref[:, cols]
+
+
+def own_kernel(sk, sv, q, ga, gb, aux, text_k, text_v):
+    def emit(cols, dk, dv):
+        text_k[:, cols] = dk
+        text_v[:, cols] = dv
+
+    key_terms(None, whole(sk), whole(sv), q, ga, gb, aux, emit)
 
 
 def text_kernel(sk, sv, valid, q, ga, gb, aux, text_k, text_v, keep, send, message):
@@ -258,12 +247,19 @@
     key_terms(None, whole(sk), whole(sv), q, ga, gb, aux, emit)
 
 
-def mate_kernel(place, lists, k, v, q, ga, gb, aux, key_in, value_in, key_acc, value_acc):
-    def emit(cols, dk, dv):
-        key_acc[:, cols] = key_in[:, cols] + dk
-        value_acc[:, cols] = value_in[:, cols] + dv
-
-    key_terms(all_offs(place, lists, place[1]), whole(k), whole(v), q, ga, gb, aux, emit)
+def near_kernel(
+    place, lists, k, v, q0, ga0, gb0, aux0, q1, ga1, gb1, aux1, key_acc, value_acc
+):
+    def put(cols, dk, dv):
+        key_acc[:, cols] = dk
+        value_acc[:, cols] = dv
+
+    def add(cols, dk, dv):
+        key_acc[:, cols] = key_acc[:, cols] + dk
+        value_acc[:, cols] = value_acc[:, cols] + dv
+
+    key_terms(all_offs(place, lists, place[0]), whole(k), whole(v), q0, ga0, gb0, aux0, put)
+    key_terms(all_offs(place, lists, place[1]), whole(k), whole(v), q1, ga1, gb1, aux1, add)
 
 
 def far_kernel(place, lists, k, v, q, ga, message, key_acc, value_acc, key_out, value_out):
@@ -388,7 +384,7 @@
     late_a, mate_q = together(grad_a, mate_q)
     mate_a, mate_b = swap(late_a), swap(grad_b)
     far_q = relay(mate_q)
-    far_k, sk, mate_a = together(far_k, sk, mate_a)
+    far_k, mate_a = together(far_k, mate_a)
     wide = pltpu.VMEM((3 * frame, width), BF)
     aux, dscores = call(
         softmax_kernel,
@@ -406,14 +402,13 @@
     own_aux = aux
     acc = sds((frame, width), F32)
     text_acc = sds((slots, width), F32)
-    accs = call(
+    text_k, text_v = call(
         own_kernel,
-        "own_keys",
-        (acc, acc, text_acc, text_acc),
-        2,
-        (place, lists, keys, values, sk, sv, queries, grad_a, grad_b, own_aux),
-    )
-    key_acc, value_acc, text_k, text_v = accs
+        "own_slots",
+        (text_acc, text_acc),
+        0,
+        (sk, sv, queries, grad_a, grad_b, own_aux),
+    )
     mate_aux, far_q = together(mate_aux, far_q)
     far_a = relay(mate_a)
     mate_aux, far_a = together(mate_aux, far_a)
@@ -430,11 +425,14 @@
     )
     far_message = relay(message)
     key_acc, value_acc = call(
-        mate_kernel,
-        "mate_keys",
+        near_kernel,
+        "near_keys",
         (acc, acc),
         2,
-        (place, lists, keys, values, mate_q, mate_a, mate_b, mate_aux, key_acc, value_acc),
+        (
+            place, lists, keys, values, queries, grad_a, grad_b, own_aux,
+            mate_q, mate_a, mate_b, mate_aux,
+        ),
     )
     query_grads = call(
         query_kernel,

time: 60.3 us -> 60.1 us (level)
    ppermute x8, starting transfers between devices: 7.29 us -> 8.6 us  [swap(): return lax.ppermute(x, both, [(i, i ^ distance) for i in range(groups)])]
    ppermute x6, starting transfers between devices: 14.8 us -> 13.9 us  [ring(): return lax.ppermute(x, 'head', turns)]
    ppermute x8, waiting for transfers between devices: 6.66 us -> 7.48 us  [swap(): return lax.ppermute(x, both, [(i, i ^ distance) for i in range(groups)])]
    ppermute x6, waiting for transfers between devices: 3.07 us -> 2.38 us  [ring(): return lax.ppermute(x, 'head', turns)]
    pallas_call x13, Pallas kernels: 20.8 us -> 20.2 us  [call(): pl.pallas_call(kernel, name=name, out_shape=outs, in_specs=[SMEM] * scala...]
  transfers between devices with their start and end apart: 19 -> 19, of which waited for: 10 -> 8; matrix products, arithmetic and copies ran while one was open for 2% -> 2% of each run, Pallas kernels for 32% -> 31%
where the time goes in v6:
time: 60.1 us; the launch traced here: 59.9 us
  starting transfers between devices  24.6 us (41%)
  Pallas kernels  20.2 us (34%)
  waiting for transfers between devices  9.87 us (16%)
  local copies, waits for them, and re-layouts  4.35 us (7%)
  between operations  0.84 us (1%)
    pallas_call x13, Pallas kernels, call(): pl.pallas_call(kernel, name=name, out_shape=outs, in_specs=[SMEM] * scala...  20.2 us
    ppermute x6, starting transfers between devices, ring(): return lax.ppermute(x, 'head', turns)  13.9 us
    ppermute x8, starting transfers between devices, swap(): return lax.ppermute(x, both, [(i, i ^ distance) for i in range(groups)])  8.6 us
    ppermute x8, waiting for transfers between devices, swap(): return lax.ppermute(x, both, [(i, i ^ distance) for i in range(groups)])  7.48 us
    unnamed x18, local copies, waits for them, and re-layouts  2.39 us
    ppermute x6, waiting for transfers between devices, ring(): return lax.ppermute(x, 'head', turns)  2.38 us
    ppermute x5, starting transfers between devices, relay(): return lax.ppermute(x, both, turns)  2.12 us
  transfers between devices with their start and end apart: 19, of which 8 were waited for; matrix products, arithmetic and copies ran while one was open for 2% of the time, Pallas kernels for 31%

profile of v6, /device:TPU:0, one launch (start us, length us, event | category | flops | bytes accessed | tf_op | source)
XLA Modules:
  0.0 59.9 jit_solution(17921831120862217738)
XLA Ops:
  1.6 4.1 %collective-permute-start.3 = (bf16[128,768]{1,0:T(8,128)(2,1)S(1)}, bf16[128,768]{1,0:T(8,128)(2,1)S(1)}, u32[]{:S(2)}, u32[]{:S(2)}) collective-permute-start(bf16[128,768]{1,0:T(8,128)(2,1)S(1)} %slice.6.refs_0_), channel_id=1, source_target_pairs={{0,4},{4,6},{6,2},{2,0},{1,5},{5,7},{7,3},{3,1},{8,12},{12,14},{14... | collective-permute-start | bytes 589832 | tf_op jit(solution)/shard_map/ppermute | solution.py:335
  5.7 1.5 %collective-permute-start.6 = (bf16[256,768]{1,0:T(8,128)(2,1)}, bf16[256,768]{1,0:T(8,128)(2,1)S(1)}, u32[]{:S(2)}, u32[]{:S(2)}) collective-permute-start(bf16[256,768]{1,0:T(8,128)(2,1)} %v.3), channel_id=1, source_target_pairs={{0,1},{1,0},{8,9},{9,8},{16,17},{17,16},{24,25},{25,24},{2,3},{3,2... | collective-permute-start | bytes 1179656 | tf_op jit(solution)/shard_map/ppermute | solution.py:327
  8.1 1.6 %collective-permute-start = (bf16[128,768]{1,0:T(8,128)(2,1)S(1)}, bf16[128,768]{1,0:T(8,128)(2,1)S(1)}, u32[]{:S(2)}, u32[]{:S(2)}) collective-permute-start(bf16[128,768]{1,0:T(8,128)(2,1)S(1)} %slice.7.refs_2_), channel_id=1, source_target_pairs={{0,4},{4,6},{6,2},{2,0},{1,5},{5,7},{7,3},{3,1},{8,12},{12,14},{14... | collective-permute-start | bytes 589832 | tf_op jit(solution)/shard_map/ppermute | solution.py:335
  10.5 3.4 %collective-permute-start.5 = (bf16[128,768]{1,0:T(8,128)(2,1)S(1)}, bf16[128,768]{1,0:T(8,128)(2,1)S(1)}, u32[]{:S(2)}, u32[]{:S(2)}) collective-permute-start(bf16[128,768]{1,0:T(8,128)(2,1)S(1)} %collective-permute-done.3.refs_1_), channel_id=1, source_target_pairs={{0,4},{4,6},{6,2},{2,0},{1,5},{5,7},{7,3},{3,1},{8,12},{12,14},{14... | collective-permute-start | bytes 589832 | tf_op jit(solution)/shard_map/ppermute | solution.py:335
  13.8 2.1 %collective-permute-done.refs_3_ = bf16[128,768]{1,0:T(8,128)(2,1)S(1)} collective-permute-done((bf16[128,768]{1,0:T(8,128)(2,1)S(1)}, bf16[128,768]{1,0:T(8,128)(2,1)S(1)}, u32[]{:S(2)}, u32[]{:S(2)}) %collective-permute-start) | collective-permute-done | bytes 196640 | tf_op jit(solution)/shard_map/ppermute | solution.py:335
  16.0 2.5 %collective-permute-start.1 = (bf16[128,768]{1,0:T(8,128)(2,1)S(1)}, bf16[128,768]{1,0:T(8,128)(2,1)S(1)}, u32[]{:S(2)}, u32[]{:S(2)}) collective-permute-start(bf16[128,768]{1,0:T(8,128)(2,1)S(1)} %collective-permute-done.refs_3_), channel_id=1, source_target_pairs={{0,4},{4,6},{6,2},{2,0},{1,5},{5,7},{7,3},{3,1},{8,12},{12,14},{14... | collective-permute-start | bytes 589832 | tf_op jit(solution)/shard_map/ppermute | solution.py:335
  18.5 1.6 %collective-permute-start.8 = (bf16[256,768]{1,0:T(8,128)(2,1)}, bf16[256,768]{1,0:T(8,128)(2,1)S(1)}, u32[]{:S(2)}, u32[]{:S(2)}) collective-permute-start(bf16[256,768]{1,0:T(8,128)(2,1)} %q0.1), channel_id=1, source_target_pairs={{0,1},{1,0},{8,9},{9,8},{16,17},{17,16},{24,25},{25,24},{2,3},{3,2... | collective-permute-start | bytes 1179656 | tf_op jit(solution)/shard_map/ppermute | solution.py:327
  20.1 2.3 %copy-done = bf16[768,3072]{1,0:T(8,128)(2,1)S(1)} copy-done((bf16[768,3072]{1,0:T(8,128)(2,1)S(1)}, bf16[768,3072]{1,0:T(8,128)(2,1)}, u32[]{:S(2)}) %copy-start) | copy-done | bytes 4718616
  22.5 2.2 %first_blocks.1.first = f32[256,768]{1,0:T(8,128)S(1)} custom-call(s32[8]{0:T(128)S(1)} %stack.19.place, bf16[128,768]{1,0:T(8,128)(2,1)S(1)} %slice.6.refs_0_, bf16[128,768]{1,0:T(8,128)(2,1)S(1)} %collective-permute-done.3.refs_1_, bf16[128,768]{1,0:T(8,128)(2,1)S(1)} %slice.7.refs_2_, bf16[128,768]{1,0:T(8,128)(2,1)S(1)} %collective-permute-done.refs_3_, ...), custom_call_target="tpu_custom_call" | custom-call | tf_op jit(solution)/shard_map/first_blocks/pallas_call | solution.py:293
  26.3 1.6 %collective-permute-start.10 = (bf16[256,768]{1,0:T(8,128)(2,1)S(1)}, bf16[256,768]{1,0:T(8,128)(2,1)S(1)}, u32[]{:S(2)}, u32[]{:S(2)}) collective-permute-start(bf16[256,768]{1,0:T(8,128)(2,1)S(1)} %collective-permute-done.6.v1), channel_id=1, source_target_pairs={{0,8},{1,25},{8,16},{9,1},{16,24},{17,9},{24,0},{25,17},{2,10},{3,... | collective-permute-start | bytes 1179656 | tf_op jit(solution)/shard_map/ppermute | solution.py:331
  28.0 1.6 %collective-permute-start.11 = (bf16[128,768]{1,0:T(8,128)(2,1)S(1)}, bf16[128,768]{1,0:T(8,128)(2,1)S(1)}, u32[]{:S(2)}, u32[]{:S(2)}) collective-permute-start(bf16[128,768]{1,0:T(8,128)(2,1)S(1)} %collective-permute-done.1.b_before), channel_id=1, source_target_pairs={{0,4},{4,6},{6,2},{2,0},{1,5},{5,7},{7,3},{3,1},{8,12},{12,14},{14... | collective-permute-start | bytes 589832 | tf_op jit(solution)/shard_map/ppermute | solution.py:335
  29.6 1.5 %second_blocks.1.second = f32[256,768]{1,0:T(8,128)S(1)} custom-call(s32[8]{0:T(128)S(1)} %stack.19.place, bf16[128,768]{1,0:T(8,128)(2,1)S(1)} %collective-permute-done.5.a_before, bf16[128,768]{1,0:T(8,128)(2,1)S(1)} %collective-permute-done.1.b_before, bf16[768,3072]{1,0:T(8,128)(2,1)S(1)} %copy-done.1, f32[256,768]{1,0:T(8,128)S(1)} %first_blocks.1.first), custom_call_target="tpu_custom_call" | custom-call | tf_op jit(solution)/shard_map/second_blocks/pallas_call | solution.py:293
  31.1 1.1 %grad_heads_0.1.ga.ga0 = bf16[128,768]{1,0:T(8,128)(2,1)S(1)} custom-call(s32[8]{0:T(128)S(1)} %stack.19.place, bf16[128,768]{1,0:T(8,128)(2,1)S(1)} %collective-permute-done.7.last, bf16[768,3072]{1,0:T(8,128)(2,1)S(1)} %copy-done.1, f32[256,768]{1,0:T(8,128)S(1)} %second_blocks.1.second), custom_call_target="tpu_custom_call" | custom-call | tf_op jit(solution)/shard_map/grad_heads_0/pallas_call | solution.py:293
  32.2 1.1 %collective-permute-done.8.q.q1 = bf16[256,768]{1,0:T(8,128)(2,1)S(1)} collective-permute-done((bf16[256,768]{1,0:T(8,128)(2,1)}, bf16[256,768]{1,0:T(8,128)(2,1)S(1)}, u32[]{:S(2)}, u32[]{:S(2)}) %collective-permute-start.8) | collective-permute-done | bytes 393248 | tf_op jit(solution)/shard_map/ppermute | solution.py:327
  33.3 1.5 %collective-permute-start.9 = (bf16[128,768]{1,0:T(8,128)(2,1)S(1)}, bf16[128,768]{1,0:T(8,128)(2,1)S(1)}, u32[]{:S(2)}, u32[]{:S(2)}) collective-permute-start(bf16[128,768]{1,0:T(8,128)(2,1)S(1)} %grad_heads_0.1.ga.ga0), channel_id=1, source_target_pairs={{0,1},{1,0},{8,9},{9,8},{16,17},{17,16},{24,25},{25,24},{2,3},{3,2... | collective-permute-start | bytes 589832 | tf_op jit(solution)/shard_map/ppermute | solution.py:327
  34.8 1.1 %grad_heads_1.1.gb.gb0 = bf16[128,768]{1,0:T(8,128)(2,1)S(1)} custom-call(s32[8]{0:T(128)S(1)} %stack.19.place, bf16[128,768]{1,0:T(8,128)(2,1)S(1)} %collective-permute-done.11.last, bf16[768,3072]{1,0:T(8,128)(2,1)S(1)} %copy-done.1, f32[256,768]{1,0:T(8,128)S(1)} %second_blocks.1.second), custom_call_target="tpu_custom_call" | custom-call | tf_op jit(solution)/shard_map/grad_heads_1/pallas_call | solution.py:293
  36.5 2.5 %collective-permute-done.9.ga.ga1 = bf16[128,768]{1,0:T(8,128)(2,1)S(1)} collective-permute-done((bf16[128,768]{1,0:T(8,128)(2,1)S(1)}, bf16[128,768]{1,0:T(8,128)(2,1)S(1)}, u32[]{:S(2)}, u32[]{:S(2)}) %collective-permute-start.9) | collective-permute-done | bytes 196640 | tf_op jit(solution)/shard_map/ppermute | solution.py:327
  39.0 3.3 %softmax.1 = (bf16[32,768]{1,0:T(8,128)(2,1)S(1)}, bf16[1280,768]{1,0:T(8,128)(2,1)S(1)}) custom-call(s32[8]{0:T(128)S(1)} %stack.19.place, s32[3,16]{1,0:T(4,128)S(1)} %bitcast.6, bf16[256,768]{1,0:T(8,128)(2,1)S(1)} %copy-done.4, bf16[256,768]{1,0:T(8,128)(2,1)S(1)} %copy-done.2, bf16[256,768]{1,0:T(8,128)(2,1)S(1)} %collective-permute-done.2.k1, ...), custom_call_target="tpu_custom_call" | custom-call | tf_op jit(solution)/shard_map/softmax/pallas_call | solution.py:293
  43.2 1.4 %collective-permute-start.13 = (bf16[32,768]{1,0:T(8,128)(2,1)S(1)}, bf16[32,768]{1,0:T(8,128)(2,1)S(1)}, u32[]{:S(2)}, u32[]{:S(2)}) collective-permute-start(bf16[32,768]{1,0:T(8,128)(2,1)S(1)} %get-tuple-element.51.aux.aux0), channel_id=1, source_target_pairs={{0,1},{1,0},{8,9},{9,8},{16,17},{17,16},{24,25},{25,24},{2,3},{3,2... | collective-permute-start | bytes 147464 | tf_op jit(solution)/shard_map/ppermute | solution.py:327
  49.4 1.2 %collective-permute-done.17.arrived = bf16[128,1536]{1,0:T(8,128)(2,1)S(1)} collective-permute-done((bf16[128,1536]{1,0:T(8,128)(2,1)S(1)}, bf16[128,1536]{1,0:T(8,128)(2,1)S(1)}, u32[]{:S(2)}, u32[]{:S(2)}) %collective-permute-start.17) | collective-permute-done | bytes 393248 | tf_op jit(solution)/shard_map/ppermute | solution.py:327
  50.6 1.4 %collective-permute-start.18 = (bf16[64,1536]{1,0:T(8,128)(2,1)S(1)}, bf16[64,1536]{1,0:T(8,128)(2,1)S(1)}, u32[]{:S(2)}, u32[]{:S(2)}) collective-permute-start(bf16[64,1536]{1,0:T(8,128)(2,1)S(1)} %get-tuple-element.72), channel_id=1, source_target_pairs={{0,16},{1,17},{8,24},{9,25},{16,0},{17,1},{24,8},{25,9},{2,18},{3,... | collective-permute-start | bytes 589832 | tf_op jit(solution)/shard_map/ppermute | solution.py:327
  52.0 2.2 %query_grads.1 = bf16[256,768]{1,0:T(8,128)(2,1)} custom-call(s32[8]{0:T(128)S(1)} %stack.19.place, s32[3,16]{1,0:T(4,128)S(1)} %bitcast.7, bf16[256,768]{1,0:T(8,128)(2,1)S(1)} %copy-done.2, bf16[256,768]{1,0:T(8,128)(2,1)S(1)} %collective-permute-done.2.k1, bf16[256,768]{1,0:T(8,128)(2,1)S(1)} %collective-permute-done.4.k2, ...), custom_call_target="tpu_custom_call" | custom-call | tf_op jit(solution)/shard_map/query_grads/pallas_call | solution.py:293
  54.2 2.5 %near_keys.1 = (f32[256,768]{1,0:T(8,128)S(1)}, f32[256,768]{1,0:T(8,128)S(1)}) custom-call(s32[8]{0:T(128)S(1)} %stack.19.place, s32[3,16]{1,0:T(4,128)S(1)} %bitcast.8, bf16[256,768]{1,0:T(8,128)(2,1)S(1)} %copy-done.2, bf16[256,768]{1,0:T(8,128)(2,1)S(1)} %copy-done.3, bf16[256,768]{1,0:T(8,128)(2,1)S(1)} %copy-done.4, ...), custom_call_target="tpu_custom_call" | custom-call | tf_op jit(solution)/shard_map/near_keys/pallas_call | solution.py:293
  56.7 2.4 %far_keys.1 = (bf16[256,768]{1,0:T(8,128)(2,1)}, bf16[256,768]{1,0:T(8,128)(2,1)}) custom-call(s32[8]{0:T(128)S(1)} %stack.19.place, s32[3,16]{1,0:T(4,128)S(1)} %bitcast.9, bf16[256,768]{1,0:T(8,128)(2,1)S(1)} %copy-done.2, bf16[256,768]{1,0:T(8,128)(2,1)S(1)} %copy-done.3, bf16[256,768]{1,0:T(8,128)(2,1)S(1)} %collective-permute-done.14.q, ...), custom_call_target="tpu_custom_call" | custom-call | tf_op jit(solution)/shard_map/far_keys/pallas_call | solution.py:293
  (48 shorter events, 11.3 us)
Async XLA Ops:
  1.6 8.9 %collective-permute-start.3 = (bf16[128,768]{1,0:T(8,128)(2,1)S(1)}, bf16[128,768]{1,0:T(8,128)(2,1)S(1)}, u32[]{:S(2)}, u32[]{:S(2)}) collective-permute-start(bf16[128,768]{1,0:T(8,128)(2,1)S(1)} %slice.6.refs_0_), channel_id=1, source_target_pairs={{0,4},{4,6},{6,2},{2,0},{1,5},{5,7},{7,3},{3,1},{8,12},{12,14},{14... | collective-permute-start | bytes 589832 | tf_op jit(solution)/shard_map/ppermute | solution.py:335
  5.7 19.1 %collective-permute-start.6 = (bf16[256,768]{1,0:T(8,128)(2,1)}, bf16[256,768]{1,0:T(8,128)(2,1)S(1)}, u32[]{:S(2)}, u32[]{:S(2)}) collective-permute-start(bf16[256,768]{1,0:T(8,128)(2,1)} %v.3), channel_id=1, source_target_pairs={{0,1},{1,0},{8,9},{9,8},{16,17},{17,16},{24,25},{25,24},{2,3},{3,2... | collective-permute-start | bytes 1179656 | tf_op jit(solution)/shard_map/ppermute | solution.py:327
  8.1 7.9 %collective-permute-start = (bf16[128,768]{1,0:T(8,128)(2,1)S(1)}, bf16[128,768]{1,0:T(8,128)(2,1)S(1)}, u32[]{:S(2)}, u32[]{:S(2)}) collective-permute-start(bf16[128,768]{1,0:T(8,128)(2,1)S(1)} %slice.7.refs_2_), channel_id=1, source_target_pairs={{0,4},{4,6},{6,2},{2,0},{1,5},{5,7},{7,3},{3,1},{8,12},{12,14},{14... | collective-permute-start | bytes 589832 | tf_op jit(solution)/shard_map/ppermute | solution.py:335
  9.7 16.6 %collective-permute-start.2 = (bf16[256,768]{1,0:T(8,128)(2,1)}, bf16[256,768]{1,0:T(8,128)(2,1)S(1)}, u32[]{:S(2)}, u32[]{:S(2)}) collective-permute-start(bf16[256,768]{1,0:T(8,128)(2,1)} %k.3), channel_id=1, source_target_pairs={{0,1},{1,0},{8,9},{9,8},{16,17},{17,16},{24,25},{25,24},{2,3},{3,2... | collective-permute-start | bytes 1179656 | tf_op jit(solution)/shard_map/ppermute | solution.py:327
  10.5 14.3 %collective-permute-start.5 = (bf16[128,768]{1,0:T(8,128)(2,1)S(1)}, bf16[128,768]{1,0:T(8,128)(2,1)S(1)}, u32[]{:S(2)}, u32[]{:S(2)}) collective-permute-start(bf16[128,768]{1,0:T(8,128)(2,1)S(1)} %collective-permute-done.3.refs_1_), channel_id=1, source_target_pairs={{0,4},{4,6},{6,2},{2,0},{1,5},{5,7},{7,3},{3,1},{8,12},{12,14},{14... | collective-permute-start | bytes 589832 | tf_op jit(solution)/shard_map/ppermute | solution.py:335
  16.0 9.5 %collective-permute-start.1 = (bf16[128,768]{1,0:T(8,128)(2,1)S(1)}, bf16[128,768]{1,0:T(8,128)(2,1)S(1)}, u32[]{:S(2)}, u32[]{:S(2)}) collective-permute-start(bf16[128,768]{1,0:T(8,128)(2,1)S(1)} %collective-permute-done.refs_3_), channel_id=1, source_target_pairs={{0,4},{4,6},{6,2},{2,0},{1,5},{5,7},{7,3},{3,1},{8,12},{12,14},{14... | collective-permute-start | bytes 589832 | tf_op jit(solution)/shard_map/ppermute | solution.py:335
  18.5 14.8 %collective-permute-start.8 = (bf16[256,768]{1,0:T(8,128)(2,1)}, bf16[256,768]{1,0:T(8,128)(2,1)S(1)}, u32[]{:S(2)}, u32[]{:S(2)}) collective-permute-start(bf16[256,768]{1,0:T(8,128)(2,1)} %q0.1), channel_id=1, source_target_pairs={{0,1},{1,0},{8,9},{9,8},{16,17},{17,16},{24,25},{25,24},{2,3},{3,2... | collective-permute-start | bytes 1179656 | tf_op jit(solution)/shard_map/ppermute | solution.py:327
  24.8 6.3 %collective-permute-start.7 = (bf16[128,768]{1,0:T(8,128)(2,1)S(1)}, bf16[128,768]{1,0:T(8,128)(2,1)S(1)}, u32[]{:S(2)}, u32[]{:S(2)}) collective-permute-start(bf16[128,768]{1,0:T(8,128)(2,1)S(1)} %collective-permute-done.5.a_before), channel_id=1, source_target_pairs={{0,4},{4,6},{6,2},{2,0},{1,5},{5,7},{7,3},{3,1},{8,12},{12,14},{14... | collective-permute-start | bytes 589832 | tf_op jit(solution)/shard_map/ppermute | solution.py:335
  26.3 10.2 %collective-permute-start.4 = (bf16[256,768]{1,0:T(8,128)(2,1)S(1)}, bf16[256,768]{1,0:T(8,128)(2,1)S(1)}, u32[]{:S(2)}, u32[]{:S(2)}) collective-permute-start(bf16[256,768]{1,0:T(8,128)(2,1)S(1)} %collective-permute-done.2.k1), channel_id=1, source_target_pairs={{0,8},{1,25},{8,16},{9,1},{16,24},{17,9},{24,0},{25,17},{2,10},{3,... | collective-permute-start | bytes 1179656 | tf_op jit(solution)/shard_map/ppermute | solution.py:331
  26.3 12.6 %collective-permute-start.10 = (bf16[256,768]{1,0:T(8,128)(2,1)S(1)}, bf16[256,768]{1,0:T(8,128)(2,1)S(1)}, u32[]{:S(2)}, u32[]{:S(2)}) collective-permute-start(bf16[256,768]{1,0:T(8,128)(2,1)S(1)} %collective-permute-done.6.v1), channel_id=1, source_target_pairs={{0,8},{1,25},{8,16},{9,1},{16,24},{17,9},{24,0},{25,17},{2,10},{3,... | collective-permute-start | bytes 1179656 | tf_op jit(solution)/shard_map/ppermute | solution.py:331
  28.0 6.8 %collective-permute-start.11 = (bf16[128,768]{1,0:T(8,128)(2,1)S(1)}, bf16[128,768]{1,0:T(8,128)(2,1)S(1)}, u32[]{:S(2)}, u32[]{:S(2)}) collective-permute-start(bf16[128,768]{1,0:T(8,128)(2,1)S(1)} %collective-permute-done.1.b_before), channel_id=1, source_target_pairs={{0,4},{4,6},{6,2},{2,0},{1,5},{5,7},{7,3},{3,1},{8,12},{12,14},{14... | collective-permute-start | bytes 589832 | tf_op jit(solution)/shard_map/ppermute | solution.py:335
  31.0 8.0 %copy-start.2 = (bf16[256,768]{1,0:T(8,128)(2,1)S(1)}, bf16[256,768]{1,0:T(8,128)(2,1)}, u32[]{:S(2)}) copy-start(bf16[256,768]{1,0:T(8,128)(2,1)} %k.3) | copy-start | bytes 1179652
  31.0 8.0 %copy-start.3 = (bf16[256,768]{1,0:T(8,128)(2,1)S(1)}, bf16[256,768]{1,0:T(8,128)(2,1)}, u32[]{:S(2)}) copy-start(bf16[256,768]{1,0:T(8,128)(2,1)} %v.3) | copy-start | bytes 1179652
  31.1 7.9 %copy-start.4 = (bf16[256,768]{1,0:T(8,128)(2,1)S(1)}, bf16[256,768]{1,0:T(8,128)(2,1)}, u32[]{:S(2)}) copy-start(bf16[256,768]{1,0:T(8,128)(2,1)} %q0.1) | copy-start | bytes 1179652
  31.1 7.9 %copy-start.5 = (bf16[256,768]{1,0:T(8,128)(2,1)S(1)}, bf16[256,768]{1,0:T(8,128)(2,1)}, u32[]{:S(2)}) copy-start(bf16[256,768]{1,0:T(8,128)(2,1)} %tk.5) | copy-start | bytes 1179652
  32.2 12.4 %copy-start.8 = (s32[256]{0:T(256)S(1)}, s32[256]{0:T(256)}, u32[]{:S(2)}) copy-start(s32[256]{0:T(256)} %param.17) | copy-start | bytes 3076
  33.3 5.7 %collective-permute-start.9 = (bf16[128,768]{1,0:T(8,128)(2,1)S(1)}, bf16[128,768]{1,0:T(8,128)(2,1)S(1)}, u32[]{:S(2)}, u32[]{:S(2)}) collective-permute-start(bf16[128,768]{1,0:T(8,128)(2,1)S(1)} %grad_heads_0.1.ga.ga0), channel_id=1, source_target_pairs={{0,1},{1,0},{8,9},{9,8},{16,17},{17,16},{24,25},{25,24},{2,3},{3,2... | collective-permute-start | bytes 589832 | tf_op jit(solution)/shard_map/ppermute | solution.py:327
  34.8 12.9 %collective-permute-start.14 = (bf16[256,768]{1,0:T(8,128)(2,1)S(1)}, bf16[256,768]{1,0:T(8,128)(2,1)S(1)}, u32[]{:S(2)}, u32[]{:S(2)}) collective-permute-start(bf16[256,768]{1,0:T(8,128)(2,1)S(1)} %collective-permute-done.8.q.q1), channel_id=1, source_target_pairs={{0,8},{1,25},{8,16},{9,1},{16,24},{17,9},{24,0},{25,17},{2,10},{3,... | collective-permute-start | bytes 1179656 | tf_op jit(solution)/shard_map/ppermute | solution.py:331
  35.9 7.2 %collective-permute-start.12 = (bf16[128,768]{1,0:T(8,128)(2,1)S(1)}, bf16[128,768]{1,0:T(8,128)(2,1)S(1)}, u32[]{:S(2)}, u32[]{:S(2)}) collective-permute-start(bf16[128,768]{1,0:T(8,128)(2,1)S(1)} %grad_heads_1.1.gb.gb0), channel_id=1, source_target_pairs={{0,1},{1,0},{8,9},{9,8},{16,17},{17,16},{24,25},{25,24},{2,3},{3,2... | collective-permute-start | bytes 589832 | tf_op jit(solution)/shard_map/ppermute | solution.py:327
  39.0 8.7 %collective-permute-start.15 = (bf16[128,768]{1,0:T(8,128)(2,1)S(1)}, bf16[128,768]{1,0:T(8,128)(2,1)S(1)}, u32[]{:S(2)}, u32[]{:S(2)}) collective-permute-start(bf16[128,768]{1,0:T(8,128)(2,1)S(1)} %collective-permute-done.9.ga.ga1), channel_id=1, source_target_pairs={{0,8},{1,25},{8,16},{9,1},{16,24},{17,9},{24,0},{25,17},{2,10},{3,... | collective-permute-start | bytes 589832 | tf_op jit(solution)/shard_map/ppermute | solution.py:331
  43.2 4.5 %collective-permute-start.13 = (bf16[32,768]{1,0:T(8,128)(2,1)S(1)}, bf16[32,768]{1,0:T(8,128)(2,1)S(1)}, u32[]{:S(2)}, u32[]{:S(2)}) collective-permute-start(bf16[32,768]{1,0:T(8,128)(2,1)S(1)} %get-tuple-element.51.aux.aux0), channel_id=1, source_target_pairs={{0,1},{1,0},{8,9},{9,8},{16,17},{17,16},{24,25},{25,24},{2,3},{3,2... | collective-permute-start | bytes 147464 | tf_op jit(solution)/shard_map/ppermute | solution.py:327
  48.8 1.8 %collective-permute-start.17 = (bf16[128,1536]{1,0:T(8,128)(2,1)S(1)}, bf16[128,1536]{1,0:T(8,128)(2,1)S(1)}, u32[]{:S(2)}, u32[]{:S(2)}) collective-permute-start(bf16[128,1536]{1,0:T(8,128)(2,1)S(1)} %get-tuple-element.70), channel_id=1, source_target_pairs={{0,8},{1,9},{8,0},{9,1},{16,24},{17,25},{24,16},{25,17},{2,10},{3,... | collective-permute-start | bytes 1179656 | tf_op jit(solution)/shard_map/ppermute | solution.py:327
  48.9 7.8 %collective-permute-start.16 = (bf16[160,768]{1,0:T(8,128)(2,1)S(1)}, bf16[160,768]{1,0:T(8,128)(2,1)S(1)}, u32[]{:S(2)}, u32[]{:S(2)}) collective-permute-start(bf16[160,768]{1,0:T(8,128)(2,1)S(1)} %get-tuple-element.64), channel_id=1, source_target_pairs={{0,8},{1,25},{8,16},{9,1},{16,24},{17,9},{24,0},{25,17},{2,10},{3,... | collective-permute-start | bytes 737288 | tf_op jit(solution)/shard_map/ppermute | solution.py:331
  50.6 8.5 %collective-permute-start.18 = (bf16[64,1536]{1,0:T(8,128)(2,1)S(1)}, bf16[64,1536]{1,0:T(8,128)(2,1)S(1)}, u32[]{:S(2)}, u32[]{:S(2)}) collective-permute-start(bf16[64,1536]{1,0:T(8,128)(2,1)S(1)} %get-tuple-element.72), channel_id=1, source_target_pairs={{0,16},{1,17},{8,24},{9,25},{16,0},{17,1},{24,8},{25,9},{2,18},{3,... | collective-permute-start | bytes 589832 | tf_op jit(solution)/shard_map/ppermute | solution.py:327
  (4 other events, 25.3 us)

commit v7 on v6

--- a/solution.py
+++ b/solution.py
@@ -262,6 +262,19 @@
     key_terms(all_offs(place, lists, place[1]), whole(k), whole(v), q1, ga1, gb1, aux1, add)
 
 
+def query_near_kernel(
+    place, lists, k, v, q0, ga0, gb0, aux0, q1, ga1, gb1, aux1, k1, k2, tk, dscores,
+    out, key_acc, value_acc, wide_k, buf, sem,
+):
+    query_kernel(place, lists, k, k1, k2, tk, dscores, buf, wide_k)
+    copy = pltpu.make_async_copy(buf, out, sem)
+    copy.start()
+    near_kernel(
+        place, lists, k, v, q0, ga0, gb0, aux0, q1, ga1, gb1, aux1, key_acc, value_acc
+    )
+    copy.wait()
+
+
 def far_kernel(place, lists, k, v, q, ga, message, key_acc, value_acc, key_out, value_out):
     gb, aux = message.at[:TILE], message.at[TILE:]
 
@@ -289,13 +302,13 @@
 SMEM = pl.BlockSpec(memory_space=pltpu.SMEM)
 
 
-def call(kernel, name, outs, scalars, arrays, scratch=()):
+def call(kernel, name, outs, scalars, arrays, scratch=(), out_specs=None):
     return pl.pallas_call(
         kernel,
         name=name,
         out_shape=outs,
         in_specs=[SMEM] * scalars + [VMEM] * (len(arrays) - scalars),
-        out_specs=jax.tree.map(lambda _: VMEM, outs),
+        out_specs=out_specs or jax.tree.map(lambda _: VMEM, outs),
         scratch_shapes=list(scratch),
         compiler_params=pltpu.CompilerParams(vmem_limit_bytes=LIMIT),
     )(*arrays)
@@ -424,23 +437,17 @@
         (sk, sv, valid, mate_q, mate_a, mate_b, mate_aux, text_k, text_v),
     )
     far_message = relay(message)
-    key_acc, value_acc = call(
-        near_kernel,
-        "near_keys",
-        (acc, acc),
+    query_grads, key_acc, value_acc = call(
+        query_near_kernel,
+        "query_near_keys",
+        (sds((frame, width), BF), acc, acc),
         2,
         (
             place, lists, keys, values, queries, grad_a, grad_b, own_aux,
-            mate_q, mate_a, mate_b, mate_aux,
+            mate_q, mate_a, mate_b, mate_aux, mate_k, far_k, text_keys, dscores,
         ),
-    )
-    query_grads = call(
-        query_kernel,
-        "query_grads",
-        sds((frame, width), BF),
-        2,
-        (place, lists, keys, mate_k, far_k, text_keys, dscores),
-        (wide,),
+        (wide, pltpu.VMEM((frame, width), BF), pltpu.SemaphoreType.DMA),
+        (pl.BlockSpec(memory_space=pl.ANY), VMEM, VMEM),
     )
     key_grads, value_grads = call(
         far_kernel,

time: 60.1 us -> 59.4 us (0.988)
  Pallas kernels: 20.2 us -> 19.3 us
    pallas_call x13 -> x12, Pallas kernels: 20.2 us -> 19.3 us  [call(): pl.pallas_call(kernel, name=name, out_shape=outs, in_specs=[SMEM] * scala...]
  transfers between devices with their start and end apart: 19 -> 19, of which waited for: 8 -> 9; matrix products, arithmetic and copies ran while one was open for 2% -> 2% of each run, Pallas kernels for 31% -> 30%
where the time goes in v7:
time: 59.4 us; the launch traced here: 59.2 us
  starting transfers between devices  24.6 us (41%)
  Pallas kernels  19.3 us (32%)
  waiting for transfers between devices  10.2 us (17%)
  local copies, waits for them, and re-layouts  4.35 us (7%)
  between operations  0.85 us (1%)
    pallas_call x12, Pallas kernels, call(): pl.pallas_call(kernel, name=name, out_shape=outs, in_specs=[SMEM] * scala...  19.3 us
    ppermute x6, starting transfers between devices, ring(): return lax.ppermute(x, 'head', turns)  13.9 us
    ppermute x8, starting transfers between devices, swap(): return lax.ppermute(x, both, [(i, i ^ distance) for i in range(groups)])  8.59 us
    ppermute x8, waiting for transfers between devices, swap(): return lax.ppermute(x, both, [(i, i ^ distance) for i in range(groups)])  7.78 us
    unnamed x18, local copies, waits for them, and re-layouts  2.39 us
    ppermute x6, waiting for transfers between devices, ring(): return lax.ppermute(x, 'head', turns)  2.38 us
    ppermute x5, starting transfers between devices, relay(): return lax.ppermute(x, both, turns)  2.12 us
  transfers between devices with their start and end apart: 19, of which 9 were waited for; matrix products, arithmetic and copies ran while one was open for 2% of the time, Pallas kernels for 30%

profile of v7, /device:TPU:0, one launch (start us, length us, event | category | flops | bytes accessed | tf_op | source)
XLA Modules:
  0.0 59.2 jit_solution(7232140412519465137)
XLA Ops:
  1.6 4.1 %collective-permute-start = (bf16[128,768]{1,0:T(8,128)(2,1)S(1)}, bf16[128,768]{1,0:T(8,128)(2,1)S(1)}, u32[]{:S(2)}, u32[]{:S(2)}) collective-permute-start(bf16[128,768]{1,0:T(8,128)(2,1)S(1)} %slice.6.refs_0_), channel_id=1, source_target_pairs={{0,4},{4,6},{6,2},{2,0},{1,5},{5,7},{7,3},{3,1},{8,12},{12,14},{14... | collective-permute-start | bytes 589832 | tf_op jit(solution)/shard_map/ppermute | solution.py:348
  5.7 1.5 %collective-permute-start.2 = (bf16[256,768]{1,0:T(8,128)(2,1)}, bf16[256,768]{1,0:T(8,128)(2,1)S(1)}, u32[]{:S(2)}, u32[]{:S(2)}) collective-permute-start(bf16[256,768]{1,0:T(8,128)(2,1)} %v.3), channel_id=1, source_target_pairs={{0,1},{1,0},{8,9},{9,8},{16,17},{17,16},{24,25},{25,24},{2,3},{3,2... | collective-permute-start | bytes 1179656 | tf_op jit(solution)/shard_map/ppermute | solution.py:340
  8.1 1.6 %collective-permute-start.4 = (bf16[128,768]{1,0:T(8,128)(2,1)S(1)}, bf16[128,768]{1,0:T(8,128)(2,1)S(1)}, u32[]{:S(2)}, u32[]{:S(2)}) collective-permute-start(bf16[128,768]{1,0:T(8,128)(2,1)S(1)} %slice.7.refs_2_), channel_id=1, source_target_pairs={{0,4},{4,6},{6,2},{2,0},{1,5},{5,7},{7,3},{3,1},{8,12},{12,14},{14... | collective-permute-start | bytes 589832 | tf_op jit(solution)/shard_map/ppermute | solution.py:348
  10.5 3.4 %collective-permute-start.1 = (bf16[128,768]{1,0:T(8,128)(2,1)S(1)}, bf16[128,768]{1,0:T(8,128)(2,1)S(1)}, u32[]{:S(2)}, u32[]{:S(2)}) collective-permute-start(bf16[128,768]{1,0:T(8,128)(2,1)S(1)} %collective-permute-done.refs_1_), channel_id=1, source_target_pairs={{0,4},{4,6},{6,2},{2,0},{1,5},{5,7},{7,3},{3,1},{8,12},{12,14},{14... | collective-permute-start | bytes 589832 | tf_op jit(solution)/shard_map/ppermute | solution.py:348
  13.8 2.1 %collective-permute-done.4.refs_3_ = bf16[128,768]{1,0:T(8,128)(2,1)S(1)} collective-permute-done((bf16[128,768]{1,0:T(8,128)(2,1)S(1)}, bf16[128,768]{1,0:T(8,128)(2,1)S(1)}, u32[]{:S(2)}, u32[]{:S(2)}) %collective-permute-start.4) | collective-permute-done | bytes 196640 | tf_op jit(solution)/shard_map/ppermute | solution.py:348
  16.0 2.5 %collective-permute-start.5 = (bf16[128,768]{1,0:T(8,128)(2,1)S(1)}, bf16[128,768]{1,0:T(8,128)(2,1)S(1)}, u32[]{:S(2)}, u32[]{:S(2)}) collective-permute-start(bf16[128,768]{1,0:T(8,128)(2,1)S(1)} %collective-permute-done.4.refs_3_), channel_id=1, source_target_pairs={{0,4},{4,6},{6,2},{2,0},{1,5},{5,7},{7,3},{3,1},{8,12},{12,14},{14... | collective-permute-start | bytes 589832 | tf_op jit(solution)/shard_map/ppermute | solution.py:348
  18.5 1.6 %collective-permute-start.9 = (bf16[256,768]{1,0:T(8,128)(2,1)}, bf16[256,768]{1,0:T(8,128)(2,1)S(1)}, u32[]{:S(2)}, u32[]{:S(2)}) collective-permute-start(bf16[256,768]{1,0:T(8,128)(2,1)} %q.3), channel_id=1, source_target_pairs={{0,1},{1,0},{8,9},{9,8},{16,17},{17,16},{24,25},{25,24},{2,3},{3,2... | collective-permute-start | bytes 1179656 | tf_op jit(solution)/shard_map/ppermute | solution.py:340
  20.1 2.3 %copy-done = bf16[768,3072]{1,0:T(8,128)(2,1)S(1)} copy-done((bf16[768,3072]{1,0:T(8,128)(2,1)S(1)}, bf16[768,3072]{1,0:T(8,128)(2,1)}, u32[]{:S(2)}) %copy-start) | copy-done | bytes 4718616
  22.5 2.2 %first_blocks.1.first = f32[256,768]{1,0:T(8,128)S(1)} custom-call(s32[8]{0:T(128)S(1)} %stack.19.place, bf16[128,768]{1,0:T(8,128)(2,1)S(1)} %slice.6.refs_0_, bf16[128,768]{1,0:T(8,128)(2,1)S(1)} %collective-permute-done.refs_1_, bf16[128,768]{1,0:T(8,128)(2,1)S(1)} %slice.7.refs_2_, bf16[128,768]{1,0:T(8,128)(2,1)S(1)} %collective-permute-done.4.refs_3_, ...), custom_call_target="tpu_custom_call" | custom-call | tf_op jit(solution)/shard_map/first_blocks/pallas_call | solution.py:306
  26.3 1.6 %collective-permute-start.11 = (bf16[256,768]{1,0:T(8,128)(2,1)S(1)}, bf16[256,768]{1,0:T(8,128)(2,1)S(1)}, u32[]{:S(2)}, u32[]{:S(2)}) collective-permute-start(bf16[256,768]{1,0:T(8,128)(2,1)S(1)} %collective-permute-done.2.v1), channel_id=1, source_target_pairs={{0,8},{1,25},{8,16},{9,1},{16,24},{17,9},{24,0},{25,17},{2,10},{3,... | collective-permute-start | bytes 1179656 | tf_op jit(solution)/shard_map/ppermute | solution.py:344
  28.0 1.6 %collective-permute-start.7 = (bf16[128,768]{1,0:T(8,128)(2,1)S(1)}, bf16[128,768]{1,0:T(8,128)(2,1)S(1)}, u32[]{:S(2)}, u32[]{:S(2)}) collective-permute-start(bf16[128,768]{1,0:T(8,128)(2,1)S(1)} %collective-permute-done.5.b_before), channel_id=1, source_target_pairs={{0,4},{4,6},{6,2},{2,0},{1,5},{5,7},{7,3},{3,1},{8,12},{12,14},{14... | collective-permute-start | bytes 589832 | tf_op jit(solution)/shard_map/ppermute | solution.py:348
  29.6 1.5 %second_blocks.1.second = f32[256,768]{1,0:T(8,128)S(1)} custom-call(s32[8]{0:T(128)S(1)} %stack.19.place, bf16[128,768]{1,0:T(8,128)(2,1)S(1)} %collective-permute-done.1.a_before, bf16[128,768]{1,0:T(8,128)(2,1)S(1)} %collective-permute-done.5.b_before, bf16[768,3072]{1,0:T(8,128)(2,1)S(1)} %copy-done.1, f32[256,768]{1,0:T(8,128)S(1)} %first_blocks.1.first), custom_call_target="tpu_custom_call" | custom-call | tf_op jit(solution)/shard_map/second_blocks/pallas_call | solution.py:306
  31.1 1.1 %grad_heads_0.1.ga.ga0 = bf16[128,768]{1,0:T(8,128)(2,1)S(1)} custom-call(s32[8]{0:T(128)S(1)} %stack.19.place, bf16[128,768]{1,0:T(8,128)(2,1)S(1)} %collective-permute-done.3.last, bf16[768,3072]{1,0:T(8,128)(2,1)S(1)} %copy-done.1, f32[256,768]{1,0:T(8,128)S(1)} %second_blocks.1.second), custom_call_target="tpu_custom_call" | custom-call | tf_op jit(solution)/shard_map/grad_heads_0/pallas_call | solution.py:306
  32.2 1.1 %collective-permute-done.9.q1.q = bf16[256,768]{1,0:T(8,128)(2,1)S(1)} collective-permute-done((bf16[256,768]{1,0:T(8,128)(2,1)}, bf16[256,768]{1,0:T(8,128)(2,1)S(1)}, u32[]{:S(2)}, u32[]{:S(2)}) %collective-permute-start.9) | collective-permute-done | bytes 393248 | tf_op jit(solution)/shard_map/ppermute | solution.py:340
  33.3 1.5 %collective-permute-start.10 = (bf16[128,768]{1,0:T(8,128)(2,1)S(1)}, bf16[128,768]{1,0:T(8,128)(2,1)S(1)}, u32[]{:S(2)}, u32[]{:S(2)}) collective-permute-start(bf16[128,768]{1,0:T(8,128)(2,1)S(1)} %grad_heads_0.1.ga.ga0), channel_id=1, source_target_pairs={{0,1},{1,0},{8,9},{9,8},{16,17},{17,16},{24,25},{25,24},{2,3},{3,2... | collective-permute-start | bytes 589832 | tf_op jit(solution)/shard_map/ppermute | solution.py:340
  34.8 1.1 %grad_heads_1.1.gb.gb0 = bf16[128,768]{1,0:T(8,128)(2,1)S(1)} custom-call(s32[8]{0:T(128)S(1)} %stack.19.place, bf16[128,768]{1,0:T(8,128)(2,1)S(1)} %collective-permute-done.7.last, bf16[768,3072]{1,0:T(8,128)(2,1)S(1)} %copy-done.1, f32[256,768]{1,0:T(8,128)S(1)} %second_blocks.1.second), custom_call_target="tpu_custom_call" | custom-call | tf_op jit(solution)/shard_map/grad_heads_1/pallas_call | solution.py:306
  36.5 2.5 %collective-permute-done.10.ga1.ga = bf16[128,768]{1,0:T(8,128)(2,1)S(1)} collective-permute-done((bf16[128,768]{1,0:T(8,128)(2,1)S(1)}, bf16[128,768]{1,0:T(8,128)(2,1)S(1)}, u32[]{:S(2)}, u32[]{:S(2)}) %collective-permute-start.10) | collective-permute-done | bytes 196640 | tf_op jit(solution)/shard_map/ppermute | solution.py:340
  39.0 3.3 %softmax.1 = (bf16[32,768]{1,0:T(8,128)(2,1)S(1)}, bf16[1280,768]{1,0:T(8,128)(2,1)S(1)}) custom-call(s32[8]{0:T(128)S(1)} %stack.19.place, s32[3,16]{1,0:T(4,128)S(1)} %bitcast.6, bf16[256,768]{1,0:T(8,128)(2,1)S(1)} %copy-done.4, bf16[256,768]{1,0:T(8,128)(2,1)S(1)} %copy-done.2, bf16[256,768]{1,0:T(8,128)(2,1)S(1)} %collective-permute-done.6.k1, ...), custom_call_target="tpu_custom_call" | custom-call | tf_op jit(solution)/shard_map/softmax/pallas_call | solution.py:306
  43.2 1.4 %collective-permute-start.13 = (bf16[32,768]{1,0:T(8,128)(2,1)S(1)}, bf16[32,768]{1,0:T(8,128)(2,1)S(1)}, u32[]{:S(2)}, u32[]{:S(2)}) collective-permute-start(bf16[32,768]{1,0:T(8,128)(2,1)S(1)} %get-tuple-element.54.aux0.aux), channel_id=1, source_target_pairs={{0,1},{1,0},{8,9},{9,8},{16,17},{17,16},{24,25},{25,24},{2,3},{3,2... | collective-permute-start | bytes 147464 | tf_op jit(solution)/shard_map/ppermute | solution.py:340
  47.7 1.1 %text_slots.1 = (f32[128,1536]{1,0:T(8,128)S(1)}, bf16[128,1536]{1,0:T(8,128)(2,1)S(1)}, bf16[160,768]{1,0:T(8,128)(2,1)S(1)}) custom-call(bf16[256,768]{1,0:T(8,128)(2,1)S(1)} %get-tuple-element.61.sk, bf16[256,768]{1,0:T(8,128)(2,1)S(1)} %get-tuple-element.62.sv, f32[256,128]{1,0:T(8,128)S(1)} %get-tuple-element.63.valid, ...), custom_call_target="tpu_custom_call" | custom-call | tf_op jit(solution)/shard_map/text_slots/pallas_call | solution.py:306
  49.4 1.2 %collective-permute-done.17.arrived = bf16[128,1536]{1,0:T(8,128)(2,1)S(1)} collective-permute-done((bf16[128,1536]{1,0:T(8,128)(2,1)S(1)}, bf16[128,1536]{1,0:T(8,128)(2,1)S(1)}, u32[]{:S(2)}, u32[]{:S(2)}) %collective-permute-start.17) | collective-permute-done | bytes 393248 | tf_op jit(solution)/shard_map/ppermute | solution.py:340
  50.6 1.4 %collective-permute-start.18 = (bf16[64,1536]{1,0:T(8,128)(2,1)S(1)}, bf16[64,1536]{1,0:T(8,128)(2,1)S(1)}, u32[]{:S(2)}, u32[]{:S(2)}) collective-permute-start(bf16[64,1536]{1,0:T(8,128)(2,1)S(1)} %get-tuple-element.74), channel_id=1, source_target_pairs={{0,16},{1,17},{8,24},{9,25},{16,0},{17,1},{24,8},{25,9},{2,18},{3,... | collective-permute-start | bytes 589832 | tf_op jit(solution)/shard_map/ppermute | solution.py:340
  52.0 3.8 %query_near_keys.1 = (bf16[256,768]{1,0:T(8,128)(2,1)}, f32[256,768]{1,0:T(8,128)S(1)}, f32[256,768]{1,0:T(8,128)S(1)}) custom-call(s32[8]{0:T(128)S(1)} %stack.19.place, s32[3,16]{1,0:T(4,128)S(1)} %bitcast.7, bf16[256,768]{1,0:T(8,128)(2,1)S(1)} %copy-done.2, bf16[256,768]{1,0:T(8,128)(2,1)S(1)} %copy-done.3, bf16[256,768]{1,0:T(8,128)(2,1)S(1)} %copy-done.4, ...), custom_call_target="tpu_custom_call" | custom-call | tf_op jit(solution)/shard_map/query_near_keys/pallas_call | solution.py:306
  55.8 2.4 %far_keys.1 = (bf16[256,768]{1,0:T(8,128)(2,1)}, bf16[256,768]{1,0:T(8,128)(2,1)}) custom-call(s32[8]{0:T(128)S(1)} %stack.19.place, s32[3,16]{1,0:T(4,128)S(1)} %bitcast.8, bf16[256,768]{1,0:T(8,128)(2,1)S(1)} %copy-done.2, bf16[256,768]{1,0:T(8,128)(2,1)S(1)} %copy-done.3, bf16[256,768]{1,0:T(8,128)(2,1)S(1)} %collective-permute-done.14.q, ...), custom_call_target="tpu_custom_call" | custom-call | tf_op jit(solution)/shard_map/far_keys/pallas_call | solution.py:306
  (47 shorter events, 10.5 us)
Async XLA Ops:
  1.6 8.9 %collective-permute-start = (bf16[128,768]{1,0:T(8,128)(2,1)S(1)}, bf16[128,768]{1,0:T(8,128)(2,1)S(1)}, u32[]{:S(2)}, u32[]{:S(2)}) collective-permute-start(bf16[128,768]{1,0:T(8,128)(2,1)S(1)} %slice.6.refs_0_), channel_id=1, source_target_pairs={{0,4},{4,6},{6,2},{2,0},{1,5},{5,7},{7,3},{3,1},{8,12},{12,14},{14... | collective-permute-start | bytes 589832 | tf_op jit(solution)/shard_map/ppermute | solution.py:348
  5.7 19.1 %collective-permute-start.2 = (bf16[256,768]{1,0:T(8,128)(2,1)}, bf16[256,768]{1,0:T(8,128)(2,1)S(1)}, u32[]{:S(2)}, u32[]{:S(2)}) collective-permute-start(bf16[256,768]{1,0:T(8,128)(2,1)} %v.3), channel_id=1, source_target_pairs={{0,1},{1,0},{8,9},{9,8},{16,17},{17,16},{24,25},{25,24},{2,3},{3,2... | collective-permute-start | bytes 1179656 | tf_op jit(solution)/shard_map/ppermute | solution.py:340
  8.1 7.9 %collective-permute-start.4 = (bf16[128,768]{1,0:T(8,128)(2,1)S(1)}, bf16[128,768]{1,0:T(8,128)(2,1)S(1)}, u32[]{:S(2)}, u32[]{:S(2)}) collective-permute-start(bf16[128,768]{1,0:T(8,128)(2,1)S(1)} %slice.7.refs_2_), channel_id=1, source_target_pairs={{0,4},{4,6},{6,2},{2,0},{1,5},{5,7},{7,3},{3,1},{8,12},{12,14},{14... | collective-permute-start | bytes 589832 | tf_op jit(solution)/shard_map/ppermute | solution.py:348
  9.7 16.6 %collective-permute-start.6 = (bf16[256,768]{1,0:T(8,128)(2,1)}, bf16[256,768]{1,0:T(8,128)(2,1)S(1)}, u32[]{:S(2)}, u32[]{:S(2)}) collective-permute-start(bf16[256,768]{1,0:T(8,128)(2,1)} %k.3), channel_id=1, source_target_pairs={{0,1},{1,0},{8,9},{9,8},{16,17},{17,16},{24,25},{25,24},{2,3},{3,2... | collective-permute-start | bytes 1179656 | tf_op jit(solution)/shard_map/ppermute | solution.py:340
  10.5 14.3 %collective-permute-start.1 = (bf16[128,768]{1,0:T(8,128)(2,1)S(1)}, bf16[128,768]{1,0:T(8,128)(2,1)S(1)}, u32[]{:S(2)}, u32[]{:S(2)}) collective-permute-start(bf16[128,768]{1,0:T(8,128)(2,1)S(1)} %collective-permute-done.refs_1_), channel_id=1, source_target_pairs={{0,4},{4,6},{6,2},{2,0},{1,5},{5,7},{7,3},{3,1},{8,12},{12,14},{14... | collective-permute-start | bytes 589832 | tf_op jit(solution)/shard_map/ppermute | solution.py:348
  16.0 9.5 %collective-permute-start.5 = (bf16[128,768]{1,0:T(8,128)(2,1)S(1)}, bf16[128,768]{1,0:T(8,128)(2,1)S(1)}, u32[]{:S(2)}, u32[]{:S(2)}) collective-permute-start(bf16[128,768]{1,0:T(8,128)(2,1)S(1)} %collective-permute-done.4.refs_3_), channel_id=1, source_target_pairs={{0,4},{4,6},{6,2},{2,0},{1,5},{5,7},{7,3},{3,1},{8,12},{12,14},{14... | collective-permute-start | bytes 589832 | tf_op jit(solution)/shard_map/ppermute | solution.py:348
  18.5 14.8 %collective-permute-start.9 = (bf16[256,768]{1,0:T(8,128)(2,1)}, bf16[256,768]{1,0:T(8,128)(2,1)S(1)}, u32[]{:S(2)}, u32[]{:S(2)}) collective-permute-start(bf16[256,768]{1,0:T(8,128)(2,1)} %q.3), channel_id=1, source_target_pairs={{0,1},{1,0},{8,9},{9,8},{16,17},{17,16},{24,25},{25,24},{2,3},{3,2... | collective-permute-start | bytes 1179656 | tf_op jit(solution)/shard_map/ppermute | solution.py:340
  24.8 6.3 %collective-permute-start.3 = (bf16[128,768]{1,0:T(8,128)(2,1)S(1)}, bf16[128,768]{1,0:T(8,128)(2,1)S(1)}, u32[]{:S(2)}, u32[]{:S(2)}) collective-permute-start(bf16[128,768]{1,0:T(8,128)(2,1)S(1)} %collective-permute-done.1.a_before), channel_id=1, source_target_pairs={{0,4},{4,6},{6,2},{2,0},{1,5},{5,7},{7,3},{3,1},{8,12},{12,14},{14... | collective-permute-start | bytes 589832 | tf_op jit(solution)/shard_map/ppermute | solution.py:348
  26.3 10.2 %collective-permute-start.8 = (bf16[256,768]{1,0:T(8,128)(2,1)S(1)}, bf16[256,768]{1,0:T(8,128)(2,1)S(1)}, u32[]{:S(2)}, u32[]{:S(2)}) collective-permute-start(bf16[256,768]{1,0:T(8,128)(2,1)S(1)} %collective-permute-done.6.k1), channel_id=1, source_target_pairs={{0,8},{1,25},{8,16},{9,1},{16,24},{17,9},{24,0},{25,17},{2,10},{3,... | collective-permute-start | bytes 1179656 | tf_op jit(solution)/shard_map/ppermute | solution.py:344
  26.3 12.6 %collective-permute-start.11 = (bf16[256,768]{1,0:T(8,128)(2,1)S(1)}, bf16[256,768]{1,0:T(8,128)(2,1)S(1)}, u32[]{:S(2)}, u32[]{:S(2)}) collective-permute-start(bf16[256,768]{1,0:T(8,128)(2,1)S(1)} %collective-permute-done.2.v1), channel_id=1, source_target_pairs={{0,8},{1,25},{8,16},{9,1},{16,24},{17,9},{24,0},{25,17},{2,10},{3,... | collective-permute-start | bytes 1179656 | tf_op jit(solution)/shard_map/ppermute | solution.py:344
  28.0 6.8 %collective-permute-start.7 = (bf16[128,768]{1,0:T(8,128)(2,1)S(1)}, bf16[128,768]{1,0:T(8,128)(2,1)S(1)}, u32[]{:S(2)}, u32[]{:S(2)}) collective-permute-start(bf16[128,768]{1,0:T(8,128)(2,1)S(1)} %collective-permute-done.5.b_before), channel_id=1, source_target_pairs={{0,4},{4,6},{6,2},{2,0},{1,5},{5,7},{7,3},{3,1},{8,12},{12,14},{14... | collective-permute-start | bytes 589832 | tf_op jit(solution)/shard_map/ppermute | solution.py:348
  31.0 8.0 %copy-start.2 = (bf16[256,768]{1,0:T(8,128)(2,1)S(1)}, bf16[256,768]{1,0:T(8,128)(2,1)}, u32[]{:S(2)}) copy-start(bf16[256,768]{1,0:T(8,128)(2,1)} %k.3) | copy-start | bytes 1179652
  31.0 8.0 %copy-start.3 = (bf16[256,768]{1,0:T(8,128)(2,1)S(1)}, bf16[256,768]{1,0:T(8,128)(2,1)}, u32[]{:S(2)}) copy-start(bf16[256,768]{1,0:T(8,128)(2,1)} %v.3) | copy-start | bytes 1179652
  31.1 7.9 %copy-start.4 = (bf16[256,768]{1,0:T(8,128)(2,1)S(1)}, bf16[256,768]{1,0:T(8,128)(2,1)}, u32[]{:S(2)}) copy-start(bf16[256,768]{1,0:T(8,128)(2,1)} %q.3) | copy-start | bytes 1179652
  31.1 7.9 %copy-start.5 = (bf16[256,768]{1,0:T(8,128)(2,1)S(1)}, bf16[256,768]{1,0:T(8,128)(2,1)}, u32[]{:S(2)}) copy-start(bf16[256,768]{1,0:T(8,128)(2,1)} %tk.5) | copy-start | bytes 1179652
  32.2 12.4 %copy-start.8 = (s32[256]{0:T(256)S(1)}, s32[256]{0:T(256)}, u32[]{:S(2)}) copy-start(s32[256]{0:T(256)} %param.17) | copy-start | bytes 3076
  33.3 5.7 %collective-permute-start.10 = (bf16[128,768]{1,0:T(8,128)(2,1)S(1)}, bf16[128,768]{1,0:T(8,128)(2,1)S(1)}, u32[]{:S(2)}, u32[]{:S(2)}) collective-permute-start(bf16[128,768]{1,0:T(8,128)(2,1)S(1)} %grad_heads_0.1.ga.ga0), channel_id=1, source_target_pairs={{0,1},{1,0},{8,9},{9,8},{16,17},{17,16},{24,25},{25,24},{2,3},{3,2... | collective-permute-start | bytes 589832 | tf_op jit(solution)/shard_map/ppermute | solution.py:340
  34.8 12.9 %collective-permute-start.14 = (bf16[256,768]{1,0:T(8,128)(2,1)S(1)}, bf16[256,768]{1,0:T(8,128)(2,1)S(1)}, u32[]{:S(2)}, u32[]{:S(2)}) collective-permute-start(bf16[256,768]{1,0:T(8,128)(2,1)S(1)} %collective-permute-done.9.q1.q), channel_id=1, source_target_pairs={{0,8},{1,25},{8,16},{9,1},{16,24},{17,9},{24,0},{25,17},{2,10},{3,... | collective-permute-start | bytes 1179656 | tf_op jit(solution)/shard_map/ppermute | solution.py:344
  35.9 7.2 %collective-permute-start.12 = (bf16[128,768]{1,0:T(8,128)(2,1)S(1)}, bf16[128,768]{1,0:T(8,128)(2,1)S(1)}, u32[]{:S(2)}, u32[]{:S(2)}) collective-permute-start(bf16[128,768]{1,0:T(8,128)(2,1)S(1)} %grad_heads_1.1.gb.gb0), channel_id=1, source_target_pairs={{0,1},{1,0},{8,9},{9,8},{16,17},{17,16},{24,25},{25,24},{2,3},{3,2... | collective-permute-start | bytes 589832 | tf_op jit(solution)/shard_map/ppermute | solution.py:340
  39.0 8.7 %collective-permute-start.15 = (bf16[128,768]{1,0:T(8,128)(2,1)S(1)}, bf16[128,768]{1,0:T(8,128)(2,1)S(1)}, u32[]{:S(2)}, u32[]{:S(2)}) collective-permute-start(bf16[128,768]{1,0:T(8,128)(2,1)S(1)} %collective-permute-done.10.ga1.ga), channel_id=1, source_target_pairs={{0,8},{1,25},{8,16},{9,1},{16,24},{17,9},{24,0},{25,17},{2,10},{3,... | collective-permute-start | bytes 589832 | tf_op jit(solution)/shard_map/ppermute | solution.py:344
  43.2 4.5 %collective-permute-start.13 = (bf16[32,768]{1,0:T(8,128)(2,1)S(1)}, bf16[32,768]{1,0:T(8,128)(2,1)S(1)}, u32[]{:S(2)}, u32[]{:S(2)}) collective-permute-start(bf16[32,768]{1,0:T(8,128)(2,1)S(1)} %get-tuple-element.54.aux0.aux), channel_id=1, source_target_pairs={{0,1},{1,0},{8,9},{9,8},{16,17},{17,16},{24,25},{25,24},{2,3},{3,2... | collective-permute-start | bytes 147464 | tf_op jit(solution)/shard_map/ppermute | solution.py:340
  48.8 1.8 %collective-permute-start.17 = (bf16[128,1536]{1,0:T(8,128)(2,1)S(1)}, bf16[128,1536]{1,0:T(8,128)(2,1)S(1)}, u32[]{:S(2)}, u32[]{:S(2)}) collective-permute-start(bf16[128,1536]{1,0:T(8,128)(2,1)S(1)} %get-tuple-element.72), channel_id=1, source_target_pairs={{0,8},{1,9},{8,0},{9,1},{16,24},{17,25},{24,16},{25,17},{2,10},{3,... | collective-permute-start | bytes 1179656 | tf_op jit(solution)/shard_map/ppermute | solution.py:340
  48.9 6.9 %collective-permute-start.16 = (bf16[160,768]{1,0:T(8,128)(2,1)S(1)}, bf16[160,768]{1,0:T(8,128)(2,1)S(1)}, u32[]{:S(2)}, u32[]{:S(2)}) collective-permute-start(bf16[160,768]{1,0:T(8,128)(2,1)S(1)} %get-tuple-element.66), channel_id=1, source_target_pairs={{0,8},{1,25},{8,16},{9,1},{16,24},{17,9},{24,0},{25,17},{2,10},{3,... | collective-permute-start | bytes 737288 | tf_op jit(solution)/shard_map/ppermute | solution.py:344
  50.6 7.9 %collective-permute-start.18 = (bf16[64,1536]{1,0:T(8,128)(2,1)S(1)}, bf16[64,1536]{1,0:T(8,128)(2,1)S(1)}, u32[]{:S(2)}, u32[]{:S(2)}) collective-permute-start(bf16[64,1536]{1,0:T(8,128)(2,1)S(1)} %get-tuple-element.74), channel_id=1, source_target_pairs={{0,16},{1,17},{8,24},{9,25},{16,0},{17,1},{24,8},{25,9},{2,18},{3,... | collective-permute-start | bytes 589832 | tf_op jit(solution)/shard_map/ppermute | solution.py:340
  (4 other events, 25.3 us)

commit v8 on v7

--- a/solution.py
+++ b/solution.py
@@ -423,6 +423,7 @@
         (sk, sv, queries, grad_a, grad_b, own_aux),
     )
     mate_aux, far_q = together(mate_aux, far_q)
+    mate_a, sk = together(mate_a, sk)
     far_a = relay(mate_a)
     mate_aux, far_a = together(mate_aux, far_a)
     keep, send, message = call(

time: 59.4 us -> 59.4 us (level)
  no operation moved by 1% of the time
where the time goes in v8:
time: 59.4 us; the launch traced here: 59.2 us
  starting transfers between devices  24.6 us (41%)
  Pallas kernels  19.3 us (32%)
  waiting for transfers between devices  10.1 us (17%)
  local copies, waits for them, and re-layouts  4.35 us (7%)
  between operations  0.85 us (1%)
    pallas_call x12, Pallas kernels, call(): pl.pallas_call(kernel, name=name, out_shape=outs, in_specs=[SMEM] * scala...  19.3 us
    ppermute x6, starting transfers between devices, ring(): return lax.ppermute(x, 'head', turns)  13.9 us
    ppermute x8, starting transfers between devices, swap(): return lax.ppermute(x, both, [(i, i ^ distance) for i in range(groups)])  8.59 us
    ppermute x8, waiting for transfers between devices, swap(): return lax.ppermute(x, both, [(i, i ^ distance) for i in range(groups)])  7.75 us
    unnamed x18, local copies, waits for them, and re-layouts  2.39 us
    ppermute x6, waiting for transfers between devices, ring(): return lax.ppermute(x, 'head', turns)  2.38 us
    ppermute x5, starting transfers between devices, relay(): return lax.ppermute(x, both, turns)  2.14 us
  transfers between devices with their start and end apart: 19, of which 9 were waited for; matrix products, arithmetic and copies ran while one was open for 2% of the time, Pallas kernels for 30%

profile of v8, /device:TPU:0, one launch (start us, length us, event | category | flops | bytes accessed | tf_op | source)
XLA Modules:
  0.0 59.2 jit_solution(10112344149583883581)
XLA Ops:
  1.6 4.1 %collective-permute-start = (bf16[128,768]{1,0:T(8,128)(2,1)S(1)}, bf16[128,768]{1,0:T(8,128)(2,1)S(1)}, u32[]{:S(2)}, u32[]{:S(2)}) collective-permute-start(bf16[128,768]{1,0:T(8,128)(2,1)S(1)} %slice.6.refs_0_), channel_id=1, source_target_pairs={{0,4},{4,6},{6,2},{2,0},{1,5},{5,7},{7,3},{3,1},{8,12},{12,14},{14... | collective-permute-start | bytes 589832 | tf_op jit(solution)/shard_map/ppermute | solution.py:348
  5.7 1.5 %collective-permute-start.2 = (bf16[256,768]{1,0:T(8,128)(2,1)}, bf16[256,768]{1,0:T(8,128)(2,1)S(1)}, u32[]{:S(2)}, u32[]{:S(2)}) collective-permute-start(bf16[256,768]{1,0:T(8,128)(2,1)} %v.3), channel_id=1, source_target_pairs={{0,1},{1,0},{8,9},{9,8},{16,17},{17,16},{24,25},{25,24},{2,3},{3,2... | collective-permute-start | bytes 1179656 | tf_op jit(solution)/shard_map/ppermute | solution.py:340
  8.1 1.6 %collective-permute-start.4 = (bf16[128,768]{1,0:T(8,128)(2,1)S(1)}, bf16[128,768]{1,0:T(8,128)(2,1)S(1)}, u32[]{:S(2)}, u32[]{:S(2)}) collective-permute-start(bf16[128,768]{1,0:T(8,128)(2,1)S(1)} %slice.7.refs_2_), channel_id=1, source_target_pairs={{0,4},{4,6},{6,2},{2,0},{1,5},{5,7},{7,3},{3,1},{8,12},{12,14},{14... | collective-permute-start | bytes 589832 | tf_op jit(solution)/shard_map/ppermute | solution.py:348
  10.5 3.4 %collective-permute-start.1 = (bf16[128,768]{1,0:T(8,128)(2,1)S(1)}, bf16[128,768]{1,0:T(8,128)(2,1)S(1)}, u32[]{:S(2)}, u32[]{:S(2)}) collective-permute-start(bf16[128,768]{1,0:T(8,128)(2,1)S(1)} %collective-permute-done.refs_1_), channel_id=1, source_target_pairs={{0,4},{4,6},{6,2},{2,0},{1,5},{5,7},{7,3},{3,1},{8,12},{12,14},{14... | collective-permute-start | bytes 589832 | tf_op jit(solution)/shard_map/ppermute | solution.py:348
  13.8 2.1 %collective-permute-done.4.refs_3_ = bf16[128,768]{1,0:T(8,128)(2,1)S(1)} collective-permute-done((bf16[128,768]{1,0:T(8,128)(2,1)S(1)}, bf16[128,768]{1,0:T(8,128)(2,1)S(1)}, u32[]{:S(2)}, u32[]{:S(2)}) %collective-permute-start.4) | collective-permute-done | bytes 196640 | tf_op jit(solution)/shard_map/ppermute | solution.py:348
  16.0 2.5 %collective-permute-start.5 = (bf16[128,768]{1,0:T(8,128)(2,1)S(1)}, bf16[128,768]{1,0:T(8,128)(2,1)S(1)}, u32[]{:S(2)}, u32[]{:S(2)}) collective-permute-start(bf16[128,768]{1,0:T(8,128)(2,1)S(1)} %collective-permute-done.4.refs_3_), channel_id=1, source_target_pairs={{0,4},{4,6},{6,2},{2,0},{1,5},{5,7},{7,3},{3,1},{8,12},{12,14},{14... | collective-permute-start | bytes 589832 | tf_op jit(solution)/shard_map/ppermute | solution.py:348
  18.5 1.6 %collective-permute-start.9 = (bf16[256,768]{1,0:T(8,128)(2,1)}, bf16[256,768]{1,0:T(8,128)(2,1)S(1)}, u32[]{:S(2)}, u32[]{:S(2)}) collective-permute-start(bf16[256,768]{1,0:T(8,128)(2,1)} %q.3), channel_id=1, source_target_pairs={{0,1},{1,0},{8,9},{9,8},{16,17},{17,16},{24,25},{25,24},{2,3},{3,2... | collective-permute-start | bytes 1179656 | tf_op jit(solution)/shard_map/ppermute | solution.py:340
  20.1 2.3 %copy-done = bf16[768,3072]{1,0:T(8,128)(2,1)S(1)} copy-done((bf16[768,3072]{1,0:T(8,128)(2,1)S(1)}, bf16[768,3072]{1,0:T(8,128)(2,1)}, u32[]{:S(2)}) %copy-start) | copy-done | bytes 4718616
  22.5 2.2 %first_blocks.1.first = f32[256,768]{1,0:T(8,128)S(1)} custom-call(s32[8]{0:T(128)S(1)} %stack.19.place, bf16[128,768]{1,0:T(8,128)(2,1)S(1)} %slice.6.refs_0_, bf16[128,768]{1,0:T(8,128)(2,1)S(1)} %collective-permute-done.refs_1_, bf16[128,768]{1,0:T(8,128)(2,1)S(1)} %slice.7.refs_2_, bf16[128,768]{1,0:T(8,128)(2,1)S(1)} %collective-permute-done.4.refs_3_, ...), custom_call_target="tpu_custom_call" | custom-call | tf_op jit(solution)/shard_map/first_blocks/pallas_call | solution.py:306
  26.3 1.6 %collective-permute-start.11 = (bf16[256,768]{1,0:T(8,128)(2,1)S(1)}, bf16[256,768]{1,0:T(8,128)(2,1)S(1)}, u32[]{:S(2)}, u32[]{:S(2)}) collective-permute-start(bf16[256,768]{1,0:T(8,128)(2,1)S(1)} %collective-permute-done.2.v1), channel_id=1, source_target_pairs={{0,8},{1,25},{8,16},{9,1},{16,24},{17,9},{24,0},{25,17},{2,10},{3,... | collective-permute-start | bytes 1179656 | tf_op jit(solution)/shard_map/ppermute | solution.py:344
  28.0 1.6 %collective-permute-start.7 = (bf16[128,768]{1,0:T(8,128)(2,1)S(1)}, bf16[128,768]{1,0:T(8,128)(2,1)S(1)}, u32[]{:S(2)}, u32[]{:S(2)}) collective-permute-start(bf16[128,768]{1,0:T(8,128)(2,1)S(1)} %collective-permute-done.5.b_before), channel_id=1, source_target_pairs={{0,4},{4,6},{6,2},{2,0},{1,5},{5,7},{7,3},{3,1},{8,12},{12,14},{14... | collective-permute-start | bytes 589832 | tf_op jit(solution)/shard_map/ppermute | solution.py:348
  29.6 1.5 %second_blocks.1.second = f32[256,768]{1,0:T(8,128)S(1)} custom-call(s32[8]{0:T(128)S(1)} %stack.19.place, bf16[128,768]{1,0:T(8,128)(2,1)S(1)} %collective-permute-done.1.a_before, bf16[128,768]{1,0:T(8,128)(2,1)S(1)} %collective-permute-done.5.b_before, bf16[768,3072]{1,0:T(8,128)(2,1)S(1)} %copy-done.1, f32[256,768]{1,0:T(8,128)S(1)} %first_blocks.1.first), custom_call_target="tpu_custom_call" | custom-call | tf_op jit(solution)/shard_map/second_blocks/pallas_call | solution.py:306
  31.1 1.1 %grad_heads_0.1.ga.ga0 = bf16[128,768]{1,0:T(8,128)(2,1)S(1)} custom-call(s32[8]{0:T(128)S(1)} %stack.19.place, bf16[128,768]{1,0:T(8,128)(2,1)S(1)} %collective-permute-done.3.last, bf16[768,3072]{1,0:T(8,128)(2,1)S(1)} %copy-done.1, f32[256,768]{1,0:T(8,128)S(1)} %second_blocks.1.second), custom_call_target="tpu_custom_call" | custom-call | tf_op jit(solution)/shard_map/grad_heads_0/pallas_call | solution.py:306
  32.2 1.1 %collective-permute-done.9.q1.q = bf16[256,768]{1,0:T(8,128)(2,1)S(1)} collective-permute-done((bf16[256,768]{1,0:T(8,128)(2,1)}, bf16[256,768]{1,0:T(8,128)(2,1)S(1)}, u32[]{:S(2)}, u32[]{:S(2)}) %collective-permute-start.9) | collective-permute-done | bytes 393248 | tf_op jit(solution)/shard_map/ppermute | solution.py:340
  33.3 1.5 %collective-permute-start.10 = (bf16[128,768]{1,0:T(8,128)(2,1)S(1)}, bf16[128,768]{1,0:T(8,128)(2,1)S(1)}, u32[]{:S(2)}, u32[]{:S(2)}) collective-permute-start(bf16[128,768]{1,0:T(8,128)(2,1)S(1)} %grad_heads_0.1.ga.ga0), channel_id=1, source_target_pairs={{0,1},{1,0},{8,9},{9,8},{16,17},{17,16},{24,25},{25,24},{2,3},{3,2... | collective-permute-start | bytes 589832 | tf_op jit(solution)/shard_map/ppermute | solution.py:340
  34.8 1.1 %grad_heads_1.1.gb.gb0 = bf16[128,768]{1,0:T(8,128)(2,1)S(1)} custom-call(s32[8]{0:T(128)S(1)} %stack.19.place, bf16[128,768]{1,0:T(8,128)(2,1)S(1)} %collective-permute-done.7.last, bf16[768,3072]{1,0:T(8,128)(2,1)S(1)} %copy-done.1, f32[256,768]{1,0:T(8,128)S(1)} %second_blocks.1.second), custom_call_target="tpu_custom_call" | custom-call | tf_op jit(solution)/shard_map/grad_heads_1/pallas_call | solution.py:306
  37.5 1.5 %collective-permute-done.10.ga1.ga = bf16[128,768]{1,0:T(8,128)(2,1)S(1)} collective-permute-done((bf16[128,768]{1,0:T(8,128)(2,1)S(1)}, bf16[128,768]{1,0:T(8,128)(2,1)S(1)}, u32[]{:S(2)}, u32[]{:S(2)}) %collective-permute-start.10) | collective-permute-done | bytes 196640 | tf_op jit(solution)/shard_map/ppermute | solution.py:340
  39.0 3.3 %softmax.1 = (bf16[32,768]{1,0:T(8,128)(2,1)S(1)}, bf16[1280,768]{1,0:T(8,128)(2,1)S(1)}) custom-call(s32[8]{0:T(128)S(1)} %stack.19.place, s32[3,16]{1,0:T(4,128)S(1)} %bitcast.6, bf16[256,768]{1,0:T(8,128)(2,1)S(1)} %copy-done.4, bf16[256,768]{1,0:T(8,128)(2,1)S(1)} %copy-done.2, bf16[256,768]{1,0:T(8,128)(2,1)S(1)} %collective-permute-done.6.k1, ...), custom_call_target="tpu_custom_call" | custom-call | tf_op jit(solution)/shard_map/softmax/pallas_call | solution.py:306
  43.2 1.4 %collective-permute-start.13 = (bf16[32,768]{1,0:T(8,128)(2,1)S(1)}, bf16[32,768]{1,0:T(8,128)(2,1)S(1)}, u32[]{:S(2)}, u32[]{:S(2)}) collective-permute-start(bf16[32,768]{1,0:T(8,128)(2,1)S(1)} %get-tuple-element.58.aux0.aux), channel_id=1, source_target_pairs={{0,1},{1,0},{8,9},{9,8},{16,17},{17,16},{24,25},{25,24},{2,3},{3,2... | collective-permute-start | bytes 147464 | tf_op jit(solution)/shard_map/ppermute | solution.py:340
  45.7 2.0 %collective-permute-done.13.aux1.aux = bf16[32,768]{1,0:T(8,128)(2,1)S(1)} collective-permute-done((bf16[32,768]{1,0:T(8,128)(2,1)S(1)}, bf16[32,768]{1,0:T(8,128)(2,1)S(1)}, u32[]{:S(2)}, u32[]{:S(2)}) %collective-permute-start.13) | collective-permute-done | bytes 49184 | tf_op jit(solution)/shard_map/ppermute | solution.py:340
  49.3 1.2 %collective-permute-done.17.arrived = bf16[128,1536]{1,0:T(8,128)(2,1)S(1)} collective-permute-done((bf16[128,1536]{1,0:T(8,128)(2,1)S(1)}, bf16[128,1536]{1,0:T(8,128)(2,1)S(1)}, u32[]{:S(2)}, u32[]{:S(2)}) %collective-permute-start.17) | collective-permute-done | bytes 393248 | tf_op jit(solution)/shard_map/ppermute | solution.py:340
  50.6 1.4 %collective-permute-start.18 = (bf16[64,1536]{1,0:T(8,128)(2,1)S(1)}, bf16[64,1536]{1,0:T(8,128)(2,1)S(1)}, u32[]{:S(2)}, u32[]{:S(2)}) collective-permute-start(bf16[64,1536]{1,0:T(8,128)(2,1)S(1)} %get-tuple-element.78), channel_id=1, source_target_pairs={{0,16},{1,17},{8,24},{9,25},{16,0},{17,1},{24,8},{25,9},{2,18},{3,... | collective-permute-start | bytes 589832 | tf_op jit(solution)/shard_map/ppermute | solution.py:340
  52.0 3.8 %query_near_keys.1 = (bf16[256,768]{1,0:T(8,128)(2,1)}, f32[256,768]{1,0:T(8,128)S(1)}, f32[256,768]{1,0:T(8,128)S(1)}) custom-call(s32[8]{0:T(128)S(1)} %stack.19.place, s32[3,16]{1,0:T(4,128)S(1)} %bitcast.7, bf16[256,768]{1,0:T(8,128)(2,1)S(1)} %copy-done.2, bf16[256,768]{1,0:T(8,128)(2,1)S(1)} %copy-done.3, bf16[256,768]{1,0:T(8,128)(2,1)S(1)} %copy-done.4, ...), custom_call_target="tpu_custom_call" | custom-call | tf_op jit(solution)/shard_map/query_near_keys/pallas_call | solution.py:306
  55.8 2.4 %far_keys.1 = (bf16[256,768]{1,0:T(8,128)(2,1)}, bf16[256,768]{1,0:T(8,128)(2,1)}) custom-call(s32[8]{0:T(128)S(1)} %stack.19.place, s32[3,16]{1,0:T(4,128)S(1)} %bitcast.8, bf16[256,768]{1,0:T(8,128)(2,1)S(1)} %copy-done.2, bf16[256,768]{1,0:T(8,128)(2,1)S(1)} %copy-done.3, bf16[256,768]{1,0:T(8,128)(2,1)S(1)} %collective-permute-done.14.q, ...), custom_call_target="tpu_custom_call" | custom-call | tf_op jit(solution)/shard_map/far_keys/pallas_call | solution.py:306
  (47 shorter events, 10.5 us)
Async XLA Ops:
  1.6 8.9 %collective-permute-start = (bf16[128,768]{1,0:T(8,128)(2,1)S(1)}, bf16[128,768]{1,0:T(8,128)(2,1)S(1)}, u32[]{:S(2)}, u32[]{:S(2)}) collective-permute-start(bf16[128,768]{1,0:T(8,128)(2,1)S(1)} %slice.6.refs_0_), channel_id=1, source_target_pairs={{0,4},{4,6},{6,2},{2,0},{1,5},{5,7},{7,3},{3,1},{8,12},{12,14},{14... | collective-permute-start | bytes 589832 | tf_op jit(solution)/shard_map/ppermute | solution.py:348
  5.7 19.1 %collective-permute-start.2 = (bf16[256,768]{1,0:T(8,128)(2,1)}, bf16[256,768]{1,0:T(8,128)(2,1)S(1)}, u32[]{:S(2)}, u32[]{:S(2)}) collective-permute-start(bf16[256,768]{1,0:T(8,128)(2,1)} %v.3), channel_id=1, source_target_pairs={{0,1},{1,0},{8,9},{9,8},{16,17},{17,16},{24,25},{25,24},{2,3},{3,2... | collective-permute-start | bytes 1179656 | tf_op jit(solution)/shard_map/ppermute | solution.py:340
  8.1 7.9 %collective-permute-start.4 = (bf16[128,768]{1,0:T(8,128)(2,1)S(1)}, bf16[128,768]{1,0:T(8,128)(2,1)S(1)}, u32[]{:S(2)}, u32[]{:S(2)}) collective-permute-start(bf16[128,768]{1,0:T(8,128)(2,1)S(1)} %slice.7.refs_2_), channel_id=1, source_target_pairs={{0,4},{4,6},{6,2},{2,0},{1,5},{5,7},{7,3},{3,1},{8,12},{12,14},{14... | collective-permute-start | bytes 589832 | tf_op jit(solution)/shard_map/ppermute | solution.py:348
  9.7 16.6 %collective-permute-start.6 = (bf16[256,768]{1,0:T(8,128)(2,1)}, bf16[256,768]{1,0:T(8,128)(2,1)S(1)}, u32[]{:S(2)}, u32[]{:S(2)}) collective-permute-start(bf16[256,768]{1,0:T(8,128)(2,1)} %k.3), channel_id=1, source_target_pairs={{0,1},{1,0},{8,9},{9,8},{16,17},{17,16},{24,25},{25,24},{2,3},{3,2... | collective-permute-start | bytes 1179656 | tf_op jit(solution)/shard_map/ppermute | solution.py:340
  10.5 14.3 %collective-permute-start.1 = (bf16[128,768]{1,0:T(8,128)(2,1)S(1)}, bf16[128,768]{1,0:T(8,128)(2,1)S(1)}, u32[]{:S(2)}, u32[]{:S(2)}) collective-permute-start(bf16[128,768]{1,0:T(8,128)(2,1)S(1)} %collective-permute-done.refs_1_), channel_id=1, source_target_pairs={{0,4},{4,6},{6,2},{2,0},{1,5},{5,7},{7,3},{3,1},{8,12},{12,14},{14... | collective-permute-start | bytes 589832 | tf_op jit(solution)/shard_map/ppermute | solution.py:348
  16.0 9.5 %collective-permute-start.5 = (bf16[128,768]{1,0:T(8,128)(2,1)S(1)}, bf16[128,768]{1,0:T(8,128)(2,1)S(1)}, u32[]{:S(2)}, u32[]{:S(2)}) collective-permute-start(bf16[128,768]{1,0:T(8,128)(2,1)S(1)} %collective-permute-done.4.refs_3_), channel_id=1, source_target_pairs={{0,4},{4,6},{6,2},{2,0},{1,5},{5,7},{7,3},{3,1},{8,12},{12,14},{14... | collective-permute-start | bytes 589832 | tf_op jit(solution)/shard_map/ppermute | solution.py:348
  18.5 14.8 %collective-permute-start.9 = (bf16[256,768]{1,0:T(8,128)(2,1)}, bf16[256,768]{1,0:T(8,128)(2,1)S(1)}, u32[]{:S(2)}, u32[]{:S(2)}) collective-permute-start(bf16[256,768]{1,0:T(8,128)(2,1)} %q.3), channel_id=1, source_target_pairs={{0,1},{1,0},{8,9},{9,8},{16,17},{17,16},{24,25},{25,24},{2,3},{3,2... | collective-permute-start | bytes 1179656 | tf_op jit(solution)/shard_map/ppermute | solution.py:340
  22.5 7.1 %copy-start.1 = (bf16[768,3072]{1,0:T(8,128)(2,1)S(1)}, bf16[768,3072]{1,0:T(8,128)(2,1)}, u32[]{:S(2)}) copy-start(bf16[768,3072]{1,0:T(8,128)(2,1)} %weight.5) | copy-start | bytes 14155780
  24.8 6.3 %collective-permute-start.3 = (bf16[128,768]{1,0:T(8,128)(2,1)S(1)}, bf16[128,768]{1,0:T(8,128)(2,1)S(1)}, u32[]{:S(2)}, u32[]{:S(2)}) collective-permute-start(bf16[128,768]{1,0:T(8,128)(2,1)S(1)} %collective-permute-done.1.a_before), channel_id=1, source_target_pairs={{0,4},{4,6},{6,2},{2,0},{1,5},{5,7},{7,3},{3,1},{8,12},{12,14},{14... | collective-permute-start | bytes 589832 | tf_op jit(solution)/shard_map/ppermute | solution.py:348
  26.3 11.2 %collective-permute-start.8 = (bf16[256,768]{1,0:T(8,128)(2,1)S(1)}, bf16[256,768]{1,0:T(8,128)(2,1)S(1)}, u32[]{:S(2)}, u32[]{:S(2)}) collective-permute-start(bf16[256,768]{1,0:T(8,128)(2,1)S(1)} %collective-permute-done.6.k1), channel_id=1, source_target_pairs={{0,8},{1,25},{8,16},{9,1},{16,24},{17,9},{24,0},{25,17},{2,10},{3,... | collective-permute-start | bytes 1179656 | tf_op jit(solution)/shard_map/ppermute | solution.py:344
  26.3 12.6 %collective-permute-start.11 = (bf16[256,768]{1,0:T(8,128)(2,1)S(1)}, bf16[256,768]{1,0:T(8,128)(2,1)S(1)}, u32[]{:S(2)}, u32[]{:S(2)}) collective-permute-start(bf16[256,768]{1,0:T(8,128)(2,1)S(1)} %collective-permute-done.2.v1), channel_id=1, source_target_pairs={{0,8},{1,25},{8,16},{9,1},{16,24},{17,9},{24,0},{25,17},{2,10},{3,... | collective-permute-start | bytes 1179656 | tf_op jit(solution)/shard_map/ppermute | solution.py:344
  28.0 6.8 %collective-permute-start.7 = (bf16[128,768]{1,0:T(8,128)(2,1)S(1)}, bf16[128,768]{1,0:T(8,128)(2,1)S(1)}, u32[]{:S(2)}, u32[]{:S(2)}) collective-permute-start(bf16[128,768]{1,0:T(8,128)(2,1)S(1)} %collective-permute-done.5.b_before), channel_id=1, source_target_pairs={{0,4},{4,6},{6,2},{2,0},{1,5},{5,7},{7,3},{3,1},{8,12},{12,14},{14... | collective-permute-start | bytes 589832 | tf_op jit(solution)/shard_map/ppermute | solution.py:348
  32.2 6.8 %copy-start.2 = (bf16[256,768]{1,0:T(8,128)(2,1)S(1)}, bf16[256,768]{1,0:T(8,128)(2,1)}, u32[]{:S(2)}) copy-start(bf16[256,768]{1,0:T(8,128)(2,1)} %k.3) | copy-start | bytes 1179652
  32.2 6.8 %copy-start.3 = (bf16[256,768]{1,0:T(8,128)(2,1)S(1)}, bf16[256,768]{1,0:T(8,128)(2,1)}, u32[]{:S(2)}) copy-start(bf16[256,768]{1,0:T(8,128)(2,1)} %v.3) | copy-start | bytes 1179652
  32.2 6.8 %copy-start.4 = (bf16[256,768]{1,0:T(8,128)(2,1)S(1)}, bf16[256,768]{1,0:T(8,128)(2,1)}, u32[]{:S(2)}) copy-start(bf16[256,768]{1,0:T(8,128)(2,1)} %q.3) | copy-start | bytes 1179652
  32.2 6.8 %copy-start.7 = (s32[16,3]{0,1:T(4,128)S(1)}, s32[16,3]{0,1:T(4,128)}, u32[]{:S(2)}) copy-start(s32[16,3]{0,1:T(4,128)} %param.16) | copy-start | bytes 580
  33.3 5.7 %collective-permute-start.10 = (bf16[128,768]{1,0:T(8,128)(2,1)S(1)}, bf16[128,768]{1,0:T(8,128)(2,1)S(1)}, u32[]{:S(2)}, u32[]{:S(2)}) collective-permute-start(bf16[128,768]{1,0:T(8,128)(2,1)S(1)} %grad_heads_0.1.ga.ga0), channel_id=1, source_target_pairs={{0,1},{1,0},{8,9},{9,8},{16,17},{17,16},{24,25},{25,24},{2,3},{3,2... | collective-permute-start | bytes 589832 | tf_op jit(solution)/shard_map/ppermute | solution.py:340
  34.8 12.9 %collective-permute-start.14 = (bf16[256,768]{1,0:T(8,128)(2,1)S(1)}, bf16[256,768]{1,0:T(8,128)(2,1)S(1)}, u32[]{:S(2)}, u32[]{:S(2)}) collective-permute-start(bf16[256,768]{1,0:T(8,128)(2,1)S(1)} %collective-permute-done.9.q1.q), channel_id=1, source_target_pairs={{0,8},{1,25},{8,16},{9,1},{16,24},{17,9},{24,0},{25,17},{2,10},{3,... | collective-permute-start | bytes 1179656 | tf_op jit(solution)/shard_map/ppermute | solution.py:344
  35.9 7.2 %collective-permute-start.12 = (bf16[128,768]{1,0:T(8,128)(2,1)S(1)}, bf16[128,768]{1,0:T(8,128)(2,1)S(1)}, u32[]{:S(2)}, u32[]{:S(2)}) collective-permute-start(bf16[128,768]{1,0:T(8,128)(2,1)S(1)} %grad_heads_1.1.gb.gb0), channel_id=1, source_target_pairs={{0,1},{1,0},{8,9},{9,8},{16,17},{17,16},{24,25},{25,24},{2,3},{3,2... | collective-permute-start | bytes 589832 | tf_op jit(solution)/shard_map/ppermute | solution.py:340
  39.0 8.7 %collective-permute-start.15 = (bf16[128,768]{1,0:T(8,128)(2,1)S(1)}, bf16[128,768]{1,0:T(8,128)(2,1)S(1)}, u32[]{:S(2)}, u32[]{:S(2)}) collective-permute-start(bf16[128,768]{1,0:T(8,128)(2,1)S(1)} %collective-permute-done.10.ga1.ga), channel_id=1, source_target_pairs={{0,8},{1,25},{8,16},{9,1},{16,24},{17,9},{24,0},{25,17},{2,10},{3,... | collective-permute-start | bytes 589832 | tf_op jit(solution)/shard_map/ppermute | solution.py:344
  43.2 4.5 %collective-permute-start.13 = (bf16[32,768]{1,0:T(8,128)(2,1)S(1)}, bf16[32,768]{1,0:T(8,128)(2,1)S(1)}, u32[]{:S(2)}, u32[]{:S(2)}) collective-permute-start(bf16[32,768]{1,0:T(8,128)(2,1)S(1)} %get-tuple-element.58.aux0.aux), channel_id=1, source_target_pairs={{0,1},{1,0},{8,9},{9,8},{16,17},{17,16},{24,25},{25,24},{2,3},{3,2... | collective-permute-start | bytes 147464 | tf_op jit(solution)/shard_map/ppermute | solution.py:340
  48.8 1.8 %collective-permute-start.17 = (bf16[128,1536]{1,0:T(8,128)(2,1)S(1)}, bf16[128,1536]{1,0:T(8,128)(2,1)S(1)}, u32[]{:S(2)}, u32[]{:S(2)}) collective-permute-start(bf16[128,1536]{1,0:T(8,128)(2,1)S(1)} %get-tuple-element.76), channel_id=1, source_target_pairs={{0,8},{1,9},{8,0},{9,1},{16,24},{17,25},{24,16},{25,17},{2,10},{3,... | collective-permute-start | bytes 1179656 | tf_op jit(solution)/shard_map/ppermute | solution.py:340
  48.8 7.0 %collective-permute-start.16 = (bf16[160,768]{1,0:T(8,128)(2,1)S(1)}, bf16[160,768]{1,0:T(8,128)(2,1)S(1)}, u32[]{:S(2)}, u32[]{:S(2)}) collective-permute-start(bf16[160,768]{1,0:T(8,128)(2,1)S(1)} %get-tuple-element.70), channel_id=1, source_target_pairs={{0,8},{1,25},{8,16},{9,1},{16,24},{17,9},{24,0},{25,17},{2,10},{3,... | collective-permute-start | bytes 737288 | tf_op jit(solution)/shard_map/ppermute | solution.py:344
  50.6 7.9 %collective-permute-start.18 = (bf16[64,1536]{1,0:T(8,128)(2,1)S(1)}, bf16[64,1536]{1,0:T(8,128)(2,1)S(1)}, u32[]{:S(2)}, u32[]{:S(2)}) collective-permute-start(bf16[64,1536]{1,0:T(8,128)(2,1)S(1)} %get-tuple-element.78), channel_id=1, source_target_pairs={{0,16},{1,17},{8,24},{9,25},{16,0},{17,1},{24,8},{25,9},{2,18},{3,... | collective-permute-start | bytes 589832 | tf_op jit(solution)/shard_map/ppermute | solution.py:340
  (4 other events, 18.7 us)
